TPU v7x, 256 devices: a whole 4x4x8 slice. The times are simulated.
256 devices in a mesh: hist: 4 (over y), tok: 8 (over x, core), cand: 8 (over z).
Axes of the slice: x: 4, y: 4, z: 8, core: 2. Of those that a mesh axis runs over, the one named last changes fastest.
Arguments:
- features: bfloat16 [1024, 16, 2048], P('cand', 'tok'), may hold values from -6 to 6
- query_weight: bfloat16 [16, 2048, 128], P('tok'), may hold values from -0.125 to 0.125
- output_weight: bfloat16 [16, 128, 2048], P('tok'), may hold values from -0.5 to 0.5
- history: bfloat16 [16, 10240, 128], P('cand', 'hist'), may hold values from -500 to 500
- actions: int32 [16, 10240], P('cand', 'hist'), may hold values from 0 to 15
- lengths: int32 [16], P('cand'), may hold values from 1 to 10240, as said below
- cand_user: int32 [1024], P('cand'), may hold values from 0 to 15, as said below
- key_weight: bfloat16 [128, 128], replicated, may hold values from -0.5 to 0.5
- action_table: bfloat16 [16, 128], replicated, may hold values from -3 to 3
- value_weight: bfloat16 [128, 128], replicated, may hold values from -0.5 to 0.5
- gate_weight: bfloat16 [16, 2048, 8192], P('tok', None, ('hist', 'cand')), may hold values from -0.125 to 0.125
- up_weight: bfloat16 [16, 2048, 8192], P('tok', None, ('hist', 'cand')), may hold values from -0.125 to 0.125
- down_weight: bfloat16 [16, 8192, 2048], P('tok', ('hist', 'cand')), may hold values from -0.25 to 0.25
- tower_weight: bfloat16 [16, 2048, 256], P('tok'), may hold values from -0.03125 to 0.03125
- tower_bias: float32 [256], replicated, may hold values from -4 to 4
- head_weight: bfloat16 [256, 4], replicated, may hold values from -0.375 to 0.375
Outputs:
- layer_out: bfloat16 [1024, 16, 2048], P(('hist', 'cand'), 'tok')
- task_scores: float32 [1024, 4], P(('hist', 'cand'))
Inputs may be any that keep to these rules, and one draw needn't show every extreme that they name: `lengths`: every user has at least one valid event, and some user has exactly 10240. `cand_user`: candidate b belongs to one of the 2 users numbered from (b // 128) * 2 on.
All inputs are finite; a program needn't handle non-finite values.
Results may differ from a plain program's by a relative error of at most 0.015.
The roundings to bfloat16 on the way count: a program that leaves them out, or rounds other values in their place, can miss the bound.
Values may be sent and summed in bfloat16 or wider, within the bound.
No kernel may reach another device: no remote copies, remote signals or barrier semaphores. Data moves between devices by JAX's collectives and lax.ppermute only.
A program may use at most 128 MiB of HBM per device.

v0:
```python
import jax
import jax.numpy as jnp
from jax import lax
from jax.sharding import PartitionSpec as P

FEATS = 16
DK = 128
ACTIONS = 16


EPS = 1e-06


def normalize(values):
    widened = values.astype(jnp.float32)
    return (widened * lax.rsqrt(jnp.mean(widened * widened, axis=-1, keepdims=True) + EPS)).astype(
        jnp.bfloat16
    )


def shards(
    features,
    query_weight,
    output_weight,
    history,
    actions,
    lengths,
    cand_user,
    key_weight,
    action_table,
    value_weight,
    gate_weight,
    up_weight,
    down_weight,
    tower_weight,
    tower_bias,
    head_weight,
):
    cand_rows, local_tokens, feat_width = features.shape
    user_rows, event_rows, event_width = history.shape
    key_part = jnp.einsum("ulh,hk->ulk", history, key_weight, preferred_element_type=jnp.float32)
    kinds_onehot = (
        actions[:, :, None] == jnp.arange(ACTIONS, dtype=jnp.int32)[None, None, :]
    ).astype(jnp.bfloat16)
    event_keys = (
        key_part
        + jnp.einsum("ula,ak->ulk", kinds_onehot, action_table, preferred_element_type=jnp.float32)
    ).astype(jnp.bfloat16)
    event_values = jnp.einsum(
        "ulh,hk->ulk", normalize(history), value_weight, preferred_element_type=jnp.float32
    ).astype(jnp.bfloat16)
    queries = jnp.einsum(
        "btd,tdk->btk", features, query_weight, preferred_element_type=jnp.float32
    ).astype(jnp.bfloat16)
    positions = lax.axis_index("hist") * event_rows + jnp.arange(event_rows, dtype=jnp.int32)
    live_events = positions[None, :] < lengths[:, None]
    local_user = cand_user - lax.axis_index("cand") * user_rows
    owned_pairs = local_user[:, None] == jnp.arange(user_rows, dtype=jnp.int32)[None, :]
    allowed = owned_pairs[:, None, :, None] & live_events[None, None, :, :]
    scores = jnp.einsum(
        "btk,ulk->btul", queries, event_keys, preferred_element_type=jnp.float32
    ) * (1.5 * DK ** (-0.5))
    filled = jnp.where(allowed, scores, -1e30)
    local_max = jnp.max(filled, axis=(2, 3))
    weights = jnp.where(allowed, jnp.exp(filled - local_max[:, :, None, None]), 0.0)
    local_total = jnp.sum(weights, axis=(2, 3))
    weights_high = weights.astype(jnp.bfloat16)
    weights_low = (weights - weights_high.astype(jnp.float32)).astype(jnp.bfloat16)
    local_weighted = jnp.einsum(
        "btul,ulk->btk", weights_high, event_values, preferred_element_type=jnp.float32
    ) + jnp.einsum("btul,ulk->btk", weights_low, event_values, preferred_element_type=jnp.float32)
    merged_max = lax.pmax(local_max, "hist")
    rescale = jnp.exp(local_max - merged_max)
    merged_total, merged_weighted = lax.psum(
        (local_total * rescale, local_weighted * rescale[:, :, None]), "hist"
    )
    attended = (merged_weighted / merged_total[:, :, None]).astype(jnp.bfloat16)
    token_input = (
        features.astype(jnp.float32)
        + jnp.einsum("btk,tkd->btd", attended, output_weight, preferred_element_type=jnp.float32)
    ).astype(jnp.bfloat16)
    head_split = token_input.reshape(cand_rows, local_tokens, FEATS, feat_width // FEATS)
    exchanged = lax.all_to_all(head_split, "tok", split_axis=2, concat_axis=1, tiled=True)
    mixed_tokens = jnp.swapaxes(exchanged, 1, 2).reshape(cand_rows, local_tokens, feat_width)
    gathered = lax.all_gather(mixed_tokens, "cand", axis=0, tiled=True)
    all_rows = gathered.shape[0]
    own_rows = all_rows // (lax.axis_size("hist") * lax.axis_size("cand"))
    own_block = lax.axis_index("hist") * lax.axis_size("cand") + lax.axis_index("cand")
    normed = normalize(gathered)
    gate_values = jnp.einsum(
        "bsd,sdf->bsf", normed, gate_weight, preferred_element_type=jnp.float32
    )
    up_values = jnp.einsum("bsd,sdf->bsf", normed, up_weight, preferred_element_type=jnp.float32)
    partial_value = lax.psum_scatter(
        jnp.einsum(
            "bsf,sfd->bsd",
            (jax.nn.silu(gate_values) * up_values).astype(jnp.bfloat16),
            down_weight,
            preferred_element_type=jnp.float32,
        ),
        ("hist", "cand"),
        scatter_dimension=0,
        tiled=True,
    )
    residual = lax.dynamic_slice_in_dim(gathered, own_block * own_rows, own_rows, 0)
    layer_out = (residual.astype(jnp.float32) + partial_value).astype(jnp.bfloat16)
    tower_part = jnp.einsum(
        "bsd,sdh->bh", layer_out, tower_weight, preferred_element_type=jnp.float32
    )
    tower_sum = lax.psum(tower_part, "tok")
    tower_hidden = jax.nn.silu(tower_sum + tower_bias).astype(jnp.bfloat16)
    task_scores = jnp.dot(tower_hidden, head_weight, preferred_element_type=jnp.float32)
    return (layer_out, task_scores)


def solution(mesh):
    in_specs = (
        P("cand", "tok", None),
        P("tok", None, None),
        P("tok", None, None),
        P("cand", "hist", None),
        P("cand", "hist"),
        P("cand"),
        P("cand"),
        P(),
        P(),
        P(),
        P("tok", None, ("hist", "cand")),
        P("tok", None, ("hist", "cand")),
        P("tok", ("hist", "cand"), None),
        P("tok", None, None),
        P(),
        P(),
    )
    out_specs = (P(("hist", "cand"), "tok", None), P(("hist", "cand"), None))
    return jax.shard_map(shards, mesh=mesh, in_specs=in_specs, out_specs=out_specs, check_vma=False)
```

profile of v0, /device:TPU:1, one launch (start us, length us, event | category | flops | bytes accessed | tf_op | source)
XLA Modules:
  0.0 508.0 jit_solution(16542501611450143678)
XLA Ops:
  7.2 0.0 copy-start
  7.2 0.0 copy-start.2
  7.2 0.0 copy-start.6
  7.2 0.0 all-reduce.2.cloned.1.call-start
  7.3 0.8 broadcast_subtract_fusion
  8.1 2.1 fusion.14
  10.2 0.7 broadcast_compare_fusion
  11.0 1.2 broadcast_and_fusion
  12.2 1.6 fusion.48
  13.8 0.0 copy-done.2
  13.8 0.0 copy-done.6
  13.8 1.6 fusion.7
  15.4 6.5 %fusion.60 = (f32[128,2]{0,1:T(2,128)S(1)}, f32[128,2,2,2560]{3,0,2,1:T(8,128)}) fusion(bf16[2,2560,128,1]{2,1,0,3:T(8,128)(2,1)} %fusion.7, bf16[2,2048,128]{2,1,0:T(8,128)(2,1)} %param.17, bf16[128,2,2048]{2,1,0:T(2,128)(2,1)} %param.16, pred[128,2,2560]{2,0,1:T(8,128)(4,1)} %broadcast_and_fusion), kind=kOutput, calls=%fused_computation.73 | convolution fusion | flops 473726720 | bytes 9307136 | tf_op jit(solution)/shard_map/btk,ulk->btul/dot_general | solution.py:60
  21.9 9.5 %pmax.7 = f32[128,2]{0,1:T(2,128)S(1)} all-reduce(f32[128,2]{0,1:T(2,128)S(1)} %get-tuple-element.10), channel_id=1, replica_groups=mesh['hist'=4,'tok'=8,'cand'=8] {'hist'}, use_global_device_ids=true, to_apply=%region_2.3 | all-reduce | flops 256 | bytes 2048 | tf_op jit(solution)/shard_map/pmax | solution.py:72
  31.4 4.1 fusion.9
  35.5 0.0 copy-done.7
  35.5 0.0 copy-start.4
  35.6 1.1 fusion.8
  36.7 0.0 copy-done.1
  36.7 0.0 copy-done.4
  36.7 1.9 fusion.33
  38.6 0.0 copy-start.5
  38.6 2.1 fusion.40
  40.7 0.0 all-reduce.2.cloned.1.call-update
  40.8 0.0 all-gather.2.cloned.1.call-start
  40.8 6.0 %psum.22 = f32[128,2]{0,1:T(2,128)S(1)} all-reduce(f32[128,2]{0,1:T(2,128)S(1)} %get-tuple-element.8), channel_id=1, replica_groups=mesh['hist'=4,'tok'=8,'cand'=8] {'hist'}, use_global_device_ids=true, to_apply=%region_5.6 | all-reduce | flops 256 | bytes 2048 | tf_op jit(solution)/shard_map/psum | solution.py:74
  46.8 41.0 %all-reduce.2.cloned.1.call-done = f32[128,2,128]{2,0,1:T(8,128)} async-done(((f32[128,2,128]{2,0,1:T(8,128)}), f32[128,2,128]{2,0,1:T(8,128)}) %all-reduce.2.cloned.1.call-update) | async-done | bytes 131088 | tf_op jit(solution)/shard_map/psum | solution.py:74
  87.8 2.3 fusion.30
  90.1 0.3 copy.47
  90.4 21.8 %all_to_all.18 = bf16[128,2,16,128]{3,0,1,2:T(8,128)(2,1)S(1)} all-to-all(bf16[128,2,16,128]{3,0,1,2:T(8,128)(2,1)S(1)} %bitcast.93), channel_id=1, replica_groups=mesh['hist'=4,'tok'=8,'cand'=8] {'tok'}, dimensions={2} | all-to-all | bytes 2097152 | tf_op jit(solution)/shard_map/all_to_all | solution.py:83
  112.3 1.1 copy.30
  113.3 1.3 reshape.88
  114.6 0.0 all-gather.2.cloned.1.call-update
  114.7 0.2 reduce-scatter.2.cloned.1.call-start
  114.9 93.0 %all-gather.2.cloned.1.call-done = bf16[1024,2,2048]{2,0,1:T(8,128)(2,1)} async-done(((bf16[128,2,2048]{2,0,1:T(8,128)(2,1)}), bf16[1024,2,2048]{2,0,1:T(8,128)(2,1)}) %all-gather.2.cloned.1.call-update) | async-done | bytes 8388624 | tf_op jit(solution)/shard_map/all_gather | solution.py:85
  207.9 5.2 %fusion = f32[1024,2]{0,1:T(2,128)S(1)} fusion(bf16[1024,2,2048]{2,0,1:T(8,128)(2,1)} %all-gather.2.cloned.1.call-done), kind=kLoop, calls=%fused_computation.2 | loop fusion | flops 12580864 | bytes 8396800 | tf_op jit(solution)/shard_map/reduce_sum | solution.py:16
  213.2 0.5 copy-done.3
  213.7 5.4 %fusion.4 = f32[2,1024,256]{2,1,0:T(8,128)} fusion(bf16[2,2048,256]{2,1,0:T(8,128)(2,1)} %param.26, bf16[1024,2,2048]{2,0,1:T(8,128)(2,1)S(1)} %copy-done.3, f32[1024,2]{0,1:T(2,128)S(1)} %add_rsqrt_fusion.1), kind=kOutput, calls=%fused_computation.5 | convolution fusion | flops 2160066560 | bytes 12591104 | tf_op jit(solution)/shard_map/bsd,sdf->bsf/dot_general | solution.py:90
  219.1 14.8 %convolution_bitcast_fusion = f32[1024,2,2048]{2,0,1:T(8,128)} fusion(bf16[2,256,2048]{2,1,0:T(8,128)(2,1)S(1)} %copy-done, f32[2,1024,256]{2,1,0:T(8,128)} %fusion.4, bf16[2,2048,256]{2,1,0:T(8,128)(2,1)} %param.27, bf16[1024,2,2048]{2,0,1:T(8,128)(2,1)} %all-gather.2.cloned.1.call-done, f32[1024,2]{0,1:T(2,128)S(1)} %add_rsqrt_fusion.1), kind=kOutput, calls=%fused_computation.6 | convolution fusion | flops 4310695936 | bytes 31465472 | tf_op jit(solution)/shard_map/bsf,sfd->bsd/dot_general | solution.py:95
  233.9 0.0 reduce-scatter.2.cloned.1.call-update
  233.9 0.0 copy-start.8
  233.9 0.0 copy-start.9
  234.0 237.6 %reduce-scatter.2.cloned.1.call-done = f32[32,2,2048]{2,0,1:T(8,128)} async-done(((f32[1024,2,2048]{2,0,1:T(8,128)}), f32[32,2,2048]{2,0,1:T(8,128)}) %reduce-scatter.2.cloned.1.call-update) | async-done | bytes 524304 | tf_op jit(solution)/shard_map/reduce_scatter | solution.py:94
  471.6 1.2 add_convert_fusion
  472.7 1.0 copy.31
  473.7 2.0 convolution_bitcast_fusion.2
  475.7 25.1 %psum.23 = f32[32,256]{1,0:T(8,128)S(1)} all-reduce(f32[32,256]{1,0:T(8,128)S(1)} %convolution_bitcast_fusion.2), channel_id=1, replica_groups=mesh['hist'=4,'tok'=8,'cand'=8] {'tok'}, use_global_device_ids=true, to_apply=%region_8.9 | all-reduce | flops 8192 | bytes 65536 | tf_op jit(solution)/shard_map/psum | solution.py:110
  500.8 0.7 fusion.53
  (12 shorter events, 0.1 us)
Async XLA Ops:
  7.2 212.0 %copy-start = (bf16[2,256,2048]{2,1,0:T(8,128)(2,1)S(1)}, bf16[2,256,2048]{2,1,0:T(8,128)(2,1)}, u32[]{:S(2)}) copy-start(bf16[2,256,2048]{2,1,0:T(8,128)(2,1)} %param.28) | copy-start | bytes 6291460
  7.2 6.6 %copy-start.2 = (bf16[2,2560,128]{2,1,0:T(8,128)(2,1)S(1)}, bf16[2,2560,128]{2,1,0:T(8,128)(2,1)}, u32[]{:S(2)}) copy-start(bf16[2,2560,128]{2,1,0:T(8,128)(2,1)} %param.19) | copy-start | bytes 3932164
  7.2 6.6 %copy-start.6 = (bf16[128,128]{1,0:T(8,128)(2,1)S(1)}, bf16[128,128]{1,0:T(8,128)(2,1)}, u32[]{:S(2)}) copy-start(bf16[128,128]{1,0:T(8,128)(2,1)} %param.23) | copy-start | bytes 98308
  7.2 80.6 %all-reduce.2.cloned.1.call-start = ((), (), s32[]{:S(2)}) async-start(), calls=%async_computation.2 | async-start | bytes 262144 | tf_op jit(solution)/shard_map/psum | solution.py:74
  31.4 4.1 copy-start.7
  31.4 5.2 %copy-start.1 = (f32[128,2,2,2560]{3,0,2,1:T(8,128)S(1)}, f32[128,2,2,2560]{3,0,2,1:T(8,128)}, u32[]{:S(2)}) copy-start(f32[128,2,2,2560]{3,0,2,1:T(8,128)} %get-tuple-element.11) | copy-start | bytes 15728644
  35.5 1.1 copy-start.4
  38.6 49.2 %copy-start.5 = (bf16[128,2,2048]{2,1,0:T(2,128)(2,1)S(1)}, bf16[128,2,2048]{2,1,0:T(2,128)(2,1)}, u32[]{:S(2)}) copy-start(bf16[128,2,2048]{2,1,0:T(2,128)(2,1)} %param.16) | copy-start | bytes 3145732
  40.8 167.1 %all-gather.2.cloned.1.call-start = ((), (), s32[]{:S(2)}) async-start(), calls=%async_computation.3 | async-start | bytes 9437184 | tf_op jit(solution)/shard_map/all_gather | solution.py:85
  114.7 356.9 %reduce-scatter.2.cloned.1.call-start = ((), (), s32[]{:S(2)}) async-start(), calls=%async_computation.4 | async-start | bytes 17301504 | tf_op jit(solution)/shard_map/reduce_scatter | solution.py:94
  207.9 5.8 %copy-start.3 = (bf16[1024,2,2048]{2,0,1:T(8,128)(2,1)S(1)}, bf16[1024,2,2048]{2,0,1:T(8,128)(2,1)}, u32[]{:S(2)}) copy-start(bf16[1024,2,2048]{2,0,1:T(8,128)(2,1)} %all-gather.2.cloned.1.call-done) | copy-start | bytes 25165828
  233.9 266.9 %copy-start.8 = (bf16[256,4]{0,1:T(4,128)(2,1)S(1)}, bf16[256,4]{0,1:T(4,128)(2,1)}, u32[]{:S(2)}) copy-start(bf16[256,4]{0,1:T(4,128)(2,1)} %param.31) | copy-start | bytes 6148
  233.9 266.8 %copy-start.9 = (f32[256]{0:T(256)S(1)}, f32[256]{0:T(256)}, u32[]{:S(2)}) copy-start(f32[256]{0:T(256)} %param.30) | copy-start | bytes 3076
Sparse Core Ops, SparseCore 0:
  40.9 46.8 all-reduce.1
  114.8 93.0 all-gather.1
  234.1 237.4 reduce-scatter.1
where the time goes:
time: 510 us; the launch traced here: 508 us
  waiting for transfers between devices  372 us (73%)
  blocking collectives  62.4 us (12%)
  matrix products  40.1 us (8%)
  other arithmetic  15.5 us (3%)
  between operations  13.9 us (3%)
    reduce_scatter x1, waiting for transfers between devices, shards(): lax.psum_scatter(jnp.einsum('bsf,sfd->bsd', (jax.nn.silu(gate_values) * u...  238 us
    all_gather x1, waiting for transfers between devices, shards(): gathered = lax.all_gather(mixed_tokens, 'cand', axis=0, tiled=True)  93 us
    psum x1, waiting for transfers between devices, shards(): lax.psum((local_total * rescale, local_weighted * rescale[:, :, None]), '...  41 us
    psum x1, blocking collectives, shards(): tower_sum = lax.psum(tower_part, 'tok')  25.1 us
    all_to_all x1, blocking collectives, shards(): lax.all_to_all(head_split, 'tok', split_axis=2, concat_axis=1, tiled=True)  21.8 us
    dot_general x1, matrix products, shards(): jnp.einsum('bsf,sfd->bsd', (jax.nn.silu(gate_values) * up_values).astype(...  14.8 us
  transfers between devices with their start and end apart: 3, of which 3 were waited for; matrix products, arithmetic and copies ran while one was open for 0% of the time, Pallas kernels for 0%

commit v1 on v0

v1 whole, which is shorter than its diff:
```python
import jax
import jax.numpy as jnp
from jax import lax
from jax.experimental import pallas as pl
from jax.experimental.pallas import tpu as pltpu
from jax.sharding import PartitionSpec as P

EPS = 1e-06
DK = 128
ACTIONS = 16
HIST, TOK, CAND = 4, 8, 8
SCALE = 1.5 * DK ** (-0.5) * 1.4426950408889634
CHUNK = 512
F32 = jnp.float32
BF16 = jnp.bfloat16


def dot(a, b, dims=((1,), (0,))):
    return lax.dot_general(a, b, (dims, ((), ())), preferred_element_type=F32)


def attention_kernel(limit_ref, q_ref, owner_ref, hist_ref, act_ref, kwt_ref, tabt_ref, vw_ref, out_ref, m_ref, l_ref, acc_ref):
    step = pl.program_id(0)

    @pl.when(step == 0)
    def _():
        m_ref[...] = jnp.full_like(m_ref, -1e29)
        l_ref[...] = jnp.zeros_like(l_ref)
        acc_ref[...] = jnp.zeros_like(acc_ref)

    first = owner_ref[...] == 0
    q = q_ref[...]
    where = lax.broadcasted_iota(jnp.int32, (1, CHUNK), 1) + step * CHUNK
    scores, values = [], []
    for u in range(2):
        h = hist_ref[u]
        kinds = lax.broadcasted_iota(jnp.int32, (ACTIONS, CHUNK), 0)
        onehot = jnp.where(kinds == act_ref[u : u + 1, :], 1.0, 0.0).astype(BF16)
        keys = dot(kwt_ref[...], h, ((1,), (1,))) + dot(tabt_ref[...], onehot)
        s = dot(q, keys.astype(BF16)) * SCALE
        scores.append(jnp.where(where < limit_ref[u], s, -1e30))
        wide = h.astype(F32)
        normed = wide * lax.rsqrt(jnp.mean(wide * wide, axis=1, keepdims=True) + EPS)
        values.append(dot(normed.astype(BF16), vw_ref[...]).astype(BF16))
    s = jnp.where(first, scores[0], scores[1])
    m_old = m_ref[...]
    m_new = jnp.maximum(m_old, jnp.max(s, axis=1, keepdims=True))
    p = jnp.exp2(s - m_new)
    fade = jnp.exp2(m_old - m_new)
    m_ref[...] = m_new
    l_ref[...] = l_ref[...] * fade + jnp.sum(p, axis=1, keepdims=True)
    high = p.astype(BF16)
    low = (p - high.astype(F32)).astype(BF16)
    zero = jnp.zeros_like(high)
    total = acc_ref[...] * fade
    for part in (high, low):
        total += dot(jnp.where(first, part, zero), values[0])
        total += dot(jnp.where(first, zero, part), values[1])
    acc_ref[...] = total

    @pl.when(step == pl.num_programs(0) - 1)
    def _():
        out_ref[0:256, :] = acc_ref[...]
        for n, ref in ((256, m_ref), (258, l_ref)):
            row = jnp.transpose(jnp.broadcast_to(ref[...], (256, 128)))
            out_ref[n : n + 1, :] = row[0:1, 0:128]
            out_ref[n + 1 : n + 2, :] = row[0:1, 128:256]
        out_ref[260:264, :] = jnp.zeros((4, 128), F32)


def attention(limits, queries, owner, history, actions, kwt, tabt, vw):
    steps = history.shape[1] // CHUNK
    whole = lambda *shape: pl.BlockSpec(shape, lambda i, lim: (0,) * len(shape))
    return pl.pallas_call(
        attention_kernel,
        out_shape=jax.ShapeDtypeStruct((264, 128), F32),
        grid_spec=pltpu.PrefetchScalarGridSpec(
            num_scalar_prefetch=1,
            grid=(steps,),
            in_specs=[
                whole(256, 128),
                whole(256, 1),
                pl.BlockSpec((2, CHUNK, 128), lambda i, lim: (0, i, 0)),
                pl.BlockSpec((2, CHUNK), lambda i, lim: (0, i)),
                whole(128, 128),
                whole(128, ACTIONS),
                whole(128, 128),
            ],
            out_specs=whole(264, 128),
            scratch_shapes=[pltpu.VMEM((256, 1), F32), pltpu.VMEM((256, 1), F32), pltpu.VMEM((256, 128), F32)],
        ),
        compiler_params=pltpu.CompilerParams(dimension_semantics=("arbitrary",), vmem_limit_bytes=24 << 20),
        cost_estimate=pl.CostEstimate(flops=2_000_000_000, bytes_accessed=2_000_000, transcendentals=700_000),
        name="attention",
    )(limits, queries, owner, history, actions, kwt, tabt, vw)


def merge_kernel(p0, p1, p2, p3, feat_ref, ow_ref, out_ref):
    parts = (p0, p1, p2, p3)

    def column(ref, n):
        rows = [jnp.transpose(jnp.broadcast_to(ref[n + i : n + i + 1, :], (128, 128))) for i in range(2)]
        return jnp.concatenate(rows, axis=0)

    maxima = [column(ref, 256) for ref in parts]
    top = jnp.maximum(jnp.maximum(maxima[0], maxima[1]), jnp.maximum(maxima[2], maxima[3]))
    total, weighted = 0.0, 0.0
    for ref, m in zip(parts, maxima):
        fade = jnp.exp2(m - top)
        total += column(ref, 258) * fade
        weighted += ref[0:256, :] * fade
    attended = (weighted / total).astype(BF16)
    for j in range(2):
        update = dot(attended[j * 128 : (j + 1) * 128], ow_ref[j])
        tokens = (feat_ref[j].astype(F32) + update).astype(BF16)
        for x in range(4):
            for k in range(2):
                for m in range(4):
                    out_ref[2 * x + k, m * 16 : (m + 1) * 16, j * 128 : (j + 1) * 128] = tokens[
                        m * 32 + k * 16 : m * 32 + k * 16 + 16, x * 128 : (x + 1) * 128
                    ]


def merge(parts, feats, ow):
    return pl.pallas_call(
        merge_kernel,
        out_shape=jax.ShapeDtypeStruct((8, 64, 256), BF16),
        compiler_params=pltpu.CompilerParams(vmem_limit_bytes=16 << 20),
        cost_estimate=pl.CostEstimate(flops=70_000_000, bytes_accessed=1_500_000, transcendentals=150_000),
        name="merge",
    )(*parts, feats, ow)


def ffn_kernel(x_ref, *refs):
    packs, out_ref = refs[:8], refs[8]
    gu, dn, normed, hidden, gu_sem, dn_sem = refs[9:]
    gu_copies = [pltpu.make_async_copy(packs[p].at[pl.ds(0, 16)], gu.at[p], gu_sem.at[p]) for p in range(8)]
    dn_copies = [
        pltpu.make_async_copy(packs[p].at[pl.ds(16, 8)], dn.at[:, pl.ds(p * 128, 128), :], dn_sem.at[p])
        for p in range(8)
    ]
    for copy in gu_copies + dn_copies:
        copy.start()
    for zb in range(8):
        wide = jnp.concatenate([x_ref[zb, s] for s in range(8)], axis=1).astype(F32)
        rows = (wide * lax.rsqrt(jnp.mean(wide * wide, axis=1, keepdims=True) + EPS)).astype(BF16)
        for m in range(4):
            to = ((zb % 2) * 4 + m) * 4 + zb // 2
            normed[to * 16 : (to + 1) * 16, :] = rows[m * 16 : (m + 1) * 16]
    for p in range(8):
        gu_copies[p].wait()
        both = dot(normed[...], gu[p].reshape(2048, 256))
        gate, up = both[:, :128], both[:, 128:]
        hidden[:, p * 128 : (p + 1) * 128] = (gate / (1.0 + jnp.exp(-gate)) * up).astype(BF16)
    for copy in dn_copies:
        copy.wait()
    for g in range(8):
        out_ref[:, g * 256 : (g + 1) * 256] = dot(hidden[...], dn[g]).astype(BF16)


def feed_forward(x, packs):
    return pl.pallas_call(
        ffn_kernel,
        out_shape=jax.ShapeDtypeStruct((512, 2048), BF16),
        in_specs=[pl.BlockSpec(memory_space=pltpu.VMEM)] + [pl.BlockSpec(memory_space=pl.ANY)] * 8,
        out_specs=pl.BlockSpec(memory_space=pltpu.VMEM),
        scratch_shapes=[
            pltpu.VMEM((8, 16, 128, 256), BF16),
            pltpu.VMEM((8, 1024, 256), BF16),
            pltpu.VMEM((512, 2048), BF16),
            pltpu.VMEM((512, 1024), BF16),
            pltpu.SemaphoreType.DMA((8,)),
            pltpu.SemaphoreType.DMA((8,)),
        ],
        compiler_params=pltpu.CompilerParams(vmem_limit_bytes=40 << 20),
        cost_estimate=pl.CostEstimate(flops=6_500_000_000, bytes_accessed=17_000_000, transcendentals=600_000),
        name="feed_forward",
    )(x, *packs)


def exchange_pairs(r, reverse):
    pairs = []
    for y in range(HIST):
        for t in range(TOK):
            x, c = t // 2, t % 2
            q = y ^ r
            source, target = (y, 2 * x + c), (2 * c + q // 2, 2 * x + q % 2)
            if reverse:
                source, target = target, source
            pairs.append((source[0] * TOK + source[1], target[0] * TOK + target[1]))
    return pairs


def shards(
    features,
    query_weight,
    output_weight,
    history,
    actions,
    lengths,
    cand_user,
    key_weight,
    action_table,
    value_weight,
    gate_weight,
    up_weight,
    down_weight,
    tower_weight,
    tower_bias,
    head_weight,
):
    y, tok, z = lax.axis_index("hist"), lax.axis_index("tok"), lax.axis_index("cand")
    core = tok % 2
    both = ("hist", "tok")

    packs = []
    for r in range(4):
        q = y ^ r
        j, k = q // 2, q % 2
        gate = lax.dynamic_slice(gate_weight, (j, 0, k * 128), (1, 2048, 128))
        up = lax.dynamic_slice(up_weight, (j, 0, k * 128), (1, 2048, 128))
        down = lax.dynamic_slice(down_weight, (j, k * 128, 0), (1, 128, 2048))
        pack = jnp.concatenate(
            [
                jnp.concatenate([gate, up], axis=2).reshape(16, 128, 256),
                jnp.swapaxes(down.reshape(128, 8, 256), 0, 1),
            ],
            axis=0,
        )
        packs.append(lax.ppermute(pack, both, exchange_pairs(r, False)))

    feats = jnp.swapaxes(features, 0, 1)
    queries = jnp.einsum("tbd,tdk->tbk", feats, query_weight, preferred_element_type=F32).astype(BF16)
    owner = cand_user - z * 2
    owner = jnp.concatenate([owner, owner])[:, None]
    part = attention(
        lengths - y * history.shape[1],
        queries.reshape(256, 128),
        owner,
        history,
        actions,
        key_weight.T,
        action_table.T,
        value_weight,
    )
    parts = [part] + [lax.ppermute(part, "hist", [(i, (i + d) % HIST) for i in range(HIST)]) for d in (1, 2, 3)]
    feat_sel = lax.dynamic_slice(feats.reshape(2, 128, 4, 4, 128), (0, 0, 0, y, 0), (2, 128, 4, 1, 128))
    ow_sel = lax.dynamic_slice(output_weight.reshape(2, 128, 4, 4, 128), (0, 0, 0, y, 0), (2, 128, 4, 1, 128))
    outgoing = merge(parts, feat_sel.reshape(2, 128, 512), ow_sel.reshape(2, 128, 512))
    mixed = lax.all_to_all(outgoing, "tok", split_axis=0, concat_axis=0, tiled=True)
    gathered = lax.all_gather(mixed[None], "cand", axis=0, tiled=True)

    swapped = [lax.ppermute(p, "tok", [(i, i ^ 1) for i in range(TOK)]) for p in packs]
    partial = feed_forward(gathered, packs + swapped)
    summed = lax.psum_scatter(partial, "cand", scatter_dimension=0, tiled=True)
    residual = lax.dynamic_slice(
        gathered.reshape(4, 2, 8, 4, 16, 256), (0, z // 4, 0, z % 4, 0, 0), (4, 1, 8, 1, 16, 256)
    ).reshape(4, 8, 16, 256)
    residual = jnp.swapaxes(residual, 1, 2).reshape(4, 16, 2048)
    block = (residual.astype(F32) + summed.reshape(4, 16, 2048).astype(F32)).astype(BF16)

    arrived = []
    mine = (y % 2) * 2 + core
    for r in range(4):
        send = lax.dynamic_index_in_dim(block, mine ^ r, 0, keepdims=False)
        arrived.append(lax.ppermute(send, both, exchange_pairs(r, True)))
    arrived = jnp.stack(arrived)
    quarters = [lax.dynamic_index_in_dim(arrived, y ^ q, 0, keepdims=False) for q in range(4)]
    tokens = [jnp.concatenate(quarters[2 * j : 2 * j + 2], axis=0) for j in range(2)]
    layer_out = jnp.stack(tokens, axis=1)

    tower_part = dot(tokens[0], tower_weight[0]) + dot(tokens[1], tower_weight[1])
    tower_sum = tower_part
    for d in range(1, TOK):
        tower_sum += lax.ppermute(tower_part, "tok", [(i, i ^ d) for i in range(TOK)])
    tower_hidden = jax.nn.silu(tower_sum + tower_bias).astype(BF16)
    task_scores = jnp.dot(tower_hidden, head_weight, preferred_element_type=F32)
    return (layer_out, task_scores)


def solution(mesh):
    in_specs = (
        P("cand", "tok", None),
        P("tok", None, None),
        P("tok", None, None),
        P("cand", "hist", None),
        P("cand", "hist"),
        P("cand"),
        P("cand"),
        P(),
        P(),
        P(),
        P("tok", None, ("hist", "cand")),
        P("tok", None, ("hist", "cand")),
        P("tok", ("hist", "cand"), None),
        P("tok", None, None),
        P(),
        P(),
    )
    out_specs = (P(("hist", "cand"), "tok", None), P(("hist", "cand"), None))
    return jax.shard_map(shards, mesh=mesh, in_specs=in_specs, out_specs=out_specs, check_vma=False)
```

time: 510 us -> 235 us (0.46)
  waiting for transfers between devices: 372 us -> 79.4 us
  blocking collectives: 62.4 us -> 0 us
  starting transfers between devices: 0.3 us -> 56.5 us
  local copies, waits for them, and re-layouts: 4.19 us -> 40.9 us
  matrix products: 40.1 us -> 4.52 us
  Pallas kernels: 0 us -> 25.5 us
    reduce_scatter x1, waiting for transfers between devices: 238 us -> 40.4 us  [shards(): summed = lax.psum_scatter(partial, 'cand', scatter_dimension=0, tiled=True)]
    all_gather x1, waiting for transfers between devices: 93 us -> 0.01 us  [shards(): gathered = lax.all_gather(mixed[None], 'cand', axis=0, tiled=True)]
    ppermute x0 -> x22, starting transfers between devices: none -> 52.1 us  [the longest x4 20.6 us: shards(): packs.append(lax.ppermute(pack, both, exchange_pairs(r, False)))]
    psum x1 -> x0, waiting for transfers between devices: 41 us -> none  [shards(): lax.psum((local_total * rescale, local_weighted * rescale[:, :, None]), '...]
    dot_general x11 -> x4, matrix products: 40.1 us -> 4.52 us  [the longest x1 1.99 us: shards(): jnp.einsum('tbd,tdk->tbk', feats, query_weight, preferred_element_type=F32)]
    ppermute x0 -> x22, waiting for transfers between devices: none -> 33.8 us  [the longest x4 28.7 us: shards(): packs.append(lax.ppermute(pack, both, exchange_pairs(r, False)))]
    psum x2 -> x0, blocking collectives: 31.1 us -> none  [the longest x1 25.1 us: shards(): tower_sum = lax.psum(tower_part, 'tok')]
    pallas_call x0 -> x3, Pallas kernels: none -> 25.5 us  [the longest x1 16.5 us: feed_forward(): pl.pallas_call(ffn_kernel, out_shape=jax.ShapeDtypeStruct((512, 2048), BF...]
  transfers between devices with their start and end apart: 3 -> 25, of which waited for: 3 -> 9; matrix products, arithmetic and copies ran while one was open for 0% -> 15% of each run, Pallas kernels for 0% -> 1%
where the time goes in v1:
time: 235 us; the launch traced here: 233 us
  waiting for transfers between devices  79.4 us (34%)
  starting transfers between devices  56.5 us (24%)
  local copies, waits for them, and re-layouts  40.9 us (17%)
  Pallas kernels  25.5 us (11%)
  between operations  14.6 us (6%)
  other arithmetic  11.7 us (5%)
  matrix products  4.52 us (2%)
    reduce_scatter x1, waiting for transfers between devices, shards(): summed = lax.psum_scatter(partial, 'cand', scatter_dimension=0, tiled=True)  40.4 us
    ppermute x4, waiting for transfers between devices, shards(): packs.append(lax.ppermute(pack, both, exchange_pairs(r, False)))  28.7 us
    unnamed x45, local copies, waits for them, and re-layouts  20.8 us
    ppermute x4, starting transfers between devices, shards(): packs.append(lax.ppermute(pack, both, exchange_pairs(r, False)))  20.6 us
    pallas_call x1, Pallas kernels, feed_forward(): pl.pallas_call(ffn_kernel, out_shape=jax.ShapeDtypeStruct((512, 2048), BF...  16.5 us
    ppermute x4, starting transfers between devices, shards(): arrived.append(lax.ppermute(send, both, exchange_pairs(r, True)))  14.7 us
    ppermute x7, starting transfers between devices, shards(): lax.ppermute(tower_part, 'tok', [(i, i ^ d) for i in range(TOK)])  10.1 us
    pallas_call x1, Pallas kernels, attention(): pl.pallas_call(attention_kernel, out_shape=jax.ShapeDtypeStruct((264, 128...  7.74 us
  transfers between devices with their start and end apart: 25, of which 9 were waited for; matrix products, arithmetic and copies ran while one was open for 15% of the time, Pallas kernels for 1%

profile of v1, /device:TPU:1, one launch (start us, length us, event | category | flops | bytes accessed | tf_op | source)
XLA Modules:
  0.0 233.1 jit_solution(2080472217783373718)
XLA Ops:
  10.5 2.0 convolution_convert_fusion
  12.6 7.7 %attention.1.p0 = f32[264,128]{1,0:T(8,128)S(1)} custom-call(s32[2]{0:T(128)S(1)} %broadcast_subtract_fusion.1.limit_ref, bf16[256,128]{1,0:T(8,128)(2,1)S(1)} %bitcast.66, s32[256,1]{1,0:T(8,128)S(1)} %copy.43.owner_ref, bf16[2,2560,128]{2,1,0:T(8,128)(2,1)S(1)} %copy-done.11, s32[2,2560]{1,0:T(2,128)S(1)} %copy-done.13, bf16[128,128]{1,0:T(8,128)(2,1)S(1)} %bitcast.65, ...), custom_call_target="tpu_custom_call" | custom-call | flops 2000000000 | bytes 2000000 | tf_op jit(solution)/shard_map/attention/pallas_call | solution.py:74
  20.3 2.2 collective-permute-start
  22.5 2.6 %collective-permute-start.1 = (f32[264,128]{1,0:T(8,128)S(1)}, f32[264,128]{1,0:T(8,128)S(1)}, u32[]{:S(2)}, u32[]{:S(2)}) collective-permute-start(f32[264,128]{1,0:T(8,128)S(1)} %attention.1.p0), channel_id=1, source_target_pairs={{0,128},{64,192},{128,0},{192,64},{1,129},{65,193},{129,1},{193,65... | collective-permute-start | bytes 405512 | tf_op jit(solution)/shard_map/ppermute | solution.py:246
  26.2 2.6 %constant_dynamic-slice_fusion = (bf16[1,128,2048]{2,1,0:T(8,128)(2,1)S(1)}, bf16[1,128,2048]{2,1,0:T(8,128)(2,1)}, bf16[1,128,2048]{2,1,0:T(8,128)(2,1)S(1)}, bf16[1,128,2048]{2,1,0:T(8,128)(2,1)S(1)}) fusion(bf16[2,256,2048]{2,1,0:T(8,128)(2,1)} %param.28, s32[]{:T(128)S(6)} %select_n.136, s32[]{:T(128)S(6)} %select_n.138, s32[]{:T(128)S(6)} %select_n.132, ...), kind=kLoop, calls=%fused_computation.37 | loop fusion | bytes 4194336 | tf_op jit(solution)/shard_map/dynamic_slice | solution.py:222
  29.8 1.2 copy.54
  31.0 3.9 %constant_dynamic-slice_fusion.1 = (bf16[1,2048,128]{2,1,0:T(8,128)(2,1)S(1)}, bf16[1,2048,128]{2,1,0:T(8,128)(2,1)}, bf16[1,2048,128]{2,1,0:T(8,128)(2,1)}, bf1...) fusion(bf16[2,2048,256]{2,1,0:T(8,128)(2,1)} %param.27, ...), kind=kLoop, calls=%fused_computation.38 | loop fusion | bytes 8388640 | tf_op jit(solution)/shard_map/dynamic_slice | solution.py:221
  35.0 1.3 pad_maximum_fusion.3
  36.3 1.9 collective-permute-start.6
  38.7 1.3 pad_maximum_fusion.5
  40.1 1.3 pad_maximum_fusion.1
  41.4 11.6 %collective-permute-start.4 = (bf16[24,128,256]{2,1,0:T(8,128)(2,1)}, bf16[24,128,256]{2,1,0:T(8,128)(2,1)}, u32[]{:S(2)}, u32[]{:S(2)}) collective-permute-start(bf16[24,128,256]{2,1,0:T(8,128)(2,1)} %pad_maximum_fusion.1), channel_id=1, source_target_pairs={{0,8},{8,136},{16,24},{24,152},{32,40},{40,168},{48,56},{56,184},{... | collective-permute-start | bytes 4718600 | tf_op jit(solution)/shard_map/ppermute | solution.py:230
  53.0 1.7 reshape.57
  54.7 2.1 copy.60
  56.8 2.1 copy.52
  58.9 1.6 dynamic-slice_reduce_fusion.1
  60.7 1.8 reshape.59
  62.5 2.3 dynamic-slice_reduce_fusion
  65.9 1.2 merge.1
  67.1 4.4 %all-to-all-start = ((bf16[8,64,256]{2,1,0:T(8,128)(2,1)}), bf16[8,64,256]{2,1,0:T(8,128)(2,1)S(1)}, u32[]{:S(2)}, u32[]{:S(2)}) async-start(bf16[8,64,256]{2,1,0:T(8,128)(2,1)} %merge.1), calls=%async_computation | async-start | bytes 524288 | tf_op jit(solution)/shard_map/all_to_all | solution.py:250
  71.5 1.3 pad_maximum_fusion.6
  72.8 5.2 %all-to-all-done = bf16[8,64,256]{2,1,0:T(8,128)(2,1)S(1)} async-done(((bf16[8,64,256]{2,1,0:T(8,128)(2,1)}), bf16[8,64,256]{2,1,0:T(8,128)(2,1)S(1)}, u32[]{:S(2)}, u32[]{:S(2)}) %all-to-all-start) | async-done | bytes 262176 | tf_op jit(solution)/shard_map/all_to_all | solution.py:250
  78.8 1.3 pad_maximum_fusion.2
  80.1 5.2 %collective-permute-start.5 = (bf16[24,128,256]{2,1,0:T(8,128)(2,1)}, bf16[24,128,256]{2,1,0:T(8,128)(2,1)S(1)}, u32[]{:S(2)}, u32[]{:S(2)}) collective-permute-start(bf16[24,128,256]{2,1,0:T(8,128)(2,1)} %pad_maximum_fusion.2), channel_id=1, source_target_pairs={{0,64},{8,192},{16,80},{24,208},{32,96},{40,224},{48,112},{56,240}... | collective-permute-start | bytes 4718600 | tf_op jit(solution)/shard_map/ppermute | solution.py:230
  86.3 1.2 copy.48
  87.5 1.3 pad_maximum_fusion.4
  89.0 1.9 collective-permute-start.3
  91.5 28.3 %collective-permute-done.5.refs_2_ = bf16[24,128,256]{2,1,0:T(8,128)(2,1)S(1)} collective-permute-done((bf16[24,128,256]{2,1,0:T(8,128)(2,1)}, bf16[24,128,256]{2,1,0:T(8,128)(2,1)S(1)}, u32[]{:S(2)}, u32[]{:S(2)}) %collective-permute-start.5) | collective-permute-done | bytes 1572896 | tf_op jit(solution)/shard_map/ppermute | solution.py:230
  120.3 1.2 copy-done.1
  121.5 1.2 copy-done.3
  122.8 1.2 copy-done.5
  125.5 1.2 copy-done.9
  126.7 1.4 copy-done.2
  128.1 1.4 copy-done.4
  129.6 1.4 copy-done.6
  131.0 1.4 copy-done.8
  132.4 1.4 copy-done.10
  133.8 16.5 %feed_forward.1 = bf16[512,2048]{1,0:T(8,128)(2,1)} custom-call(bf16[8,8,64,256]{3,2,1,0:T(8,128)(2,1)} %bitcast.87, bf16[24,128,256]{2,1,0:T(8,128)(2,1)S(1)} %copy-done.2, bf16[24,128,256]{2,1,0:T(8,128)(2,1)} %collective-permute-done.4.refs_1_, bf16[24,128,256]{2,1,0:T(8,128)(2,1)S(1)} %collective-permute-done.5.refs_2_, ...), custom_call_target="tpu_custom_call" | custom-call | flops 6499999744 | bytes 17000000 | tf_op jit(solution)/shard_map/feed_forward/pallas_call | solution.py:162
  151.5 40.4 %reduce-scatter.2.cloned.1.call-done = bf16[64,2048]{1,0:T(8,128)(2,1)} async-done(((bf16[512,2048]{1,0:T(8,128)(2,1)}), bf16[64,2048]{1,0:T(8,128)(2,1)}) %reduce-scatter.2.cloned.1.call-update) | async-done | bytes 262160 | tf_op jit(solution)/shard_map/reduce_scatter | solution.py:255
  192.9 8.5 %collective-permute-start.11 = (bf16[16,2048]{1,0:T(8,128)(2,1)S(1)}, bf16[16,2048]{1,0:T(8,128)(2,1)S(1)}, u32[]{:S(2)}, u32[]{:S(2)}) collective-permute-start(bf16[16,2048]{1,0:T(8,128)(2,1)S(1)} %get-tuple-element.22), channel_id=1, source_target_pairs={{0,0},{128,8},{16,16},{144,24},{32,32},{160,40},{48,48},{176,56},{... | collective-permute-start | bytes 196616 | tf_op jit(solution)/shard_map/ppermute | solution.py:266
  201.6 1.7 collective-permute-start.13
  203.3 4.4 %collective-permute-start.14 = (bf16[16,2048]{1,0:T(8,128)(2,1)S(1)}, bf16[16,2048]{1,0:T(8,128)(2,1)S(1)}, u32[]{:S(2)}, u32[]{:S(2)}) collective-permute-start(bf16[16,2048]{1,0:T(8,128)(2,1)S(1)} %get-tuple-element.23), channel_id=1, source_target_pairs={{72,0},{200,8},{88,16},{216,24},{104,32},{232,40},{120,48},{248,56... | collective-permute-start | bytes 196616 | tf_op jit(solution)/shard_map/ppermute | solution.py:266
  207.8 2.0 collective-permute-done.14
  209.9 1.5 fusion.1
  211.7 2.1 collective-permute-start.15
  215.5 2.6 %collective-permute-start.18 = (f32[32,256]{1,0:T(8,128)S(1)}, f32[32,256]{1,0:T(8,128)S(1)}, u32[]{:S(2)}, u32[]{:S(2)}) collective-permute-start(f32[32,256]{1,0:T(8,128)S(1)} %convolution_add_fusion), channel_id=1, source_target_pairs={{0,32},{8,40},{16,48},{24,56},{32,0},{40,8},{48,16},{56,24},{1,33}... | collective-permute-start | bytes 98312 | tf_op jit(solution)/shard_map/ppermute | solution.py:275
  218.8 2.1 collective-permute-start.20
  224.0 1.5 collective-permute-done.21
  (90 shorter events, 20.5 us)
Async XLA Ops:
  7.2 3.4 %copy-start = (bf16[2,2048,128]{2,1,0:T(8,128)(2,1)S(1)}, bf16[2,2048,128]{2,1,0:T(8,128)(2,1)}, u32[]{:S(2)}) copy-start(bf16[2,2048,128]{2,1,0:T(8,128)(2,1)} %param.17) | copy-start | bytes 3145732
  7.2 5.4 %copy-start.11 = (bf16[2,2560,128]{2,1,0:T(8,128)(2,1)S(1)}, bf16[2,2560,128]{2,1,0:T(8,128)(2,1)}, u32[]{:S(2)}) copy-start(bf16[2,2560,128]{2,1,0:T(8,128)(2,1)} %hist_ref.1) | copy-start | bytes 3932164
  7.2 5.4 %copy-start.13 = (s32[2,2560]{1,0:T(2,128)S(1)}, s32[2,2560]{1,0:T(2,128)}, u32[]{:S(2)}) copy-start(s32[2,2560]{1,0:T(2,128)} %act_ref.1) | copy-start | bytes 61444
  7.2 5.4 %copy-start.12 = (bf16[128,128]{1,0:T(8,128)(2,1)S(1)}, bf16[128,128]{1,0:T(8,128)(2,1)}, u32[]{:S(2)}) copy-start(bf16[128,128]{1,0:T(8,128)(2,1)} %vw_ref.1) | copy-start | bytes 98308
  20.3 45.6 %collective-permute-start = (f32[264,128]{1,0:T(8,128)S(1)}, f32[264,128]{1,0:T(8,128)S(1)}, u32[]{:S(2)}, u32[]{:S(2)}) collective-permute-start(f32[264,128]{1,0:T(8,128)S(1)} %attention.1.p0), channel_id=1, source_target_pairs={{0,64},{64,128},{128,192},{192,0},{1,65},{65,129},{129,193},{193,1... | collective-permute-start | bytes 405512 | tf_op jit(solution)/shard_map/ppermute | solution.py:246
  22.5 43.4 %collective-permute-start.1 = (f32[264,128]{1,0:T(8,128)S(1)}, f32[264,128]{1,0:T(8,128)S(1)}, u32[]{:S(2)}, u32[]{:S(2)}) collective-permute-start(f32[264,128]{1,0:T(8,128)S(1)} %attention.1.p0), channel_id=1, source_target_pairs={{0,128},{64,192},{128,0},{192,64},{1,129},{65,193},{129,1},{193,65... | collective-permute-start | bytes 405512 | tf_op jit(solution)/shard_map/ppermute | solution.py:246
  25.1 40.7 %collective-permute-start.2 = (f32[264,128]{1,0:T(8,128)S(1)}, f32[264,128]{1,0:T(8,128)S(1)}, u32[]{:S(2)}, u32[]{:S(2)}) collective-permute-start(f32[264,128]{1,0:T(8,128)S(1)} %attention.1.p0), channel_id=1, source_target_pairs={{0,192},{64,0},{128,64},{192,128},{1,193},{65,1},{129,65},{193,129... | collective-permute-start | bytes 405512 | tf_op jit(solution)/shard_map/ppermute | solution.py:246
  36.3 54.6 %collective-permute-start.6 = (bf16[24,128,256]{2,1,0:T(8,128)(2,1)}, bf16[24,128,256]{2,1,0:T(8,128)(2,1)}, u32[]{:S(2)}, u32[]{:S(2)}) collective-permute-start(bf16[24,128,256]{2,1,0:T(8,128)(2,1)} %pad_maximum_fusion.3), channel_id=1, source_target_pairs={{0,72},{8,200},{16,88},{24,216},{32,104},{40,232},{48,120},{56,248... | collective-permute-start | bytes 4718600 | tf_op jit(solution)/shard_map/ppermute | solution.py:230
  41.4 49.6 %collective-permute-start.4 = (bf16[24,128,256]{2,1,0:T(8,128)(2,1)}, bf16[24,128,256]{2,1,0:T(8,128)(2,1)}, u32[]{:S(2)}, u32[]{:S(2)}) collective-permute-start(bf16[24,128,256]{2,1,0:T(8,128)(2,1)} %pad_maximum_fusion.1), channel_id=1, source_target_pairs={{0,8},{8,136},{16,24},{24,152},{32,40},{40,168},{48,56},{56,184},{... | collective-permute-start | bytes 4718600 | tf_op jit(solution)/shard_map/ppermute | solution.py:230
  65.8 12.9 %copy-start.14 = (bf16[128,8,256]{2,0,1:T(8,128)(2,1)S(1)}, bf16[128,8,256]{2,0,1:T(8,128)(2,1)}, u32[]{:S(2)}) copy-start(bf16[128,8,256]{2,0,1:T(8,128)(2,1)} %copy.52) | copy-start | bytes 1572868
  67.1 10.9 %all-to-all-start = ((bf16[8,64,256]{2,1,0:T(8,128)(2,1)}), bf16[8,64,256]{2,1,0:T(8,128)(2,1)S(1)}, u32[]{:S(2)}, u32[]{:S(2)}) async-start(bf16[8,64,256]{2,1,0:T(8,128)(2,1)} %merge.1), calls=%async_computation | async-start | bytes 524288 | tf_op jit(solution)/shard_map/all_to_all | solution.py:250
  71.5 55.2 %all-gather.3.cloned.1.call-start = ((), (), s32[]{:S(2)}) async-start(), calls=%async_computation.3 | async-start | bytes 2359296 | tf_op jit(solution)/shard_map/all_gather | solution.py:251
  78.0 0.7 copy-start.15
  78.7 113.2 %reduce-scatter.2.cloned.1.call-start = ((), (), s32[]{:S(2)}) async-start(), calls=%async_computation.2 | async-start | bytes 2359296 | tf_op jit(solution)/shard_map/reduce_scatter | solution.py:255
  80.1 39.7 %collective-permute-start.5 = (bf16[24,128,256]{2,1,0:T(8,128)(2,1)}, bf16[24,128,256]{2,1,0:T(8,128)(2,1)S(1)}, u32[]{:S(2)}, u32[]{:S(2)}) collective-permute-start(bf16[24,128,256]{2,1,0:T(8,128)(2,1)} %pad_maximum_fusion.2), channel_id=1, source_target_pairs={{0,64},{8,192},{16,80},{24,208},{32,96},{40,224},{48,112},{56,240}... | collective-permute-start | bytes 4718600 | tf_op jit(solution)/shard_map/ppermute | solution.py:230
  89.0 31.2 %collective-permute-start.3 = (bf16[24,128,256]{2,1,0:T(8,128)(2,1)S(1)}, bf16[24,128,256]{2,1,0:T(8,128)(2,1)S(1)}, u32[]{:S(2)}, u32[]{:S(2)}) collective-permute-start(bf16[24,128,256]{2,1,0:T(8,128)(2,1)S(1)} %pad_maximum_fusion), channel_id=1, source_target_pairs={{0,0},{8,128},{16,16},{24,144},{32,32},{40,160},{48,48},{56,176},{... | collective-permute-start | bytes 4718600 | tf_op jit(solution)/shard_map/ppermute | solution.py:230
  90.9 30.6 %collective-permute-start.10 = (bf16[24,128,256]{2,1,0:T(8,128)(2,1)}, bf16[24,128,256]{2,1,0:T(8,128)(2,1)S(1)}, u32[]{:S(2)}, u32[]{:S(2)}) collective-permute-start(bf16[24,128,256]{2,1,0:T(8,128)(2,1)} %collective-permute-done.6.refs_3_), channel_id=1, source_target_pairs={{0,8},{8,0},{16,24},{24,16},{32,40},{40,32},{48,56},{56,48},{1,9},... | collective-permute-start | bytes 4718600 | tf_op jit(solution)/shard_map/ppermute | solution.py:253
  91.0 31.7 %collective-permute-start.8 = (bf16[24,128,256]{2,1,0:T(8,128)(2,1)}, bf16[24,128,256]{2,1,0:T(8,128)(2,1)S(1)}, u32[]{:S(2)}, u32[]{:S(2)}) collective-permute-start(bf16[24,128,256]{2,1,0:T(8,128)(2,1)} %collective-permute-done.4.refs_1_), channel_id=1, source_target_pairs={{0,8},{8,0},{16,24},{24,16},{32,40},{40,32},{48,56},{56,48},{1,9},... | collective-permute-start | bytes 4718600 | tf_op jit(solution)/shard_map/ppermute | solution.py:253
  119.8 4.1 %collective-permute-start.9 = (bf16[24,128,256]{2,1,0:T(8,128)(2,1)S(1)}, bf16[24,128,256]{2,1,0:T(8,128)(2,1)S(1)}, u32[]{:S(2)}, u32[]{:S(2)}) collective-permute-start(bf16[24,128,256]{2,1,0:T(8,128)(2,1)S(1)} %collective-permute-done.5.refs_2_), channel_id=1, source_target_pairs={{0,8},{8,0},{16,24},{24,16},{32,40},{40,32},{48,56},{56,48},{1,9},... | collective-permute-start | bytes 4718600 | tf_op jit(solution)/shard_map/ppermute | solution.py:253
  120.2 5.3 %collective-permute-start.7 = (bf16[24,128,256]{2,1,0:T(8,128)(2,1)S(1)}, bf16[24,128,256]{2,1,0:T(8,128)(2,1)S(1)}, u32[]{:S(2)}, u32[]{:S(2)}) collective-permute-start(bf16[24,128,256]{2,1,0:T(8,128)(2,1)S(1)} %collective-permute-done.3.refs_0_), channel_id=1, source_target_pairs={{0,8},{8,0},{16,24},{24,16},{32,40},{40,32},{48,56},{56,48},{1,9},... | collective-permute-start | bytes 4718600 | tf_op jit(solution)/shard_map/ppermute | solution.py:253
  120.3 1.2 copy-start.1
  121.5 1.2 copy-start.3
  122.8 1.2 copy-start.5
  123.9 1.2 copy-start.7
  125.5 1.2 copy-start.9
  126.7 1.4 copy-start.2
  128.1 1.4 copy-start.4
  129.5 1.4 copy-start.6
  131.0 1.4 copy-start.8
  132.4 1.4 copy-start.10
  192.9 14.8 %collective-permute-start.11 = (bf16[16,2048]{1,0:T(8,128)(2,1)S(1)}, bf16[16,2048]{1,0:T(8,128)(2,1)S(1)}, u32[]{:S(2)}, u32[]{:S(2)}) collective-permute-start(bf16[16,2048]{1,0:T(8,128)(2,1)S(1)} %get-tuple-element.22), channel_id=1, source_target_pairs={{0,0},{128,8},{16,16},{144,24},{32,32},{160,40},{48,48},{176,56},{... | collective-permute-start | bytes 196616 | tf_op jit(solution)/shard_map/ppermute | solution.py:266
  201.5 6.3 %collective-permute-start.12 = (bf16[16,2048]{1,0:T(8,128)(2,1)S(1)}, bf16[16,2048]{1,0:T(8,128)(2,1)S(1)}, u32[]{:S(2)}, u32[]{:S(2)}) collective-permute-start(bf16[16,2048]{1,0:T(8,128)(2,1)S(1)} %get-tuple-element.25), channel_id=1, source_target_pairs={{8,0},{136,8},{24,16},{152,24},{40,32},{168,40},{56,48},{184,56},{... | collective-permute-start | bytes 196616 | tf_op jit(solution)/shard_map/ppermute | solution.py:266
  201.6 6.2 %collective-permute-start.13 = (bf16[16,2048]{1,0:T(8,128)(2,1)S(1)}, bf16[16,2048]{1,0:T(8,128)(2,1)S(1)}, u32[]{:S(2)}, u32[]{:S(2)}) collective-permute-start(bf16[16,2048]{1,0:T(8,128)(2,1)S(1)} %get-tuple-element.24), channel_id=1, source_target_pairs={{64,0},{192,8},{80,16},{208,24},{96,32},{224,40},{112,48},{240,56}... | collective-permute-start | bytes 196616 | tf_op jit(solution)/shard_map/ppermute | solution.py:266
  203.3 6.5 %collective-permute-start.14 = (bf16[16,2048]{1,0:T(8,128)(2,1)S(1)}, bf16[16,2048]{1,0:T(8,128)(2,1)S(1)}, u32[]{:S(2)}, u32[]{:S(2)}) collective-permute-start(bf16[16,2048]{1,0:T(8,128)(2,1)S(1)} %get-tuple-element.23), channel_id=1, source_target_pairs={{72,0},{200,8},{88,16},{216,24},{104,32},{232,40},{120,48},{248,56... | collective-permute-start | bytes 196616 | tf_op jit(solution)/shard_map/ppermute | solution.py:266
  207.7 3.7 %copy-start.18 = (bf16[2,2048,256]{2,1,0:T(8,128)(2,1)S(1)}, bf16[2,2048,256]{2,1,0:T(8,128)(2,1)}, u32[]{:S(2)}) copy-start(bf16[2,2048,256]{2,1,0:T(8,128)(2,1)} %param.29) | copy-start | bytes 6291460
  209.8 15.7 %copy-start.16 = (bf16[256,4]{0,1:T(4,128)(2,1)S(1)}, bf16[256,4]{0,1:T(4,128)(2,1)}, u32[]{:S(2)}) copy-start(bf16[256,4]{0,1:T(4,128)(2,1)} %param.31) | copy-start | bytes 6148
  209.8 15.7 %copy-start.17 = (f32[256]{0:T(256)S(1)}, f32[256]{0:T(256)}, u32[]{:S(2)}) copy-start(f32[256]{0:T(256)} %param.30) | copy-start | bytes 3076
  211.7 7.2 %collective-permute-start.15 = (f32[32,256]{1,0:T(8,128)S(1)}, f32[32,256]{1,0:T(8,128)S(1)}, u32[]{:S(2)}, u32[]{:S(2)}) collective-permute-start(f32[32,256]{1,0:T(8,128)S(1)} %convolution_add_fusion), channel_id=1, source_target_pairs={{0,8},{8,0},{16,24},{24,16},{32,40},{40,32},{48,56},{56,48},{1,9},... | collective-permute-start | bytes 98312 | tf_op jit(solution)/shard_map/ppermute | solution.py:275
  213.8 7.2 %collective-permute-start.16 = (f32[32,256]{1,0:T(8,128)S(1)}, f32[32,256]{1,0:T(8,128)S(1)}, u32[]{:S(2)}, u32[]{:S(2)}) collective-permute-start(f32[32,256]{1,0:T(8,128)S(1)} %convolution_add_fusion), channel_id=1, source_target_pairs={{0,16},{8,24},{16,0},{24,8},{32,48},{40,56},{48,32},{56,40},{1,17}... | collective-permute-start | bytes 98312 | tf_op jit(solution)/shard_map/ppermute | solution.py:275
  214.7 8.2 %collective-permute-start.17 = (f32[32,256]{1,0:T(8,128)S(1)}, f32[32,256]{1,0:T(8,128)S(1)}, u32[]{:S(2)}, u32[]{:S(2)}) collective-permute-start(f32[32,256]{1,0:T(8,128)S(1)} %convolution_add_fusion), channel_id=1, source_target_pairs={{0,24},{8,16},{16,8},{24,0},{32,56},{40,48},{48,40},{56,32},{1,25}... | collective-permute-start | bytes 98312 | tf_op jit(solution)/shard_map/ppermute | solution.py:275
  215.5 7.3 %collective-permute-start.18 = (f32[32,256]{1,0:T(8,128)S(1)}, f32[32,256]{1,0:T(8,128)S(1)}, u32[]{:S(2)}, u32[]{:S(2)}) collective-permute-start(f32[32,256]{1,0:T(8,128)S(1)} %convolution_add_fusion), channel_id=1, source_target_pairs={{0,32},{8,40},{16,48},{24,56},{32,0},{40,8},{48,16},{56,24},{1,33}... | collective-permute-start | bytes 98312 | tf_op jit(solution)/shard_map/ppermute | solution.py:275
  218.1 5.0 %collective-permute-start.19 = (f32[32,256]{1,0:T(8,128)S(1)}, f32[32,256]{1,0:T(8,128)S(1)}, u32[]{:S(2)}, u32[]{:S(2)}) collective-permute-start(f32[32,256]{1,0:T(8,128)S(1)} %convolution_add_fusion), channel_id=1, source_target_pairs={{0,40},{8,32},{16,56},{24,48},{32,8},{40,0},{48,24},{56,16},{1,41}... | collective-permute-start | bytes 98312 | tf_op jit(solution)/shard_map/ppermute | solution.py:275
  218.8 5.2 %collective-permute-start.20 = (f32[32,256]{1,0:T(8,128)S(1)}, f32[32,256]{1,0:T(8,128)S(1)}, u32[]{:S(2)}, u32[]{:S(2)}) collective-permute-start(f32[32,256]{1,0:T(8,128)S(1)} %convolution_add_fusion), channel_id=1, source_target_pairs={{0,48},{8,56},{16,32},{24,40},{32,16},{40,24},{48,0},{56,8},{1,49}... | collective-permute-start | bytes 98312 | tf_op jit(solution)/shard_map/ppermute | solution.py:275
  221.0 4.6 %collective-permute-start.21 = (f32[32,256]{1,0:T(8,128)S(1)}, f32[32,256]{1,0:T(8,128)S(1)}, u32[]{:S(2)}, u32[]{:S(2)}) collective-permute-start(f32[32,256]{1,0:T(8,128)S(1)} %convolution_add_fusion), channel_id=1, source_target_pairs={{0,56},{8,48},{16,40},{24,32},{32,24},{40,16},{48,8},{56,0},{1,57}... | collective-permute-start | bytes 98312 | tf_op jit(solution)/shard_map/ppermute | solution.py:275
Sparse Core Ops, SparseCore 0:
  78.9 40.2 all-gather.2
  150.5 41.3 reduce-scatter.1

commit v2 on v1

v2 whole, which is shorter than its diff:
```python
import jax
import jax.numpy as jnp
from jax import lax
from jax.experimental import pallas as pl
from jax.experimental.pallas import tpu as pltpu
from jax.sharding import PartitionSpec as P

EPS = 1e-06
DK = 128
ACTIONS = 16
HIST, TOK, CAND = 4, 8, 8
SCALE = 1.5 * DK ** (-0.5) * 1.4426950408889634
CHUNK = 512
F32 = jnp.float32
BF16 = jnp.bfloat16


def dot(a, b, dims=((1,), (0,))):
    return lax.dot_general(a, b, (dims, ((), ())), preferred_element_type=F32)


def pack_copies(gate_ref, up_ref, down_ref, held, sem):
    y = lax.axis_index("hist")
    copies = []
    for r in range(4):
        j, k = lax.rem(y // 2 + r // 2, 2), lax.rem(y + r, 2)
        half = pl.ds(pl.multiple_of(k * 128, 128), 128)
        moves = [
            (gate_ref.at[j, :, half], held.at[r, pl.ds(0, 2048), pl.ds(0, 128)]),
            (up_ref.at[j, :, half], held.at[r, pl.ds(0, 2048), pl.ds(128, 128)]),
        ]
        for g in range(8):
            moves.append((down_ref.at[j, half, pl.ds(g * 256, 256)], held.at[r, pl.ds(2048 + g * 128, 128), :]))
        copies += [pltpu.make_async_copy(source, target, sem.at[r, n]) for n, (source, target) in enumerate(moves)]
    return copies


def unload_copies(held, packs, sem):
    return [pltpu.make_async_copy(held.at[r], packs[r], sem.at[r, 10]) for r in range(4)]


def attention_kernel(length_ref, q_ref, user_ref, hist_ref, act_ref, kw_ref, tab_ref, vw_ref, gate_ref, up_ref, down_ref, *refs):
    out_ref, packs, (m_ref, l_ref, acc_ref, kwt_ref, tabt_ref, owner_ref, held, sem) = refs[0], refs[1:5], refs[5:]
    step = pl.program_id(0)
    events = CHUNK * pl.num_programs(0)
    offset = lax.axis_index("hist") * events + step * CHUNK

    @pl.when(step == 0)
    def _():
        for copy in pack_copies(gate_ref, up_ref, down_ref, held, sem):
            copy.start()
        m_ref[...] = jnp.full_like(m_ref, -1e29)
        l_ref[...] = jnp.zeros_like(l_ref)
        acc_ref[...] = jnp.zeros_like(acc_ref)
        kwt_ref[...] = jnp.transpose(kw_ref[...].astype(F32)).astype(BF16)
        tabt_ref[...] = jnp.transpose(tab_ref[...].astype(F32)).astype(BF16)
        user = jnp.transpose(jnp.broadcast_to(user_ref[...], (128, 128))) - lax.axis_index("cand") * 2
        owner_ref[0:128, :] = user[:, 0:1]
        owner_ref[128:256, :] = user[:, 0:1]

    @pl.when(step == 3)
    def _():
        for copy in pack_copies(gate_ref, up_ref, down_ref, held, sem):
            copy.wait()
        for copy in unload_copies(held, packs, sem):
            copy.start()

    first = owner_ref[...] == 0
    q = q_ref[...]
    where = lax.broadcasted_iota(jnp.int32, (1, CHUNK), 1) + offset
    scores, values = [], []
    for u in range(2):
        h = hist_ref[u]
        kinds = lax.broadcasted_iota(jnp.int32, (ACTIONS, CHUNK), 0)
        onehot = jnp.where(kinds == act_ref[u : u + 1, :], 1.0, 0.0).astype(BF16)
        keys = dot(kwt_ref[...], h, ((1,), (1,))) + dot(tabt_ref[...], onehot)
        s = dot(q, keys.astype(BF16)) * SCALE
        scores.append(jnp.where(where < length_ref[u], s, -1e30))
        wide = h.astype(F32)
        normed = wide * lax.rsqrt(jnp.mean(wide * wide, axis=1, keepdims=True) + EPS)
        values.append(dot(normed.astype(BF16), vw_ref[...]).astype(BF16))
    s = jnp.where(first, scores[0], scores[1])
    m_old = m_ref[...]
    m_new = jnp.maximum(m_old, jnp.max(s, axis=1, keepdims=True))
    p = jnp.exp2(s - m_new)
    fade = jnp.exp2(m_old - m_new)
    m_ref[...] = m_new
    l_ref[...] = l_ref[...] * fade + jnp.sum(p, axis=1, keepdims=True)
    acc_ref[...] = acc_ref[...] * fade + dot(p.astype(BF16), jnp.concatenate(values, axis=1))

    @pl.when(step == pl.num_programs(0) - 1)
    def _():
        weighted = jnp.where(first, acc_ref[:, 0:128], acc_ref[:, 128:256])
        out_ref[0:256, :] = (weighted / jnp.maximum(l_ref[...], 1e-30)).astype(BF16)
        for n, ref in ((256, m_ref), (272, l_ref)):
            row = jnp.transpose(jnp.broadcast_to(ref[...], (256, 128)))[0:1, :]
            rows = []
            for _ in range(3):
                piece = row.astype(BF16).astype(F32)
                row = row - piece
                rows += [piece[:, 0:128], piece[:, 128:256]]
            rows += [jnp.zeros((10, 128), F32)]
            out_ref[n : n + 16, :] = jnp.concatenate(rows, axis=0).astype(BF16)
        for copy in unload_copies(held, packs, sem):
            copy.wait()


def attention(lengths, queries, user, history, actions, kw, tab, vw, gate, up, down):
    steps = history.shape[1] // CHUNK
    whole = lambda *shape: pl.BlockSpec(shape, lambda i, lim: (0,) * len(shape))
    anywhere = pl.BlockSpec(memory_space=pl.ANY)
    return pl.pallas_call(
        attention_kernel,
        out_shape=[jax.ShapeDtypeStruct((288, 128), BF16)] + [jax.ShapeDtypeStruct((3072, 256), BF16)] * 4,
        grid_spec=pltpu.PrefetchScalarGridSpec(
            num_scalar_prefetch=1,
            grid=(steps,),
            in_specs=[
                whole(256, 128),
                whole(1, 128),
                pl.BlockSpec((2, CHUNK, 128), lambda i, lim: (0, i, 0)),
                pl.BlockSpec((2, CHUNK), lambda i, lim: (0, i)),
                whole(128, 128),
                whole(ACTIONS, 128),
                whole(128, 128),
                anywhere,
                anywhere,
                anywhere,
            ],
            out_specs=[whole(288, 128)] + [anywhere] * 4,
            scratch_shapes=[
                pltpu.VMEM((256, 1), F32),
                pltpu.VMEM((256, 1), F32),
                pltpu.VMEM((256, 256), F32),
                pltpu.VMEM((128, 128), BF16),
                pltpu.VMEM((128, ACTIONS), BF16),
                pltpu.VMEM((256, 1), jnp.int32),
                pltpu.VMEM((4, 3072, 256), BF16),
                pltpu.SemaphoreType.DMA((4, 11)),
            ],
        ),
        compiler_params=pltpu.CompilerParams(dimension_semantics=("arbitrary",), vmem_limit_bytes=58 << 20),
        cost_estimate=pl.CostEstimate(flops=1_000_000, bytes_accessed=100_000, transcendentals=1_000),
        name="attention",
    )(lengths, queries, user, history, actions, kw, tab, vw, gate, up, down)


def merge_kernel(p0, p1, p2, p3, feat_ref, ow_ref, out_ref):
    parts = (p0, p1, p2, p3)

    def column(ref, n):
        pieces = ref[n : n + 16, :].astype(F32)
        rows = pieces[0:2] + (pieces[2:4] + pieces[4:6])
        rows = [jnp.transpose(jnp.broadcast_to(rows[i : i + 1], (128, 128))) for i in range(2)]
        return jnp.concatenate(rows, axis=0)

    maxima = [column(ref, 256) for ref in parts]
    top = jnp.maximum(jnp.maximum(maxima[0], maxima[1]), jnp.maximum(maxima[2], maxima[3]))
    total, weighted = 0.0, 0.0
    for ref, m in zip(parts, maxima):
        share = column(ref, 272) * jnp.exp2(m - top)
        total += share
        weighted += ref[0:256, :].astype(F32) * share
    attended = (weighted / total).astype(BF16)
    y = lax.axis_index("hist")
    for x in range(4):
        columns = pl.ds(pl.multiple_of((4 * x + y) * 128, 128), 128)
        for j in range(2):
            update = dot(attended[j * 128 : (j + 1) * 128], ow_ref[j, :, columns])
            tokens = (feat_ref[j, :, columns].astype(F32) + update).astype(BF16)
            for k in range(2):
                for m in range(4):
                    out_ref[2 * x + k, m * 16 : (m + 1) * 16, j * 128 : (j + 1) * 128] = tokens[
                        m * 32 + k * 16 : m * 32 + k * 16 + 16
                    ]


def merge(parts, feats, ow):
    return pl.pallas_call(
        merge_kernel,
        out_shape=jax.ShapeDtypeStruct((8, 64, 256), BF16),
        compiler_params=pltpu.CompilerParams(vmem_limit_bytes=16 << 20),
        cost_estimate=pl.CostEstimate(flops=70_000_000, bytes_accessed=1_500_000, transcendentals=150_000),
        name="merge",
    )(*parts, feats, ow)


def hidden_part(normed, weights, hidden, p):
    both = dot(normed[...], weights)
    gate, up = both[:, :128], both[:, 128:]
    hidden[:, p * 128 : (p + 1) * 128] = (gate / (1.0 + jnp.exp(-gate)) * up).astype(BF16)


def first_kernel(x_ref, *refs):
    packs, (normed, hidden, gu, sem) = refs[:4], refs[4:]
    copies = [pltpu.make_async_copy(packs[p].at[pl.ds(0, 2048)], gu.at[p], sem.at[p]) for p in range(4)]
    for copy in copies:
        copy.start()
    z = lax.axis_index("cand")
    for zb in range(8):
        wide = jnp.concatenate([x_ref[zb, s] for s in range(8)], axis=1).astype(F32)
        rows = (wide * lax.rsqrt(jnp.mean(wide * wide, axis=1, keepdims=True) + EPS)).astype(BF16)
        for m in range(4):
            away = lax.rem((zb % 2) * 4 + m + 8 - z, 8)
            to = pl.multiple_of(away * 64 + (zb // 2) * 16, 16)
            normed[pl.ds(to, 16), :] = rows[m * 16 : (m + 1) * 16]
    for p in range(4):
        copies[p].wait()
        hidden_part(normed, gu[p], hidden, p)


def middle_kernel(normed, hidden_in, *refs):
    early, late, (so_far,), (hidden, gu, dn, gu_sem, dn_sem) = refs[:4], refs[4:6], refs[6:7], refs[7:]
    gu_copies = [pltpu.make_async_copy(late[p].at[pl.ds(0, 2048)], gu.at[p], gu_sem.at[p]) for p in range(2)]
    dn_copies = [
        pltpu.make_async_copy(pack.at[pl.ds(2048, 1024)], dn.at[p], dn_sem.at[p])
        for p, pack in enumerate(early + late)
    ]
    for copy in gu_copies + dn_copies:
        copy.start()
    for p in range(4):
        hidden[:, p * 128 : (p + 1) * 128] = hidden_in[:, p * 128 : (p + 1) * 128]
    for p in range(2):
        gu_copies[p].wait()
        hidden_part(normed, gu[p], hidden, 4 + p)
    for copy in dn_copies:
        copy.wait()
    for g in range(8):
        weights = jnp.concatenate([dn[p, g * 128 : (g + 1) * 128, :] for p in range(6)], axis=0)
        so_far[:, g * 256 : (g + 1) * 256] = dot(hidden[...], weights)


FAR = slice(256, 320)


def last_columns(normed, so_far, packs, hidden, g):
    weights = jnp.concatenate([pack[2048 + g * 128 : 2176 + g * 128, :] for pack in packs], axis=0)
    return (so_far[:, g * 256 : (g + 1) * 256] + dot(hidden[...], weights)).astype(BF16)


def far_kernel(normed, so_far, *refs):
    packs, (far_a, far_b, hidden) = refs[:2], refs[2:]
    for p in range(2):
        hidden_part(normed.at[FAR], packs[p][0:2048, :], hidden, p)
    for g in range(8):
        (far_a, far_b)[g // 4][:, (g % 4) * 256 : (g % 4 + 1) * 256] = last_columns(
            normed, so_far.at[FAR], packs, hidden, g
        )


def near_kernel(normed, so_far, *refs):
    packs, (near, hidden) = refs[:2], refs[2:]
    for p in range(2):
        hidden_part(normed, packs[p][0:2048, :], hidden, p)
    for g in range(8):
        columns = last_columns(normed, so_far, packs, hidden, g)
        for away in range(8):
            near[away, :, g * 256 : (g + 1) * 256] = columns[away * 64 : (away + 1) * 64]


def gate_kernel(*refs):
    pass


def gated(packs):
    shape = jax.ShapeDtypeStruct((3072, 256), BF16)
    n = len(packs)
    return pl.pallas_call(
        gate_kernel,
        out_shape=[shape] * n,
        in_specs=[pl.BlockSpec(memory_space=pl.ANY)] * n,
        out_specs=[pl.BlockSpec(memory_space=pl.ANY)] * n,
        input_output_aliases={i: i for i in range(n)},
        cost_estimate=pl.CostEstimate(flops=200_000_000_000, bytes_accessed=1000, transcendentals=0),
        name="gate",
    )(*packs)


VMEM_SPEC = pl.BlockSpec(memory_space=pltpu.VMEM)
ANY_SPEC = pl.BlockSpec(memory_space=pl.ANY)
FFN_PARAMS = pltpu.CompilerParams(vmem_limit_bytes=28 << 20)
FFN_COST = pl.CostEstimate(flops=3_000_000_000, bytes_accessed=8_000_000, transcendentals=300_000)


def feed_forward_first(x, packs):
    return pl.pallas_call(
        first_kernel,
        out_shape=[jax.ShapeDtypeStruct((512, 2048), BF16), jax.ShapeDtypeStruct((512, 512), BF16)],
        in_specs=[VMEM_SPEC] + [ANY_SPEC] * 4,
        out_specs=[VMEM_SPEC] * 2,
        scratch_shapes=[pltpu.VMEM((4, 2048, 256), BF16), pltpu.SemaphoreType.DMA((4,))],
        compiler_params=FFN_PARAMS,
        cost_estimate=FFN_COST,
        name="feed_forward_first",
    )(x, *packs)


def feed_forward_middle(normed, hidden, early, late):
    return pl.pallas_call(
        middle_kernel,
        out_shape=jax.ShapeDtypeStruct((512, 2048), F32),
        in_specs=[VMEM_SPEC] * 2 + [ANY_SPEC] * 6,
        out_specs=VMEM_SPEC,
        scratch_shapes=[
            pltpu.VMEM((512, 768), BF16),
            pltpu.VMEM((2, 2048, 256), BF16),
            pltpu.VMEM((6, 1024, 256), BF16),
            pltpu.SemaphoreType.DMA((2,)),
            pltpu.SemaphoreType.DMA((6,)),
        ],
        compiler_params=FFN_PARAMS,
        cost_estimate=FFN_COST,
        name="feed_forward_middle",
    )(normed, hidden, *early, *late)


def feed_forward_last(kernel, rows, outs, normed, so_far, packs, name):
    return pl.pallas_call(
        kernel,
        out_shape=[jax.ShapeDtypeStruct(shape, BF16) for shape in outs],
        in_specs=[VMEM_SPEC] * 4,
        out_specs=[VMEM_SPEC] * len(outs),
        scratch_shapes=[pltpu.VMEM((rows, 256), BF16)],
        compiler_params=FFN_PARAMS,
        cost_estimate=FFN_COST,
        name=name,
    )(normed, so_far, *packs)


def exchange_pairs(r, reverse):
    pairs = []
    for y in range(HIST):
        for t in range(TOK):
            x, c = t // 2, t % 2
            q = y ^ r
            source, target = (y, 2 * x + c), (2 * c + q // 2, 2 * x + q % 2)
            if reverse:
                source, target = target, source
            pairs.append((source[0] * TOK + source[1], target[0] * TOK + target[1]))
    return pairs


def shards(
    features,
    query_weight,
    output_weight,
    history,
    actions,
    lengths,
    cand_user,
    key_weight,
    action_table,
    value_weight,
    gate_weight,
    up_weight,
    down_weight,
    tower_weight,
    tower_bias,
    head_weight,
):
    y, tok, z = lax.axis_index("hist"), lax.axis_index("tok"), lax.axis_index("cand")
    core = tok % 2
    both = ("hist", "tok")

    feats = jnp.swapaxes(features, 0, 1)
    queries = jnp.einsum("tbd,tdk->tbk", feats, query_weight, preferred_element_type=F32).astype(BF16)
    part, *packs = attention(
        lengths,
        queries.reshape(256, 128),
        cand_user[None, :],
        history,
        actions,
        key_weight,
        action_table,
        value_weight,
        gate_weight,
        up_weight,
        down_weight,
    )
    parts = [part] + [lax.ppermute(part, "hist", [(i, (i + d) % HIST) for i in range(HIST)]) for d in (1, 2, 3)]
    packs, parts = lax.optimization_barrier((packs, parts))
    packs = [lax.ppermute(pack, both, exchange_pairs(r, False)) for r, pack in enumerate(packs)]

    outgoing = merge(parts, feats, output_weight)
    mixed = lax.all_to_all(outgoing, "tok", split_axis=0, concat_axis=0, tiled=True)
    gathered = lax.all_gather(mixed[None], "cand", axis=0, tiled=True)

    swap = lambda v: lax.ppermute(v, "tok", [(i, i ^ 1) for i in range(TOK)])
    early = list(gated(packs[:2]))
    late, early = lax.optimization_barrier((packs[2:], early))
    late = list(gated(late))
    own, swapped = early + late, [swap(v) for v in early + late]
    normed, hidden = feed_forward_first(gathered, own)
    so_far = feed_forward_middle(normed, hidden, own, swapped[:2])
    far_a, far_b = feed_forward_last(
        far_kernel, 64, ((64, 1024), (64, 1024)), normed, so_far, swapped[2:], "feed_forward_far"
    )
    (near,) = feed_forward_last(near_kernel, 512, ((8, 64, 2048),), normed, so_far, swapped[2:], "feed_forward_near")
    right = [(i, (i + 1) % CAND) for i in range(CAND)]
    left = [(i, (i - 1) % CAND) for i in range(CAND)]
    wide = lambda v: v.astype(F32)
    add = lambda v, w: (wide(v) + wide(w)).astype(BF16)
    up, down = lax.ppermute(far_a, "cand", right), lax.ppermute(far_b, "cand", left)
    up, down = jnp.pad(up, ((0, 0), (0, 1024))), jnp.pad(down, ((0, 0), (1024, 0)))
    for i in (3, 2, 1):
        up, down = lax.optimization_barrier((add(near[i], up), add(near[8 - i], down)))
        up, down = lax.ppermute(up, "cand", right), lax.ppermute(down, "cand", left)
    residual = lax.dynamic_slice(
        gathered.reshape(4, 2, 8, 4, 16, 256), (0, z // 4, 0, z % 4, 0, 0), (4, 1, 8, 1, 16, 256)
    ).reshape(4, 8, 16, 256)
    residual = jnp.swapaxes(residual, 1, 2).reshape(64, 2048)
    block = (wide(residual) + (wide(near[0]) + wide(up) + wide(down))).astype(BF16).reshape(4, 16, 2048)

    arrived = []
    mine = (y % 2) * 2 + core
    for r in range(4):
        send = lax.dynamic_index_in_dim(block, mine ^ r, 0, keepdims=False)
        arrived.append(lax.ppermute(send, both, exchange_pairs(r, True)))
    arrived = jnp.stack(arrived)
    quarters = [lax.dynamic_index_in_dim(arrived, y ^ q, 0, keepdims=False) for q in range(4)]
    tokens = [jnp.concatenate(quarters[2 * j : 2 * j + 2], axis=0) for j in range(2)]
    layer_out = jnp.stack(tokens, axis=1)

    tower_part = dot(tokens[0], tower_weight[0]) + dot(tokens[1], tower_weight[1])
    tower_part += swap(tower_part)
    tower_sum = tower_part
    for d in (2, 4, 6):
        tower_sum += lax.ppermute(tower_part, "tok", [(i, i ^ d) for i in range(TOK)])
    tower_hidden = jax.nn.silu(tower_sum + tower_bias).astype(BF16)
    task_scores = jnp.dot(tower_hidden, head_weight, preferred_element_type=F32)
    return (layer_out, task_scores)


def solution(mesh):
    in_specs = (
        P("cand", "tok", None),
        P("tok", None, None),
        P("tok", None, None),
        P("cand", "hist", None),
        P("cand", "hist"),
        P("cand"),
        P("cand"),
        P(),
        P(),
        P(),
        P("tok", None, ("hist", "cand")),
        P("tok", None, ("hist", "cand")),
        P("tok", ("hist", "cand"), None),
        P("tok", None, None),
        P(),
        P(),
    )
    out_specs = (P(("hist", "cand"), "tok", None), P(("hist", "cand"), None))
    return jax.shard_map(shards, mesh=mesh, in_specs=in_specs, out_specs=out_specs, check_vma=False)
```

time: 235 us -> 205 us (0.87)
  local copies, waits for them, and re-layouts: 40.9 us -> 8.9 us
  waiting for transfers between devices: 79.4 us -> 93.6 us
  other arithmetic: 11.7 us -> 2.35 us
  starting transfers between devices: 56.5 us -> 48.9 us
  Pallas kernels: 25.5 us -> 29 us
    ppermute x8 -> x17, waiting for transfers between devices: 29.1 us -> 80 us  [the longest x4 60.5 us: shards(): lax.ppermute(pack, both, exchange_pairs(r, False))]
    reduce_scatter x1 -> x0, waiting for transfers between devices: 40.4 us -> none  [shards(): summed = lax.psum_scatter(partial, 'cand', scatter_dimension=0, tiled=True)]
    unnamed x45 -> x31, local copies, waits for them, and re-layouts: 20.8 us -> 7.87 us
    reshape x9 -> x0, local copies, waits for them, and re-layouts: 9.46 us -> none  [the longest x4 4.76 us: shards(): down.reshape(128, 8, 256)]
    dynamic_slice x4 -> x1, local copies, waits for them, and re-layouts: 10.4 us -> 0.97 us  [shards(): lax.dynamic_slice(gathered.reshape(4, 2, 8, 4, 16, 256), (0, z // 4, 0, z...]
    concatenate x9 -> x0, other arithmetic: 8.12 us -> none  [the longest x4 4.06 us: shards(): jnp.concatenate([gate, up], axis=2).reshape(16, 128, 256)]
    ppermute x7 -> x3, starting transfers between devices: 10.1 us -> 3.27 us  [shards(): lax.ppermute(tower_part, 'tok', [(i, i ^ d) for i in range(TOK)])]
    ppermute x4, starting transfers between devices: 14.7 us -> 9.88 us  [shards(): arrived.append(lax.ppermute(send, both, exchange_pairs(r, True)))]
  transfers between devices with their start and end apart: 25 -> 29, of which waited for: 9 -> 17; matrix products, arithmetic and copies ran while one was open for 15% -> 1% of each run, Pallas kernels for 1% -> 8%
where the time goes in v2:
time: 205 us; the launch traced here: 202 us
  waiting for transfers between devices  93.6 us (46%)
  starting transfers between devices  48.9 us (24%)
  Pallas kernels  29 us (14%)
  between operations  14.4 us (7%)
  local copies, waits for them, and re-layouts  8.9 us (4%)
  matrix products  5.16 us (3%)
  other arithmetic  2.35 us (1%)
    ppermute x4, waiting for transfers between devices, shards(): lax.ppermute(pack, both, exchange_pairs(r, False))  60.5 us
    ppermute x3, waiting for transfers between devices, shards(): lax.ppermute(down, 'cand', left)  11.4 us
    pallas_call x1, Pallas kernels, attention(): pl.pallas_call(attention_kernel, out_shape=[jax.ShapeDtypeStruct((288, 12...  10.6 us
    ppermute x4, starting transfers between devices, shards(): arrived.append(lax.ppermute(send, both, exchange_pairs(r, True)))  9.88 us
    ppermute x4, starting transfers between devices, shards(): lax.ppermute(pack, both, exchange_pairs(r, False))  9.85 us
    unnamed x31, local copies, waits for them, and re-layouts  7.87 us
    ppermute x3, waiting for transfers between devices, shards(): lax.ppermute(up, 'cand', right)  6.12 us
    pallas_call x2, Pallas kernels, feed_forward_last(): pl.pallas_call(kernel, out_shape=[jax.ShapeDtypeStruct(shape, BF16) for s...  5.98 us
  transfers between devices with their start and end apart: 29, of which 17 were waited for; matrix products, arithmetic and copies ran while one was open for 1% of the time, Pallas kernels for 8%

profile of v2, /device:TPU:1, one launch (start us, length us, event | category | flops | bytes accessed | tf_op | source)
XLA Modules:
  0.0 202.3 jit_solution(15480279475635949267)
XLA Ops:
  7.2 1.2 copy-done
  8.4 2.6 %convolution_convert_fusion = bf16[2,128,128]{2,1,0:T(8,128)(2,1)} fusion(bf16[2,2048,128]{2,1,0:T(8,128)(2,1)S(1)} %copy-done, bf16[128,2,2048]{2,1,0:T(2,128)(2,1)} %param.16), kind=kOutput, calls=%fused_computation | convolution fusion | flops 134250496 | bytes 2162688 | tf_op jit(solution)/shard_map/tbd,tdk->tbk/dot_general | solution.py:366
  11.0 10.6 %attention.1 = (bf16[288,128]{1,0:T(8,128)(2,1)}, bf16[3072,256]{1,0:T(8,128)(2,1)}, bf16[3072,256]{1,0:T(8,128)(2,1)}, bf16[3072,256]{1,0:T(8,128)(2,1)}, bf16[3072,256]{1,0:T(8,128)(2,1)}) custom-call(s32[2]{0:T(128)} %length_ref.1, bf16[256,128]{1,0:T(8,128)(2,1)} %bitcast.91, s32[1,128]{1,0:T(1,128)} %bitcast.96, bf16[2,2560,128]{2,1,0:T(8,128)(2,1)} %hist_ref.1, ...), custom_call_target="tpu_custom_call" | custom-call | flops 1000000 | bytes 100000 | tf_op jit(solution)/shard_map/attention/pallas_call | solution.py:112
  21.6 2.2 %collective-permute-start = (bf16[288,128]{1,0:T(8,128)(2,1)}, bf16[288,128]{1,0:T(8,128)(2,1)S(1)}, u32[]{:S(2)}, u32[]{:S(2)}) collective-permute-start(bf16[288,128]{1,0:T(8,128)(2,1)} %get-tuple-element.38.p0), channel_id=1, source_target_pairs={{0,64},{64,128},{128,192},{192,0},{1,65},{65,129},{129,193},{193,1... | collective-permute-start | bytes 221192 | tf_op jit(solution)/shard_map/ppermute | solution.py:380
  23.8 2.6 %collective-permute-start.1 = (bf16[288,128]{1,0:T(8,128)(2,1)}, bf16[288,128]{1,0:T(8,128)(2,1)S(1)}, u32[]{:S(2)}, u32[]{:S(2)}) collective-permute-start(bf16[288,128]{1,0:T(8,128)(2,1)} %get-tuple-element.38.p0), channel_id=1, source_target_pairs={{0,128},{64,192},{128,0},{192,64},{1,129},{65,193},{129,1},{193,65... | collective-permute-start | bytes 221192 | tf_op jit(solution)/shard_map/ppermute | solution.py:380
  26.5 1.1 collective-permute-start.2
  27.5 2.1 %collective-permute-done.1.p2 = bf16[288,128]{1,0:T(8,128)(2,1)S(1)} collective-permute-done((bf16[288,128]{1,0:T(8,128)(2,1)}, bf16[288,128]{1,0:T(8,128)(2,1)S(1)}, u32[]{:S(2)}, u32[]{:S(2)}) %collective-permute-start.1) | collective-permute-done | bytes 73760 | tf_op jit(solution)/shard_map/ppermute | solution.py:380
  30.2 5.3 %collective-permute-start.5 = (bf16[3072,256]{1,0:T(8,128)(2,1)}, bf16[3072,256]{1,0:T(8,128)(2,1)S(1)}, u32[]{:S(2)}, u32[]{:S(2)}) collective-permute-start(bf16[3072,256]{1,0:T(8,128)(2,1)} %get-tuple-element.44), channel_id=1, source_target_pairs={{0,0},{8,128},{16,16},{24,144},{32,32},{40,160},{48,48},{56,176},{... | collective-permute-start | bytes 4718600 | tf_op jit(solution)/shard_map/ppermute | solution.py:382
  35.5 2.3 %collective-permute-start.6 = (bf16[3072,256]{1,0:T(8,128)(2,1)}, bf16[3072,256]{1,0:T(8,128)(2,1)}, u32[]{:S(2)}, u32[]{:S(2)}) collective-permute-start(bf16[3072,256]{1,0:T(8,128)(2,1)} %get-tuple-element.45), channel_id=1, source_target_pairs={{0,8},{8,136},{16,24},{24,152},{32,40},{40,168},{48,56},{56,184},{... | collective-permute-start | bytes 4718600 | tf_op jit(solution)/shard_map/ppermute | solution.py:382
  38.2 1.3 merge.1
  39.5 4.2 %all-to-all-start = ((bf16[8,64,256]{2,1,0:T(8,128)(2,1)}), bf16[8,64,256]{2,1,0:T(8,128)(2,1)S(1)}, u32[]{:S(2)}, u32[]{:S(2)}) async-start(bf16[8,64,256]{2,1,0:T(8,128)(2,1)} %merge.1), calls=%async_computation | async-start | bytes 524288 | tf_op jit(solution)/shard_map/all_to_all | solution.py:385
  43.7 2.2 %collective-permute-start.4 = (bf16[3072,256]{1,0:T(8,128)(2,1)}, bf16[3072,256]{1,0:T(8,128)(2,1)}, u32[]{:S(2)}, u32[]{:S(2)}) collective-permute-start(bf16[3072,256]{1,0:T(8,128)(2,1)} %get-tuple-element.43), channel_id=1, source_target_pairs={{0,72},{8,200},{16,88},{24,216},{32,104},{40,232},{48,120},{56,248... | collective-permute-start | bytes 4718600 | tf_op jit(solution)/shard_map/ppermute | solution.py:382
  45.9 4.7 %all-to-all-done = bf16[8,64,256]{2,1,0:T(8,128)(2,1)S(1)} async-done(((bf16[8,64,256]{2,1,0:T(8,128)(2,1)}), bf16[8,64,256]{2,1,0:T(8,128)(2,1)S(1)}, u32[]{:S(2)}, u32[]{:S(2)}) %all-to-all-start) | async-done | bytes 262176 | tf_op jit(solution)/shard_map/all_to_all | solution.py:385
  51.3 11.1 %collective-permute-done.5.refs_0_ = bf16[3072,256]{1,0:T(8,128)(2,1)S(1)} collective-permute-done((bf16[3072,256]{1,0:T(8,128)(2,1)}, bf16[3072,256]{1,0:T(8,128)(2,1)S(1)}, u32[]{:S(2)}, u32[]{:S(2)}) %collective-permute-start.5) | collective-permute-done | bytes 1572896 | tf_op jit(solution)/shard_map/ppermute | solution.py:382
  62.4 32.9 %collective-permute-done.6.refs_1_ = bf16[3072,256]{1,0:T(8,128)(2,1)} collective-permute-done((bf16[3072,256]{1,0:T(8,128)(2,1)}, bf16[3072,256]{1,0:T(8,128)(2,1)}, u32[]{:S(2)}, u32[]{:S(2)}) %collective-permute-start.6) | collective-permute-done | bytes 1572896 | tf_op jit(solution)/shard_map/ppermute | solution.py:382
  95.3 16.5 %collective-permute-done.4.refs_1_ = bf16[3072,256]{1,0:T(8,128)(2,1)} collective-permute-done((bf16[3072,256]{1,0:T(8,128)(2,1)}, bf16[3072,256]{1,0:T(8,128)(2,1)}, u32[]{:S(2)}, u32[]{:S(2)}) %collective-permute-start.4) | collective-permute-done | bytes 1572896 | tf_op jit(solution)/shard_map/ppermute | solution.py:382
  111.8 4.5 %collective-permute-start.7 = (bf16[3072,256]{1,0:T(8,128)(2,1)}, bf16[3072,256]{1,0:T(8,128)(2,1)}, u32[]{:S(2)}, u32[]{:S(2)}) collective-permute-start(bf16[3072,256]{1,0:T(8,128)(2,1)} %get-tuple-element.48.refs_0_), channel_id=1, source_target_pairs={{0,8},{8,0},{16,24},{24,16},{32,40},{40,32},{48,56},{56,48},{1,9},... | collective-permute-start | bytes 4718600 | tf_op jit(solution)/shard_map/ppermute | solution.py:388
  116.8 1.4 copy-done.4
  118.2 1.6 copy-done.8
  119.8 5.6 %feed_forward_first.1 = (bf16[512,2048]{1,0:T(8,128)(2,1)S(1)}, bf16[512,512]{1,0:T(8,128)(2,1)S(1)}) custom-call(bf16[8,8,64,256]{3,2,1,0:T(8,128)(2,1)S(1)} %bitcast.87, bf16[3072,256]{1,0:T(8,128)(2,1)S(1)} %copy-done.4, bf16[3072,256]{1,0:T(8,128)(2,1)} %get-tuple-element.49.refs_1_, bf16[3072,256]{1,0:T(8,128)(2,1)} %get-tuple-element.52.refs_2_, ...), custom_call_target="tpu_custom_call" | custom-call | flops 3000000000 | bytes 8000000 | tf_op jit(solution)/shard_map/feed_forward_first/pallas_call | solution.py:286
  125.4 5.6 %feed_forward_middle.1.so_far = f32[512,2048]{1,0:T(8,128)S(1)} custom-call(bf16[512,2048]{1,0:T(8,128)(2,1)S(1)} %get-tuple-element.54.normed, bf16[512,512]{1,0:T(8,128)(2,1)S(1)} %get-tuple-element.55.hidden_in, bf16[3072,256]{1,0:T(8,128)(2,1)S(1)} %copy-done.5, bf16[3072,256]{1,0:T(8,128)(2,1)} %get-tuple-element.49.refs_1_, ...), custom_call_target="tpu_custom_call" | custom-call | flops 3000000000 | bytes 8000000 | tf_op jit(solution)/shard_map/feed_forward_middle/pallas_call | solution.py:299
  131.1 2.7 %feed_forward_far.1 = (bf16[64,1024]{1,0:T(8,128)(2,1)S(1)}, bf16[64,1024]{1,0:T(8,128)(2,1)S(1)}) custom-call(bf16[512,2048]{1,0:T(8,128)(2,1)S(1)} %get-tuple-element.54.normed, f32[512,2048]{1,0:T(8,128)S(1)} %feed_forward_middle.1.so_far, bf16[3072,256]{1,0:T(8,128)(2,1)S(1)} %collective-permute-done.9.refs_0_, ...), custom_call_target="tpu_custom_call" | custom-call | flops 3000000000 | bytes 8000000 | tf_op jit(solution)/shard_map/feed_forward_far/pallas_call | solution.py:318
  133.8 5.6 %collective-permute-start.12 = (bf16[64,1024]{1,0:T(8,128)(2,1)S(1)}, bf16[64,1024]{1,0:T(8,128)(2,1)S(1)}, u32[]{:S(2)}, u32[]{:S(2)}) collective-permute-start(bf16[64,1024]{1,0:T(8,128)(2,1)S(1)} %get-tuple-element.57), channel_id=1, source_target_pairs={{0,7},{1,0},{2,1},{3,2},{4,3},{5,4},{6,5},{7,6},{8,15},{9,8},{10,9... | collective-permute-start | bytes 393224 | tf_op jit(solution)/shard_map/ppermute | solution.py:403
  139.5 1.4 copy-done.2
  140.9 3.3 %feed_forward_near.1 = bf16[8,64,2048]{2,1,0:T(8,128)(2,1)S(1)} custom-call(bf16[512,2048]{1,0:T(8,128)(2,1)S(1)} %get-tuple-element.54.normed, f32[512,2048]{1,0:T(8,128)S(1)} %feed_forward_middle.1.so_far, bf16[3072,256]{1,0:T(8,128)(2,1)S(1)} %copy-done.2, bf16[3072,256]{1,0:T(8,128)(2,1)} %collective-permute-done.10.refs_1_), custom_call_target="tpu_custom_call" | custom-call | flops 3000000000 | bytes 8000000 | tf_op jit(solution)/shard_map/feed_forward_near/pallas_call | solution.py:318
  144.2 0.8 collective-permute-done.11
  145.0 2.0 collective-permute-start.14
  147.0 4.5 %collective-permute-done.14 = bf16[64,2048]{1,0:T(8,128)(2,1)S(1)} collective-permute-done((bf16[64,2048]{1,0:T(8,128)(2,1)S(1)}, bf16[64,2048]{1,0:T(8,128)(2,1)S(1)}, u32[]{:S(2)}, u32[]{:S(2)}) %collective-permute-start.14) | collective-permute-done | bytes 262176 | tf_op jit(solution)/shard_map/ppermute | solution.py:407
  151.5 3.1 %collective-permute-done.13 = bf16[64,2048]{1,0:T(8,128)(2,1)S(1)} collective-permute-done((bf16[64,2048]{1,0:T(8,128)(2,1)S(1)}, bf16[64,2048]{1,0:T(8,128)(2,1)S(1)}, u32[]{:S(2)}, u32[]{:S(2)}) %collective-permute-start.13) | collective-permute-done | bytes 262176 | tf_op jit(solution)/shard_map/ppermute | solution.py:407
  154.7 0.8 fusion.6
  155.8 1.2 collective-permute-start.15
  157.0 4.4 %collective-permute-done.16 = bf16[64,2048]{1,0:T(8,128)(2,1)} collective-permute-done((bf16[64,2048]{1,0:T(8,128)(2,1)}, bf16[64,2048]{1,0:T(8,128)(2,1)}, u32[]{:S(2)}, u32[]{:S(2)}) %collective-permute-start.16) | collective-permute-done | bytes 262176 | tf_op jit(solution)/shard_map/ppermute | solution.py:407
  161.3 1.3 collective-permute-done.15
  162.6 1.2 fusion.5
  164.3 1.0 collective-permute-start.17
  165.3 1.0 constant_dynamic-slice_fusion
  166.6 2.5 %collective-permute-done.18 = bf16[64,2048]{1,0:T(8,128)(2,1)S(1)} collective-permute-done((bf16[64,2048]{1,0:T(8,128)(2,1)S(1)}, bf16[64,2048]{1,0:T(8,128)(2,1)S(1)}, u32[]{:S(2)}, u32[]{:S(2)}) %collective-permute-start.18) | collective-permute-done | bytes 262176 | tf_op jit(solution)/shard_map/ppermute | solution.py:407
  169.1 1.7 collective-permute-done.17
  170.9 1.9 collective-permute-start.22
  172.9 3.6 %collective-permute-start.21 = (bf16[16,2048]{1,0:T(8,128)(2,1)S(1)}, bf16[16,2048]{1,0:T(8,128)(2,1)S(1)}, u32[]{:S(2)}, u32[]{:S(2)}) collective-permute-start(bf16[16,2048]{1,0:T(8,128)(2,1)S(1)} %get-tuple-element.80), channel_id=1, source_target_pairs={{64,0},{192,8},{80,16},{208,24},{96,32},{224,40},{112,48},{240,56}... | collective-permute-start | bytes 196616 | tf_op jit(solution)/shard_map/ppermute | solution.py:418
  176.4 0.9 collective-permute-start.20
  177.4 3.4 %collective-permute-start.19 = (bf16[16,2048]{1,0:T(8,128)(2,1)S(1)}, bf16[16,2048]{1,0:T(8,128)(2,1)S(1)}, u32[]{:S(2)}, u32[]{:S(2)}) collective-permute-start(bf16[16,2048]{1,0:T(8,128)(2,1)S(1)} %get-tuple-element.78), channel_id=1, source_target_pairs={{0,0},{128,8},{16,16},{144,24},{32,32},{160,40},{48,48},{176,56},{... | collective-permute-start | bytes 196616 | tf_op jit(solution)/shard_map/ppermute | solution.py:418
  181.1 3.6 %collective-permute-done.19 = bf16[16,2048]{1,0:T(8,128)(2,1)S(1)} collective-permute-done((bf16[16,2048]{1,0:T(8,128)(2,1)S(1)}, bf16[16,2048]{1,0:T(8,128)(2,1)S(1)}, u32[]{:S(2)}, u32[]{:S(2)}) %collective-permute-start.19) | collective-permute-done | bytes 65568 | tf_op jit(solution)/shard_map/ppermute | solution.py:418
  184.7 1.5 fusion.1
  186.7 1.2 collective-permute-done.23
  187.9 2.6 %collective-permute-start.26 = (f32[32,256]{1,0:T(8,128)S(1)}, f32[32,256]{1,0:T(8,128)S(1)}, u32[]{:S(2)}, u32[]{:S(2)}) collective-permute-start(f32[32,256]{1,0:T(8,128)S(1)} %add.127), channel_id=1, source_target_pairs={{0,48},{8,56},{16,32},{24,40},{32,16},{40,24},{48,0},{56,8},{1,49}... | collective-permute-start | bytes 98312 | tf_op jit(solution)/shard_map/ppermute | solution.py:428
  191.2 1.0 copy.29
  192.1 2.6 %collective-permute-done.25 = f32[32,256]{1,0:T(8,128)S(1)} collective-permute-done((f32[32,256]{1,0:T(8,128)S(1)}, f32[32,256]{1,0:T(8,128)S(1)}, u32[]{:S(2)}, u32[]{:S(2)}) %collective-permute-start.25) | collective-permute-done | bytes 32800 | tf_op jit(solution)/shard_map/ppermute | solution.py:428
  (66 shorter events, 5.6 us)
Async XLA Ops:
  7.2 1.2 copy-start
  11.0 26.8 %copy-start.9 = (bf16[128,2,2048]{2,1,0:T(2,128)(2,1)S(1)}, bf16[128,2,2048]{2,1,0:T(2,128)(2,1)}, u32[]{:S(2)}) copy-start(bf16[128,2,2048]{2,1,0:T(2,128)(2,1)} %param.16) | copy-start | bytes 3145732
  21.6 16.6 %copy-start.6 = (bf16[2,128,2048]{2,1,0:T(8,128)(2,1)S(1)}, bf16[2,128,2048]{2,1,0:T(8,128)(2,1)}, u32[]{:S(2)}) copy-start(bf16[2,128,2048]{2,1,0:T(8,128)(2,1)} %ow_ref.1) | copy-start | bytes 3145732
  21.6 16.6 %copy-start.7 = (bf16[288,128]{1,0:T(8,128)(2,1)S(1)}, bf16[288,128]{1,0:T(8,128)(2,1)}, u32[]{:S(2)}) copy-start(bf16[288,128]{1,0:T(8,128)(2,1)} %get-tuple-element.38.p0) | copy-start | bytes 221188
  21.6 5.9 %collective-permute-start = (bf16[288,128]{1,0:T(8,128)(2,1)}, bf16[288,128]{1,0:T(8,128)(2,1)S(1)}, u32[]{:S(2)}, u32[]{:S(2)}) collective-permute-start(bf16[288,128]{1,0:T(8,128)(2,1)} %get-tuple-element.38.p0), channel_id=1, source_target_pairs={{0,64},{64,128},{128,192},{192,0},{1,65},{65,129},{129,193},{193,1... | collective-permute-start | bytes 221192 | tf_op jit(solution)/shard_map/ppermute | solution.py:380
  23.8 5.8 %collective-permute-start.1 = (bf16[288,128]{1,0:T(8,128)(2,1)}, bf16[288,128]{1,0:T(8,128)(2,1)S(1)}, u32[]{:S(2)}, u32[]{:S(2)}) collective-permute-start(bf16[288,128]{1,0:T(8,128)(2,1)} %get-tuple-element.38.p0), channel_id=1, source_target_pairs={{0,128},{64,192},{128,0},{192,64},{1,129},{65,193},{129,1},{193,65... | collective-permute-start | bytes 221192 | tf_op jit(solution)/shard_map/ppermute | solution.py:380
  26.5 3.7 %collective-permute-start.2 = (bf16[288,128]{1,0:T(8,128)(2,1)}, bf16[288,128]{1,0:T(8,128)(2,1)S(1)}, u32[]{:S(2)}, u32[]{:S(2)}) collective-permute-start(bf16[288,128]{1,0:T(8,128)(2,1)} %get-tuple-element.38.p0), channel_id=1, source_target_pairs={{0,192},{64,0},{128,64},{192,128},{1,193},{65,1},{129,65},{193,129... | collective-permute-start | bytes 221192 | tf_op jit(solution)/shard_map/ppermute | solution.py:380
  30.2 32.2 %collective-permute-start.5 = (bf16[3072,256]{1,0:T(8,128)(2,1)}, bf16[3072,256]{1,0:T(8,128)(2,1)S(1)}, u32[]{:S(2)}, u32[]{:S(2)}) collective-permute-start(bf16[3072,256]{1,0:T(8,128)(2,1)} %get-tuple-element.44), channel_id=1, source_target_pairs={{0,0},{8,128},{16,16},{24,144},{32,32},{40,160},{48,48},{56,176},{... | collective-permute-start | bytes 4718600 | tf_op jit(solution)/shard_map/ppermute | solution.py:382
  35.5 59.7 %collective-permute-start.6 = (bf16[3072,256]{1,0:T(8,128)(2,1)}, bf16[3072,256]{1,0:T(8,128)(2,1)}, u32[]{:S(2)}, u32[]{:S(2)}) collective-permute-start(bf16[3072,256]{1,0:T(8,128)(2,1)} %get-tuple-element.45), channel_id=1, source_target_pairs={{0,8},{8,136},{16,24},{24,152},{32,40},{40,168},{48,56},{56,184},{... | collective-permute-start | bytes 4718600 | tf_op jit(solution)/shard_map/ppermute | solution.py:382
  39.5 11.1 %all-to-all-start = ((bf16[8,64,256]{2,1,0:T(8,128)(2,1)}), bf16[8,64,256]{2,1,0:T(8,128)(2,1)S(1)}, u32[]{:S(2)}, u32[]{:S(2)}) async-start(bf16[8,64,256]{2,1,0:T(8,128)(2,1)} %merge.1), calls=%async_computation | async-start | bytes 524288 | tf_op jit(solution)/shard_map/all_to_all | solution.py:385
  43.7 73.1 %all-gather.3.cloned.1.call-start = ((), (), s32[]{:S(2)}) async-start(), calls=%async_computation.1 | async-start | bytes 2359296 | tf_op jit(solution)/shard_map/all_gather | solution.py:386
  43.7 51.6 %collective-permute-start.3 = (bf16[3072,256]{1,0:T(8,128)(2,1)}, bf16[3072,256]{1,0:T(8,128)(2,1)}, u32[]{:S(2)}, u32[]{:S(2)}) collective-permute-start(bf16[3072,256]{1,0:T(8,128)(2,1)} %get-tuple-element.42), channel_id=1, source_target_pairs={{0,64},{8,192},{16,80},{24,208},{32,96},{40,224},{48,112},{56,240}... | collective-permute-start | bytes 4718600 | tf_op jit(solution)/shard_map/ppermute | solution.py:382
  43.7 68.1 %collective-permute-start.4 = (bf16[3072,256]{1,0:T(8,128)(2,1)}, bf16[3072,256]{1,0:T(8,128)(2,1)}, u32[]{:S(2)}, u32[]{:S(2)}) collective-permute-start(bf16[3072,256]{1,0:T(8,128)(2,1)} %get-tuple-element.43), channel_id=1, source_target_pairs={{0,72},{8,200},{16,88},{24,216},{32,104},{40,232},{48,120},{56,248... | collective-permute-start | bytes 4718600 | tf_op jit(solution)/shard_map/ppermute | solution.py:382
  50.6 0.7 copy-start.10
  62.4 32.9 %copy-start.3 = (bf16[3072,256]{1,0:T(8,128)(2,1)}, bf16[3072,256]{1,0:T(8,128)(2,1)S(1)}, u32[]{:S(2)}) copy-start(bf16[3072,256]{1,0:T(8,128)(2,1)S(1)} %collective-permute-done.5.refs_0_) | copy-start | bytes 4718596
  111.8 13.6 %collective-permute-start.7 = (bf16[3072,256]{1,0:T(8,128)(2,1)}, bf16[3072,256]{1,0:T(8,128)(2,1)}, u32[]{:S(2)}, u32[]{:S(2)}) collective-permute-start(bf16[3072,256]{1,0:T(8,128)(2,1)} %get-tuple-element.48.refs_0_), channel_id=1, source_target_pairs={{0,8},{8,0},{16,24},{24,16},{32,40},{40,32},{48,56},{56,48},{1,9},... | collective-permute-start | bytes 4718600 | tf_op jit(solution)/shard_map/ppermute | solution.py:388
  116.3 9.1 %collective-permute-start.8 = (bf16[3072,256]{1,0:T(8,128)(2,1)}, bf16[3072,256]{1,0:T(8,128)(2,1)}, u32[]{:S(2)}, u32[]{:S(2)}) collective-permute-start(bf16[3072,256]{1,0:T(8,128)(2,1)} %get-tuple-element.49.refs_1_), channel_id=1, source_target_pairs={{0,8},{8,0},{16,24},{24,16},{32,40},{40,32},{48,56},{56,48},{1,9},... | collective-permute-start | bytes 4718600 | tf_op jit(solution)/shard_map/ppermute | solution.py:388
  116.3 14.8 %collective-permute-start.9 = (bf16[3072,256]{1,0:T(8,128)(2,1)}, bf16[3072,256]{1,0:T(8,128)(2,1)S(1)}, u32[]{:S(2)}, u32[]{:S(2)}) collective-permute-start(bf16[3072,256]{1,0:T(8,128)(2,1)} %get-tuple-element.52.refs_2_), channel_id=1, source_target_pairs={{0,8},{8,0},{16,24},{24,16},{32,40},{40,32},{48,56},{56,48},{1,9},... | collective-permute-start | bytes 4718600 | tf_op jit(solution)/shard_map/ppermute | solution.py:388
  116.8 14.3 %collective-permute-start.10 = (bf16[3072,256]{1,0:T(8,128)(2,1)}, bf16[3072,256]{1,0:T(8,128)(2,1)}, u32[]{:S(2)}, u32[]{:S(2)}) collective-permute-start(bf16[3072,256]{1,0:T(8,128)(2,1)} %get-tuple-element.53.refs_3_), channel_id=1, source_target_pairs={{0,8},{8,0},{16,24},{24,16},{32,40},{40,32},{48,56},{56,48},{1,9},... | collective-permute-start | bytes 4718600 | tf_op jit(solution)/shard_map/ppermute | solution.py:388
  116.8 1.4 copy-start.4
  118.2 1.6 copy-start.8
  119.8 5.6 %copy-start.5 = (bf16[3072,256]{1,0:T(8,128)(2,1)S(1)}, bf16[3072,256]{1,0:T(8,128)(2,1)}, u32[]{:S(2)}) copy-start(bf16[3072,256]{1,0:T(8,128)(2,1)} %get-tuple-element.48.refs_0_) | copy-start | bytes 4718596
  131.1 2.8 %copy-start.1 = (bf16[3072,256]{1,0:T(8,128)(2,1)}, bf16[3072,256]{1,0:T(8,128)(2,1)S(1)}, u32[]{:S(2)}) copy-start(bf16[3072,256]{1,0:T(8,128)(2,1)S(1)} %collective-permute-done.9.refs_0_) | copy-start | bytes 4718596
  133.8 10.3 %collective-permute-start.12 = (bf16[64,1024]{1,0:T(8,128)(2,1)S(1)}, bf16[64,1024]{1,0:T(8,128)(2,1)S(1)}, u32[]{:S(2)}, u32[]{:S(2)}) collective-permute-start(bf16[64,1024]{1,0:T(8,128)(2,1)S(1)} %get-tuple-element.57), channel_id=1, source_target_pairs={{0,7},{1,0},{2,1},{3,2},{4,3},{5,4},{6,5},{7,6},{8,15},{9,8},{10,9... | collective-permute-start | bytes 393224 | tf_op jit(solution)/shard_map/ppermute | solution.py:403
  139.5 5.4 %collective-permute-start.11 = (bf16[64,1024]{1,0:T(8,128)(2,1)S(1)}, bf16[64,1024]{1,0:T(8,128)(2,1)S(1)}, u32[]{:S(2)}, u32[]{:S(2)}) collective-permute-start(bf16[64,1024]{1,0:T(8,128)(2,1)S(1)} %get-tuple-element.56), channel_id=1, source_target_pairs={{0,1},{1,2},{2,3},{3,4},{4,5},{5,6},{6,7},{7,0},{8,9},{9,10},{10,1... | collective-permute-start | bytes 393224 | tf_op jit(solution)/shard_map/ppermute | solution.py:403
  139.5 1.4 copy-start.2
  145.0 6.5 %collective-permute-start.14 = (bf16[64,2048]{1,0:T(8,128)(2,1)S(1)}, bf16[64,2048]{1,0:T(8,128)(2,1)S(1)}, u32[]{:S(2)}, u32[]{:S(2)}) collective-permute-start(bf16[64,2048]{1,0:T(8,128)(2,1)S(1)} %get-tuple-element.59), channel_id=1, source_target_pairs={{0,7},{1,0},{2,1},{3,2},{4,3},{5,4},{6,5},{7,6},{8,15},{9,8},{10,9... | collective-permute-start | bytes 786440 | tf_op jit(solution)/shard_map/ppermute | solution.py:407
  147.0 7.7 %collective-permute-start.13 = (bf16[64,2048]{1,0:T(8,128)(2,1)S(1)}, bf16[64,2048]{1,0:T(8,128)(2,1)S(1)}, u32[]{:S(2)}, u32[]{:S(2)}) collective-permute-start(bf16[64,2048]{1,0:T(8,128)(2,1)S(1)} %get-tuple-element.58), channel_id=1, source_target_pairs={{0,1},{1,2},{2,3},{3,4},{4,5},{5,6},{6,7},{7,0},{8,9},{9,10},{10,1... | collective-permute-start | bytes 786440 | tf_op jit(solution)/shard_map/ppermute | solution.py:407
  155.5 5.8 %collective-permute-start.16 = (bf16[64,2048]{1,0:T(8,128)(2,1)}, bf16[64,2048]{1,0:T(8,128)(2,1)}, u32[]{:S(2)}, u32[]{:S(2)}) collective-permute-start(bf16[64,2048]{1,0:T(8,128)(2,1)} %get-tuple-element.61), channel_id=1, source_target_pairs={{0,7},{1,0},{2,1},{3,2},{4,3},{5,4},{6,5},{7,6},{8,15},{9,8},{10,9... | collective-permute-start | bytes 786440 | tf_op jit(solution)/shard_map/ppermute | solution.py:407
  155.8 6.8 %collective-permute-start.15 = (bf16[64,2048]{1,0:T(8,128)(2,1)S(1)}, bf16[64,2048]{1,0:T(8,128)(2,1)}, u32[]{:S(2)}, u32[]{:S(2)}) collective-permute-start(bf16[64,2048]{1,0:T(8,128)(2,1)S(1)} %get-tuple-element.60), channel_id=1, source_target_pairs={{0,1},{1,2},{2,3},{3,4},{4,5},{5,6},{6,7},{7,0},{8,9},{9,10},{10,1... | collective-permute-start | bytes 786440 | tf_op jit(solution)/shard_map/ppermute | solution.py:407
  163.8 5.3 %collective-permute-start.18 = (bf16[64,2048]{1,0:T(8,128)(2,1)S(1)}, bf16[64,2048]{1,0:T(8,128)(2,1)S(1)}, u32[]{:S(2)}, u32[]{:S(2)}) collective-permute-start(bf16[64,2048]{1,0:T(8,128)(2,1)S(1)} %get-tuple-element.63), channel_id=1, source_target_pairs={{0,7},{1,0},{2,1},{3,2},{4,3},{5,4},{6,5},{7,6},{8,15},{9,8},{10,9... | collective-permute-start | bytes 786440 | tf_op jit(solution)/shard_map/ppermute | solution.py:407
  164.3 6.4 %collective-permute-start.17 = (bf16[64,2048]{1,0:T(8,128)(2,1)S(1)}, bf16[64,2048]{1,0:T(8,128)(2,1)S(1)}, u32[]{:S(2)}, u32[]{:S(2)}) collective-permute-start(bf16[64,2048]{1,0:T(8,128)(2,1)S(1)} %get-tuple-element.62), channel_id=1, source_target_pairs={{0,1},{1,2},{2,3},{3,4},{4,5},{5,6},{6,7},{7,0},{8,9},{9,10},{10,1... | collective-permute-start | bytes 786440 | tf_op jit(solution)/shard_map/ppermute | solution.py:407
  170.9 9.9 %collective-permute-start.22 = (bf16[16,2048]{1,0:T(8,128)(2,1)S(1)}, bf16[16,2048]{1,0:T(8,128)(2,1)S(1)}, u32[]{:S(2)}, u32[]{:S(2)}) collective-permute-start(bf16[16,2048]{1,0:T(8,128)(2,1)S(1)} %get-tuple-element.79), channel_id=1, source_target_pairs={{72,0},{200,8},{88,16},{216,24},{104,32},{232,40},{120,48},{248,56... | collective-permute-start | bytes 196616 | tf_op jit(solution)/shard_map/ppermute | solution.py:418
  172.9 8.0 %collective-permute-start.21 = (bf16[16,2048]{1,0:T(8,128)(2,1)S(1)}, bf16[16,2048]{1,0:T(8,128)(2,1)S(1)}, u32[]{:S(2)}, u32[]{:S(2)}) collective-permute-start(bf16[16,2048]{1,0:T(8,128)(2,1)S(1)} %get-tuple-element.80), channel_id=1, source_target_pairs={{64,0},{192,8},{80,16},{208,24},{96,32},{224,40},{112,48},{240,56}... | collective-permute-start | bytes 196616 | tf_op jit(solution)/shard_map/ppermute | solution.py:418
  176.4 4.6 %collective-permute-start.20 = (bf16[16,2048]{1,0:T(8,128)(2,1)S(1)}, bf16[16,2048]{1,0:T(8,128)(2,1)S(1)}, u32[]{:S(2)}, u32[]{:S(2)}) collective-permute-start(bf16[16,2048]{1,0:T(8,128)(2,1)S(1)} %get-tuple-element.81), channel_id=1, source_target_pairs={{8,0},{136,8},{24,16},{152,24},{40,32},{168,40},{56,48},{184,56},{... | collective-permute-start | bytes 196616 | tf_op jit(solution)/shard_map/ppermute | solution.py:418
  177.4 7.2 %collective-permute-start.19 = (bf16[16,2048]{1,0:T(8,128)(2,1)S(1)}, bf16[16,2048]{1,0:T(8,128)(2,1)S(1)}, u32[]{:S(2)}, u32[]{:S(2)}) collective-permute-start(bf16[16,2048]{1,0:T(8,128)(2,1)S(1)} %get-tuple-element.78), channel_id=1, source_target_pairs={{0,0},{128,8},{16,16},{144,24},{32,32},{160,40},{48,48},{176,56},{... | collective-permute-start | bytes 196616 | tf_op jit(solution)/shard_map/ppermute | solution.py:418
  180.9 5.4 %copy-start.11 = (bf16[2,2048,256]{2,1,0:T(8,128)(2,1)S(1)}, bf16[2,2048,256]{2,1,0:T(8,128)(2,1)}, u32[]{:S(2)}) copy-start(bf16[2,2048,256]{2,1,0:T(8,128)(2,1)} %param.29) | copy-start | bytes 6291460
  184.7 10.0 %copy-start.12 = (bf16[256,4]{0,1:T(4,128)(2,1)S(1)}, bf16[256,4]{0,1:T(4,128)(2,1)}, u32[]{:S(2)}) copy-start(bf16[256,4]{0,1:T(4,128)(2,1)} %param.31) | copy-start | bytes 6148
  184.7 10.0 %copy-start.13 = (f32[256]{0:T(256)S(1)}, f32[256]{0:T(256)}, u32[]{:S(2)}) copy-start(f32[256]{0:T(256)} %param.30) | copy-start | bytes 3076
  186.6 1.3 collective-permute-start.23
  187.9 4.3 %collective-permute-start.26 = (f32[32,256]{1,0:T(8,128)S(1)}, f32[32,256]{1,0:T(8,128)S(1)}, u32[]{:S(2)}, u32[]{:S(2)}) collective-permute-start(f32[32,256]{1,0:T(8,128)S(1)} %add.127), channel_id=1, source_target_pairs={{0,48},{8,56},{16,32},{24,40},{32,16},{40,24},{48,0},{56,8},{1,49}... | collective-permute-start | bytes 98312 | tf_op jit(solution)/shard_map/ppermute | solution.py:428
  190.5 4.3 %collective-permute-start.25 = (f32[32,256]{1,0:T(8,128)S(1)}, f32[32,256]{1,0:T(8,128)S(1)}, u32[]{:S(2)}, u32[]{:S(2)}) collective-permute-start(f32[32,256]{1,0:T(8,128)S(1)} %add.127), channel_id=1, source_target_pairs={{0,32},{8,40},{16,48},{24,56},{32,0},{40,8},{48,16},{56,24},{1,33}... | collective-permute-start | bytes 98312 | tf_op jit(solution)/shard_map/ppermute | solution.py:428
  191.0 3.7 %collective-permute-start.24 = (f32[32,256]{1,0:T(8,128)S(1)}, f32[32,256]{1,0:T(8,128)S(1)}, u32[]{:S(2)}, u32[]{:S(2)}) collective-permute-start(f32[32,256]{1,0:T(8,128)S(1)} %add.127), channel_id=1, source_target_pairs={{0,16},{8,24},{16,0},{24,8},{32,48},{40,56},{48,32},{56,40},{1,17}... | collective-permute-start | bytes 98312 | tf_op jit(solution)/shard_map/ppermute | solution.py:428
Sparse Core Ops, SparseCore 0:
  51.4 43.9 all-gather.2

commit v3 on v2

--- a/solution.py
+++ b/solution.py
@@ -74,7 +74,7 @@
         kinds = lax.broadcasted_iota(jnp.int32, (ACTIONS, CHUNK), 0)
         onehot = jnp.where(kinds == act_ref[u : u + 1, :], 1.0, 0.0).astype(BF16)
         keys = dot(kwt_ref[...], h, ((1,), (1,))) + dot(tabt_ref[...], onehot)
-        s = dot(q, keys.astype(BF16)) * SCALE
+        s = dot(q, keys.astype(BF16))
         scores.append(jnp.where(where < length_ref[u], s, -1e30))
         wide = h.astype(F32)
         normed = wide * lax.rsqrt(jnp.mean(wide * wide, axis=1, keepdims=True) + EPS)
@@ -82,8 +82,8 @@
     s = jnp.where(first, scores[0], scores[1])
     m_old = m_ref[...]
     m_new = jnp.maximum(m_old, jnp.max(s, axis=1, keepdims=True))
-    p = jnp.exp2(s - m_new)
-    fade = jnp.exp2(m_old - m_new)
+    p = jnp.exp2((s - m_new) * SCALE)
+    fade = jnp.exp2((m_old - m_new) * SCALE)
     m_ref[...] = m_new
     l_ref[...] = l_ref[...] * fade + jnp.sum(p, axis=1, keepdims=True)
     acc_ref[...] = acc_ref[...] * fade + dot(p.astype(BF16), jnp.concatenate(values, axis=1))
@@ -158,7 +158,7 @@
     top = jnp.maximum(jnp.maximum(maxima[0], maxima[1]), jnp.maximum(maxima[2], maxima[3]))
     total, weighted = 0.0, 0.0
     for ref, m in zip(parts, maxima):
-        share = column(ref, 272) * jnp.exp2(m - top)
+        share = column(ref, 272) * jnp.exp2((m - top) * SCALE)
         total += share
         weighted += ref[0:256, :].astype(F32) * share
     attended = (weighted / total).astype(BF16)
@@ -191,9 +191,13 @@
     hidden[:, p * 128 : (p + 1) * 128] = (gate / (1.0 + jnp.exp(-gate)) * up).astype(BF16)
 
 
+def down_weights(refs, g):
+    return jnp.concatenate([ref[g * 128 : (g + 1) * 128, :] for ref in refs], axis=0)
+
+
 def first_kernel(x_ref, *refs):
-    packs, (normed, hidden, gu, sem) = refs[:4], refs[4:]
-    copies = [pltpu.make_async_copy(packs[p].at[pl.ds(0, 2048)], gu.at[p], sem.at[p]) for p in range(4)]
+    packs, (normed, so_far, hidden, held, sem) = refs[:4], refs[4:]
+    copies = [pltpu.make_async_copy(packs[p], held.at[p], sem.at[p]) for p in range(4)]
     for copy in copies:
         copy.start()
     z = lax.axis_index("cand")
@@ -206,56 +210,58 @@
             normed[pl.ds(to, 16), :] = rows[m * 16 : (m + 1) * 16]
     for p in range(4):
         copies[p].wait()
+        hidden_part(normed, held[p, 0:2048, :], hidden, p)
+    downs = [held.at[p, pl.ds(2048, 1024)] for p in range(4)]
+    for g in range(8):
+        so_far[:, g * 256 : (g + 1) * 256] = dot(hidden[...], down_weights(downs, g))
+
+
+def middle_kernel(normed, *refs):
+    late, (hidden, gu, gu_sem) = refs[:2], refs[2:]
+    copies = [pltpu.make_async_copy(late[p].at[pl.ds(0, 2048)], gu.at[p], gu_sem.at[p]) for p in range(2)]
+    for copy in copies:
+        copy.start()
+    for p in range(2):
+        copies[p].wait()
         hidden_part(normed, gu[p], hidden, p)
 
 
-def middle_kernel(normed, hidden_in, *refs):
-    early, late, (so_far,), (hidden, gu, dn, gu_sem, dn_sem) = refs[:4], refs[4:6], refs[6:7], refs[7:]
-    gu_copies = [pltpu.make_async_copy(late[p].at[pl.ds(0, 2048)], gu.at[p], gu_sem.at[p]) for p in range(2)]
-    dn_copies = [
-        pltpu.make_async_copy(pack.at[pl.ds(2048, 1024)], dn.at[p], dn_sem.at[p])
-        for p, pack in enumerate(early + late)
-    ]
-    for copy in gu_copies + dn_copies:
+def far_kernel(normed_all, so_far_all, hidden_all, *refs):
+    late, swapped, (far_a, far_b, hidden, normed, so_far, downs, sem) = refs[:2], refs[2:4], refs[4:]
+    copies = [
+        pltpu.make_async_copy(normed_all.at[pl.ds(256, 64)], normed, sem.at[0]),
+        pltpu.make_async_copy(so_far_all.at[pl.ds(256, 64)], so_far, sem.at[1]),
+    ] + [pltpu.make_async_copy(late[p].at[pl.ds(2048, 1024)], downs.at[p], sem.at[2 + p]) for p in range(2)]
+    for copy in copies:
         copy.start()
-    for p in range(4):
-        hidden[:, p * 128 : (p + 1) * 128] = hidden_in[:, p * 128 : (p + 1) * 128]
+    hidden[:, 0:256] = hidden_all[256:320, :]
+    copies[0].wait()
     for p in range(2):
-        gu_copies[p].wait()
-        hidden_part(normed, gu[p], hidden, 4 + p)
-    for copy in dn_copies:
+        hidden_part(normed, swapped[p][0:2048, :], hidden, 2 + p)
+    for copy in copies[1:]:
         copy.wait()
+    parts = [downs.at[p] for p in range(2)] + [swapped[p].at[pl.ds(2048, 1024)] for p in range(2)]
     for g in range(8):
-        weights = jnp.concatenate([dn[p, g * 128 : (g + 1) * 128, :] for p in range(6)], axis=0)
-        so_far[:, g * 256 : (g + 1) * 256] = dot(hidden[...], weights)
-
-
-FAR = slice(256, 320)
-
-
-def last_columns(normed, so_far, packs, hidden, g):
-    weights = jnp.concatenate([pack[2048 + g * 128 : 2176 + g * 128, :] for pack in packs], axis=0)
-    return (so_far[:, g * 256 : (g + 1) * 256] + dot(hidden[...], weights)).astype(BF16)
-
-
-def far_kernel(normed, so_far, *refs):
-    packs, (far_a, far_b, hidden) = refs[:2], refs[2:]
+        columns = so_far[:, g * 256 : (g + 1) * 256] + dot(hidden[...], down_weights(parts, g))
+        (far_a, far_b)[g // 4][:, (g % 4) * 256 : (g % 4 + 1) * 256] = columns.astype(BF16)
+
+
+def near_kernel(normed, so_far, hidden_in, *refs):
+    late, swapped, (near, hidden, downs, sem) = refs[:2], refs[2:4], refs[4:]
+    copies = [pltpu.make_async_copy(late[p].at[pl.ds(2048, 1024)], downs.at[p], sem.at[p]) for p in range(2)]
+    for copy in copies:
+        copy.start()
+    hidden[:, 0:256] = hidden_in[...]
     for p in range(2):
-        hidden_part(normed.at[FAR], packs[p][0:2048, :], hidden, p)
+        hidden_part(normed, swapped[p][0:2048, :], hidden, 2 + p)
+    for copy in copies:
+        copy.wait()
+    parts = [downs.at[p] for p in range(2)] + [swapped[p].at[pl.ds(2048, 1024)] for p in range(2)]
     for g in range(8):
-        (far_a, far_b)[g // 4][:, (g % 4) * 256 : (g % 4 + 1) * 256] = last_columns(
-            normed, so_far.at[FAR], packs, hidden, g
-        )
-
-
-def near_kernel(normed, so_far, *refs):
-    packs, (near, hidden) = refs[:2], refs[2:]
-    for p in range(2):
-        hidden_part(normed, packs[p][0:2048, :], hidden, p)
-    for g in range(8):
-        columns = last_columns(normed, so_far, packs, hidden, g)
+        span = slice(g * 256, (g + 1) * 256)
+        columns = (so_far[:, span] + dot(hidden[...], down_weights(parts, g))).astype(BF16)
         for away in range(8):
-            near[away, :, g * 256 : (g + 1) * 256] = columns[away * 64 : (away + 1) * 64]
+            near[away, :, span] = columns[away * 64 : (away + 1) * 64]
 
 
 def gate_kernel(*refs):
@@ -278,53 +284,74 @@
 
 VMEM_SPEC = pl.BlockSpec(memory_space=pltpu.VMEM)
 ANY_SPEC = pl.BlockSpec(memory_space=pl.ANY)
-FFN_PARAMS = pltpu.CompilerParams(vmem_limit_bytes=28 << 20)
+FFN_PARAMS = pltpu.CompilerParams(vmem_limit_bytes=54 << 20)
 FFN_COST = pl.CostEstimate(flops=3_000_000_000, bytes_accessed=8_000_000, transcendentals=300_000)
 
 
 def feed_forward_first(x, packs):
     return pl.pallas_call(
         first_kernel,
-        out_shape=[jax.ShapeDtypeStruct((512, 2048), BF16), jax.ShapeDtypeStruct((512, 512), BF16)],
+        out_shape=[jax.ShapeDtypeStruct((512, 2048), BF16), jax.ShapeDtypeStruct((512, 2048), F32)],
         in_specs=[VMEM_SPEC] + [ANY_SPEC] * 4,
         out_specs=[VMEM_SPEC] * 2,
-        scratch_shapes=[pltpu.VMEM((4, 2048, 256), BF16), pltpu.SemaphoreType.DMA((4,))],
+        scratch_shapes=[
+            pltpu.VMEM((512, 512), BF16),
+            pltpu.VMEM((4, 3072, 256), BF16),
+            pltpu.SemaphoreType.DMA((4,)),
+        ],
         compiler_params=FFN_PARAMS,
         cost_estimate=FFN_COST,
         name="feed_forward_first",
     )(x, *packs)
 
 
-def feed_forward_middle(normed, hidden, early, late):
+def feed_forward_middle(normed, late):
     return pl.pallas_call(
         middle_kernel,
-        out_shape=jax.ShapeDtypeStruct((512, 2048), F32),
-        in_specs=[VMEM_SPEC] * 2 + [ANY_SPEC] * 6,
+        out_shape=jax.ShapeDtypeStruct((512, 256), BF16),
+        in_specs=[VMEM_SPEC] + [ANY_SPEC] * 2,
         out_specs=VMEM_SPEC,
-        scratch_shapes=[
-            pltpu.VMEM((512, 768), BF16),
-            pltpu.VMEM((2, 2048, 256), BF16),
-            pltpu.VMEM((6, 1024, 256), BF16),
-            pltpu.SemaphoreType.DMA((2,)),
-            pltpu.SemaphoreType.DMA((6,)),
-        ],
+        scratch_shapes=[pltpu.VMEM((2, 2048, 256), BF16), pltpu.SemaphoreType.DMA((2,))],
         compiler_params=FFN_PARAMS,
         cost_estimate=FFN_COST,
         name="feed_forward_middle",
-    )(normed, hidden, *early, *late)
-
-
-def feed_forward_last(kernel, rows, outs, normed, so_far, packs, name):
-    return pl.pallas_call(
-        kernel,
-        out_shape=[jax.ShapeDtypeStruct(shape, BF16) for shape in outs],
-        in_specs=[VMEM_SPEC] * 4,
-        out_specs=[VMEM_SPEC] * len(outs),
-        scratch_shapes=[pltpu.VMEM((rows, 256), BF16)],
-        compiler_params=FFN_PARAMS,
+    )(normed, *late)
+
+
+def feed_forward_far(normed, so_far, hidden, late, swapped):
+    return pl.pallas_call(
+        far_kernel,
+        out_shape=[jax.ShapeDtypeStruct((64, 1024), BF16)] * 2,
+        in_specs=[ANY_SPEC, ANY_SPEC, VMEM_SPEC, ANY_SPEC, ANY_SPEC, VMEM_SPEC, VMEM_SPEC],
+        out_specs=[VMEM_SPEC] * 2,
+        scratch_shapes=[
+            pltpu.VMEM((64, 512), BF16),
+            pltpu.VMEM((64, 2048), BF16),
+            pltpu.VMEM((64, 2048), F32),
+            pltpu.VMEM((2, 1024, 256), BF16),
+            pltpu.SemaphoreType.DMA((4,)),
+        ],
+        compiler_params=pltpu.CompilerParams(vmem_limit_bytes=28 << 20),
         cost_estimate=FFN_COST,
-        name=name,
-    )(normed, so_far, *packs)
+        name="feed_forward_far",
+    )(normed, so_far, hidden, *late, *swapped)
+
+
+def feed_forward_near(normed, so_far, hidden, late, swapped):
+    return pl.pallas_call(
+        near_kernel,
+        out_shape=jax.ShapeDtypeStruct((8, 64, 2048), BF16),
+        in_specs=[VMEM_SPEC] * 3 + [ANY_SPEC, ANY_SPEC, VMEM_SPEC, VMEM_SPEC],
+        out_specs=VMEM_SPEC,
+        scratch_shapes=[
+            pltpu.VMEM((512, 512), BF16),
+            pltpu.VMEM((2, 1024, 256), BF16),
+            pltpu.SemaphoreType.DMA((2,)),
+        ],
+        compiler_params=pltpu.CompilerParams(vmem_limit_bytes=28 << 20),
+        cost_estimate=FFN_COST,
+        name="feed_forward_near",
+    )(normed, so_far, hidden, *late, *swapped)
 
 
 def exchange_pairs(r, reverse):
@@ -386,16 +413,15 @@
     gathered = lax.all_gather(mixed[None], "cand", axis=0, tiled=True)
 
     swap = lambda v: lax.ppermute(v, "tok", [(i, i ^ 1) for i in range(TOK)])
-    early = list(gated(packs[:2]))
-    late, early = lax.optimization_barrier((packs[2:], early))
+    early = list(gated([packs[0], packs[2]]))
+    early += [swap(v) for v in early]
+    normed, so_far = feed_forward_first(gathered, early)
+    late, normed = lax.optimization_barrier(([packs[1], packs[3]], normed))
     late = list(gated(late))
-    own, swapped = early + late, [swap(v) for v in early + late]
-    normed, hidden = feed_forward_first(gathered, own)
-    so_far = feed_forward_middle(normed, hidden, own, swapped[:2])
-    far_a, far_b = feed_forward_last(
-        far_kernel, 64, ((64, 1024), (64, 1024)), normed, so_far, swapped[2:], "feed_forward_far"
-    )
-    (near,) = feed_forward_last(near_kernel, 512, ((8, 64, 2048),), normed, so_far, swapped[2:], "feed_forward_near")
+    swapped = [swap(v) for v in late]
+    hidden = feed_forward_middle(normed, late)
+    far_a, far_b = feed_forward_far(normed, so_far, hidden, late, swapped)
+    near = feed_forward_near(normed, so_far, hidden, late, swapped)
     right = [(i, (i + 1) % CAND) for i in range(CAND)]
     left = [(i, (i - 1) % CAND) for i in range(CAND)]
     wide = lambda v: v.astype(F32)

time: 205 us -> 197 us (0.961)
  waiting for transfers between devices: 93.6 us -> 69.7 us
  blocking collectives: 0 us -> 10.9 us
  Pallas kernels: 29 us -> 38.6 us
  local copies, waits for them, and re-layouts: 8.9 us -> 4.7 us
    ppermute x4, waiting for transfers between devices: 60.5 us -> 38.6 us  [shards(): lax.ppermute(pack, both, exchange_pairs(r, False))]
    ppermute x3, waiting for transfers between devices: 11.4 us -> 0.01 us  [shards(): lax.ppermute(down, 'cand', left)]
    all_to_all x0 -> x1, blocking collectives: none -> 10.9 us  [shards(): lax.all_to_all(outgoing, 'tok', split_axis=0, concat_axis=0, tiled=True)]
    ppermute x3, waiting for transfers between devices: 6.12 us -> 13.5 us  [shards(): lax.ppermute(up, 'cand', right)]
    pallas_call x1, Pallas kernels: 5.59 us -> 11.5 us  [feed_forward_first(): pl.pallas_call(first_kernel, out_shape=[jax.ShapeDtypeStruct((512, 2048),...]
    ppermute x3, starting transfers between devices: 2.86 us -> 7.67 us  [shards(): lax.ppermute(down, 'cand', left)]
    all_to_all x1 -> x0, waiting for transfers between devices: 4.68 us -> none  [shards(): lax.all_to_all(outgoing, 'tok', split_axis=0, concat_axis=0, tiled=True)]
    all_gather x1, waiting for transfers between devices: 0.01 us -> 4.61 us  [shards(): gathered = lax.all_gather(mixed[None], 'cand', axis=0, tiled=True)]
  transfers between devices with their start and end apart: 29 -> 28, of which waited for: 17 -> 16; matrix products, arithmetic and copies ran while one was open for 1% -> 1% of each run, Pallas kernels for 8% -> 12%
where the time goes in v3:
time: 197 us; the launch traced here: 195 us
  waiting for transfers between devices  69.7 us (35%)
  starting transfers between devices  49.4 us (25%)
  Pallas kernels  38.6 us (20%)
  between operations  14.4 us (7%)
  blocking collectives  10.9 us (6%)
  matrix products  5.15 us (3%)
  local copies, waits for them, and re-layouts  4.7 us (2%)
  other arithmetic  2.35 us (1%)
    ppermute x4, waiting for transfers between devices, shards(): lax.ppermute(pack, both, exchange_pairs(r, False))  38.6 us
    ppermute x3, waiting for transfers between devices, shards(): lax.ppermute(up, 'cand', right)  13.5 us
    pallas_call x1, Pallas kernels, feed_forward_first(): pl.pallas_call(first_kernel, out_shape=[jax.ShapeDtypeStruct((512, 2048),...  11.5 us
    all_to_all x1, blocking collectives, shards(): lax.all_to_all(outgoing, 'tok', split_axis=0, concat_axis=0, tiled=True)  10.9 us
    pallas_call x1, Pallas kernels, attention(): pl.pallas_call(attention_kernel, out_shape=[jax.ShapeDtypeStruct((288, 12...  10.5 us
    ppermute x4, starting transfers between devices, shards(): arrived.append(lax.ppermute(send, both, exchange_pairs(r, True)))  9.71 us
    ppermute x4, starting transfers between devices, shards(): lax.ppermute(pack, both, exchange_pairs(r, False))  9.49 us
    ppermute x3, starting transfers between devices, shards(): lax.ppermute(down, 'cand', left)  7.67 us
  transfers between devices with their start and end apart: 28, of which 16 were waited for; matrix products, arithmetic and copies ran while one was open for 1% of the time, Pallas kernels for 12%

profile of v3, /device:TPU:1, one launch (start us, length us, event | category | flops | bytes accessed | tf_op | source)
XLA Modules:
  0.0 195.2 jit_solution(18243274047414467197)
XLA Ops:
  7.2 1.2 copy-done
  8.4 2.6 %convolution_convert_fusion = bf16[2,128,128]{2,1,0:T(8,128)(2,1)} fusion(bf16[2,2048,128]{2,1,0:T(8,128)(2,1)S(1)} %copy-done, bf16[128,2,2048]{2,1,0:T(2,128)(2,1)} %param.16), kind=kOutput, calls=%fused_computation | convolution fusion | flops 134250496 | bytes 2162688 | tf_op jit(solution)/shard_map/tbd,tdk->tbk/dot_general | solution.py:393
  11.0 10.5 %attention.1 = (bf16[288,128]{1,0:T(8,128)(2,1)}, bf16[3072,256]{1,0:T(8,128)(2,1)}, bf16[3072,256]{1,0:T(8,128)(2,1)}, bf16[3072,256]{1,0:T(8,128)(2,1)}, bf16[3072,256]{1,0:T(8,128)(2,1)}) custom-call(s32[2]{0:T(128)} %length_ref.1, bf16[256,128]{1,0:T(8,128)(2,1)} %bitcast.89, s32[1,128]{1,0:T(1,128)} %bitcast.96, bf16[2,2560,128]{2,1,0:T(8,128)(2,1)} %hist_ref.1, ...), custom_call_target="tpu_custom_call" | custom-call | flops 1000000 | bytes 100000 | tf_op jit(solution)/shard_map/attention/pallas_call | solution.py:112
  21.6 2.2 %collective-permute-start = (bf16[288,128]{1,0:T(8,128)(2,1)}, bf16[288,128]{1,0:T(8,128)(2,1)S(1)}, u32[]{:S(2)}, u32[]{:S(2)}) collective-permute-start(bf16[288,128]{1,0:T(8,128)(2,1)} %get-tuple-element.37.p0), channel_id=1, source_target_pairs={{0,64},{64,128},{128,192},{192,0},{1,65},{65,129},{129,193},{193,1... | collective-permute-start | bytes 221192 | tf_op jit(solution)/shard_map/ppermute | solution.py:407
  23.8 2.6 %collective-permute-start.1 = (bf16[288,128]{1,0:T(8,128)(2,1)}, bf16[288,128]{1,0:T(8,128)(2,1)S(1)}, u32[]{:S(2)}, u32[]{:S(2)}) collective-permute-start(bf16[288,128]{1,0:T(8,128)(2,1)} %get-tuple-element.37.p0), channel_id=1, source_target_pairs={{0,128},{64,192},{128,0},{192,64},{1,129},{65,193},{129,1},{193,65... | collective-permute-start | bytes 221192 | tf_op jit(solution)/shard_map/ppermute | solution.py:407
  26.4 1.1 collective-permute-start.2
  27.5 2.1 %collective-permute-done.1.p2 = bf16[288,128]{1,0:T(8,128)(2,1)S(1)} collective-permute-done((bf16[288,128]{1,0:T(8,128)(2,1)}, bf16[288,128]{1,0:T(8,128)(2,1)S(1)}, u32[]{:S(2)}, u32[]{:S(2)}) %collective-permute-start.1) | collective-permute-done | bytes 73760 | tf_op jit(solution)/shard_map/ppermute | solution.py:407
  30.1 5.3 %collective-permute-start.5 = (bf16[3072,256]{1,0:T(8,128)(2,1)}, bf16[3072,256]{1,0:T(8,128)(2,1)S(1)}, u32[]{:S(2)}, u32[]{:S(2)}) collective-permute-start(bf16[3072,256]{1,0:T(8,128)(2,1)} %get-tuple-element.43), channel_id=1, source_target_pairs={{0,0},{8,128},{16,16},{24,144},{32,32},{40,160},{48,48},{56,176},{... | collective-permute-start | bytes 4718600 | tf_op jit(solution)/shard_map/ppermute | solution.py:409
  35.5 1.1 collective-permute-start.6
  37.6 10.9 %all_to_all.5 = bf16[8,64,256]{2,1,0:T(8,128)(2,1)} all-to-all(bf16[8,64,256]{2,1,0:T(8,128)(2,1)S(1)} %merge.1), channel_id=1, replica_groups=mesh['hist'=4,'tok'=8,'cand'=8] {'tok'}, dimensions={0} | all-to-all | bytes 524288 | tf_op jit(solution)/shard_map/all_to_all | solution.py:412
  48.5 21.5 %collective-permute-done.5.refs_0_ = bf16[3072,256]{1,0:T(8,128)(2,1)S(1)} collective-permute-done((bf16[3072,256]{1,0:T(8,128)(2,1)}, bf16[3072,256]{1,0:T(8,128)(2,1)S(1)}, u32[]{:S(2)}, u32[]{:S(2)}) %collective-permute-start.5) | collective-permute-done | bytes 1572896 | tf_op jit(solution)/shard_map/ppermute | solution.py:409
  70.0 3.6 %collective-permute-done.6.refs_1_ = bf16[3072,256]{1,0:T(8,128)(2,1)} collective-permute-done((bf16[3072,256]{1,0:T(8,128)(2,1)}, bf16[3072,256]{1,0:T(8,128)(2,1)}, u32[]{:S(2)}, u32[]{:S(2)}) %collective-permute-start.6) | collective-permute-done | bytes 1572896 | tf_op jit(solution)/shard_map/ppermute | solution.py:409
  74.1 0.7 collective-permute-start.3
  74.8 2.3 %collective-permute-start.4 = (bf16[3072,256]{1,0:T(8,128)(2,1)}, bf16[3072,256]{1,0:T(8,128)(2,1)}, u32[]{:S(2)}, u32[]{:S(2)}) collective-permute-start(bf16[3072,256]{1,0:T(8,128)(2,1)} %get-tuple-element.42), channel_id=1, source_target_pairs={{0,72},{8,200},{16,88},{24,216},{32,104},{40,232},{48,120},{56,248... | collective-permute-start | bytes 4718600 | tf_op jit(solution)/shard_map/ppermute | solution.py:409
  77.3 4.5 %collective-permute-done.8.refs_3_ = bf16[3072,256]{1,0:T(8,128)(2,1)} collective-permute-done((bf16[3072,256]{1,0:T(8,128)(2,1)}, bf16[3072,256]{1,0:T(8,128)(2,1)}, u32[]{:S(2)}, u32[]{:S(2)}) %collective-permute-start.8) | collective-permute-done | bytes 1572896 | tf_op jit(solution)/shard_map/ppermute | solution.py:415
  81.8 4.6 %all-gather.3.cloned.1.call-done = bf16[64,64,256]{2,1,0:T(8,128)(2,1)} async-done(((bf16[8,64,256]{2,1,0:T(8,128)(2,1)}), bf16[64,64,256]{2,1,0:T(8,128)(2,1)}) %all-gather.3.cloned.1.call-update) | async-done | bytes 2097168 | tf_op jit(solution)/shard_map/all_gather | solution.py:413
  86.4 11.5 %feed_forward_first.1 = (bf16[512,2048]{1,0:T(8,128)(2,1)}, f32[512,2048]{1,0:T(8,128)}) custom-call(bf16[8,8,64,256]{3,2,1,0:T(8,128)(2,1)} %bitcast.94, bf16[3072,256]{1,0:T(8,128)(2,1)} %get-tuple-element.45.refs_0_, bf16[3072,256]{1,0:T(8,128)(2,1)} %get-tuple-element.46.refs_1_, bf16[3072,256]{1,0:T(8,128)(2,1)} %collective-permute-done.7.refs_2_, ...), custom_call_target="tpu_custom_call" | custom-call | flops 3000000000 | bytes 8000000 | tf_op jit(solution)/shard_map/feed_forward_first/pallas_call | solution.py:292
  97.9 8.9 %collective-permute-done.3.refs_0_ = bf16[3072,256]{1,0:T(8,128)(2,1)S(1)} collective-permute-done((bf16[3072,256]{1,0:T(8,128)(2,1)}, bf16[3072,256]{1,0:T(8,128)(2,1)S(1)}, u32[]{:S(2)}, u32[]{:S(2)}) %collective-permute-start.3) | collective-permute-done | bytes 1572896 | tf_op jit(solution)/shard_map/ppermute | solution.py:409
  106.9 4.6 %collective-permute-done.4.refs_1_ = bf16[3072,256]{1,0:T(8,128)(2,1)} collective-permute-done((bf16[3072,256]{1,0:T(8,128)(2,1)}, bf16[3072,256]{1,0:T(8,128)(2,1)}, u32[]{:S(2)}, u32[]{:S(2)}) %collective-permute-start.4) | collective-permute-done | bytes 1572896 | tf_op jit(solution)/shard_map/ppermute | solution.py:409
  111.5 3.8 %collective-permute-start.10 = (bf16[3072,256]{1,0:T(8,128)(2,1)}, bf16[3072,256]{1,0:T(8,128)(2,1)}, u32[]{:S(2)}, u32[]{:S(2)}) collective-permute-start(bf16[3072,256]{1,0:T(8,128)(2,1)} %get-tuple-element.53.refs_1_), channel_id=1, source_target_pairs={{0,8},{8,0},{16,24},{24,16},{32,40},{40,32},{48,56},{56,48},{1,9},... | collective-permute-start | bytes 4718600 | tf_op jit(solution)/shard_map/ppermute | solution.py:415
  115.4 7.0 %feed_forward_middle.1.hidden_in.hidden_all = bf16[512,256]{1,0:T(8,128)(2,1)} custom-call(bf16[512,2048]{1,0:T(8,128)(2,1)} %get-tuple-element.48.normed.normed_all, bf16[3072,256]{1,0:T(8,128)(2,1)} %get-tuple-element.52.refs_0_, bf16[3072,256]{1,0:T(8,128)(2,1)} %get-tuple-element.53.refs_1_), custom_call_target="tpu_custom_call" | custom-call | flops 3000000000 | bytes 8000000 | tf_op jit(solution)/shard_map/feed_forward_middle/pallas_call | solution.py:309
  122.4 0.9 copy-done.6
  123.4 3.6 %feed_forward_far.1 = (bf16[64,1024]{1,0:T(8,128)(2,1)S(1)}, bf16[64,1024]{1,0:T(8,128)(2,1)S(1)}) custom-call(bf16[512,2048]{1,0:T(8,128)(2,1)S(1)} %copy-done.2, f32[512,2048]{1,0:T(8,128)S(1)} %copy-done.1, bf16[512,256]{1,0:T(8,128)(2,1)S(1)} %copy-done.6, bf16[3072,256]{1,0:T(8,128)(2,1)S(1)} %copy-done.4, bf16[3072,256]{1,0:T(8,128)(2,1)} %get-tuple-element.53.refs_1_, ...), custom_call_target="tpu_custom_call" | custom-call | flops 3000000000 | bytes 8000000 | tf_op jit(solution)/shard_map/feed_forward_far/pallas_call | solution.py:322
  127.0 1.4 collective-permute-start.11
  128.4 4.3 %collective-permute-start.12 = (bf16[64,1024]{1,0:T(8,128)(2,1)S(1)}, bf16[64,1024]{1,0:T(8,128)(2,1)S(1)}, u32[]{:S(2)}, u32[]{:S(2)}) collective-permute-start(bf16[64,1024]{1,0:T(8,128)(2,1)S(1)} %get-tuple-element.55), channel_id=1, source_target_pairs={{0,7},{1,0},{2,1},{3,2},{4,3},{5,4},{6,5},{7,6},{8,15},{9,8},{10,9... | collective-permute-start | bytes 393224 | tf_op jit(solution)/shard_map/ppermute | solution.py:429
  132.7 5.4 %feed_forward_near.1 = bf16[8,64,2048]{2,1,0:T(8,128)(2,1)S(1)} custom-call(bf16[512,2048]{1,0:T(8,128)(2,1)S(1)} %copy-done.2, f32[512,2048]{1,0:T(8,128)S(1)} %copy-done.1, bf16[512,256]{1,0:T(8,128)(2,1)S(1)} %copy-done.6, bf16[3072,256]{1,0:T(8,128)(2,1)S(1)} %copy-done.5, bf16[3072,256]{1,0:T(8,128)(2,1)} %get-tuple-element.53.refs_1_, ...), custom_call_target="tpu_custom_call" | custom-call | flops 3000000000 | bytes 8000000 | tf_op jit(solution)/shard_map/feed_forward_near/pallas_call | solution.py:341
  138.3 2.7 %collective-permute-start.14 = (bf16[64,2048]{1,0:T(8,128)(2,1)S(1)}, bf16[64,2048]{1,0:T(8,128)(2,1)S(1)}, u32[]{:S(2)}, u32[]{:S(2)}) collective-permute-start(bf16[64,2048]{1,0:T(8,128)(2,1)S(1)} %get-tuple-element.57), channel_id=1, source_target_pairs={{0,7},{1,0},{2,1},{3,2},{4,3},{5,4},{6,5},{7,6},{8,15},{9,8},{10,9... | collective-permute-start | bytes 786440 | tf_op jit(solution)/shard_map/ppermute | solution.py:433
  140.9 5.8 %collective-permute-done.13 = bf16[64,2048]{1,0:T(8,128)(2,1)S(1)} collective-permute-done((bf16[64,2048]{1,0:T(8,128)(2,1)S(1)}, bf16[64,2048]{1,0:T(8,128)(2,1)S(1)}, u32[]{:S(2)}, u32[]{:S(2)}) %collective-permute-start.13) | collective-permute-done | bytes 262176 | tf_op jit(solution)/shard_map/ppermute | solution.py:433
  146.7 0.8 fusion.6
  147.6 2.7 %collective-permute-start.16 = (bf16[64,2048]{1,0:T(8,128)(2,1)S(1)}, bf16[64,2048]{1,0:T(8,128)(2,1)}, u32[]{:S(2)}, u32[]{:S(2)}) collective-permute-start(bf16[64,2048]{1,0:T(8,128)(2,1)S(1)} %get-tuple-element.59), channel_id=1, source_target_pairs={{0,7},{1,0},{2,1},{3,2},{4,3},{5,4},{6,5},{7,6},{8,15},{9,8},{10,9... | collective-permute-start | bytes 786440 | tf_op jit(solution)/shard_map/ppermute | solution.py:433
  150.3 5.2 %collective-permute-done.15 = bf16[64,2048]{1,0:T(8,128)(2,1)} collective-permute-done((bf16[64,2048]{1,0:T(8,128)(2,1)}, bf16[64,2048]{1,0:T(8,128)(2,1)}, u32[]{:S(2)}, u32[]{:S(2)}) %collective-permute-start.15) | collective-permute-done | bytes 262176 | tf_op jit(solution)/shard_map/ppermute | solution.py:433
  155.4 1.2 fusion.5
  157.0 2.3 %collective-permute-start.18 = (bf16[64,2048]{1,0:T(8,128)(2,1)S(1)}, bf16[64,2048]{1,0:T(8,128)(2,1)S(1)}, u32[]{:S(2)}, u32[]{:S(2)}) collective-permute-start(bf16[64,2048]{1,0:T(8,128)(2,1)S(1)} %get-tuple-element.61), channel_id=1, source_target_pairs={{0,7},{1,0},{2,1},{3,2},{4,3},{5,4},{6,5},{7,6},{8,15},{9,8},{10,9... | collective-permute-start | bytes 786440 | tf_op jit(solution)/shard_map/ppermute | solution.py:433
  159.4 1.0 constant_dynamic-slice_fusion
  160.6 2.5 %collective-permute-done.17 = bf16[64,2048]{1,0:T(8,128)(2,1)S(1)} collective-permute-done((bf16[64,2048]{1,0:T(8,128)(2,1)S(1)}, bf16[64,2048]{1,0:T(8,128)(2,1)S(1)}, u32[]{:S(2)}, u32[]{:S(2)}) %collective-permute-start.17) | collective-permute-done | bytes 262176 | tf_op jit(solution)/shard_map/ppermute | solution.py:433
  163.3 3.1 %collective-permute-start.19 = (bf16[16,2048]{1,0:T(8,128)(2,1)S(1)}, bf16[16,2048]{1,0:T(8,128)(2,1)S(1)}, u32[]{:S(2)}, u32[]{:S(2)}) collective-permute-start(bf16[16,2048]{1,0:T(8,128)(2,1)S(1)} %get-tuple-element.76), channel_id=1, source_target_pairs={{0,0},{128,8},{16,16},{144,24},{32,32},{160,40},{48,48},{176,56},{... | collective-permute-start | bytes 196616 | tf_op jit(solution)/shard_map/ppermute | solution.py:444
  166.4 1.2 collective-permute-start.20
  167.6 1.0 collective-permute-start.21
  168.6 4.4 %collective-permute-start.22 = (bf16[16,2048]{1,0:T(8,128)(2,1)S(1)}, bf16[16,2048]{1,0:T(8,128)(2,1)S(1)}, u32[]{:S(2)}, u32[]{:S(2)}) collective-permute-start(bf16[16,2048]{1,0:T(8,128)(2,1)S(1)} %get-tuple-element.77), channel_id=1, source_target_pairs={{72,0},{200,8},{88,16},{216,24},{104,32},{232,40},{120,48},{248,56... | collective-permute-start | bytes 196616 | tf_op jit(solution)/shard_map/ppermute | solution.py:444
  173.1 2.0 %collective-permute-done.22 = bf16[16,2048]{1,0:T(8,128)(2,1)S(1)} collective-permute-done((bf16[16,2048]{1,0:T(8,128)(2,1)S(1)}, bf16[16,2048]{1,0:T(8,128)(2,1)S(1)}, u32[]{:S(2)}, u32[]{:S(2)}) %collective-permute-start.22) | collective-permute-done | bytes 65568 | tf_op jit(solution)/shard_map/ppermute | solution.py:444
  175.2 1.5 fusion.1
  177.0 2.1 %collective-permute-start.23 = (f32[32,256]{1,0:T(8,128)S(1)}, f32[32,256]{1,0:T(8,128)S(1)}, u32[]{:S(2)}, u32[]{:S(2)}) collective-permute-start(f32[32,256]{1,0:T(8,128)S(1)} %convolution_add_fusion), channel_id=1, source_target_pairs={{0,8},{8,0},{16,24},{24,16},{32,40},{40,32},{48,56},{56,48},{1,9},... | collective-permute-start | bytes 98312 | tf_op jit(solution)/shard_map/ppermute | solution.py:415
  179.1 0.8 collective-permute-done.23
  179.9 1.2 collective-permute-start.24
  181.2 2.4 %collective-permute-start.25 = (f32[32,256]{1,0:T(8,128)S(1)}, f32[32,256]{1,0:T(8,128)S(1)}, u32[]{:S(2)}, u32[]{:S(2)}) collective-permute-start(f32[32,256]{1,0:T(8,128)S(1)} %add.127), channel_id=1, source_target_pairs={{0,32},{8,40},{16,48},{24,56},{32,0},{40,8},{48,16},{56,24},{1,33}... | collective-permute-start | bytes 98312 | tf_op jit(solution)/shard_map/ppermute | solution.py:454
  183.8 1.0 copy.29
  185.5 2.1 %collective-permute-done.26 = f32[32,256]{1,0:T(8,128)S(1)} collective-permute-done((f32[32,256]{1,0:T(8,128)S(1)}, f32[32,256]{1,0:T(8,128)S(1)}, u32[]{:S(2)}, u32[]{:S(2)}) %collective-permute-start.26) | collective-permute-done | bytes 32800 | tf_op jit(solution)/shard_map/ppermute | solution.py:454
  187.6 0.7 fusion.17
  (65 shorter events, 4.7 us)
Async XLA Ops:
  7.2 1.2 copy-start
  7.2 79.3 %all-gather.3.cloned.1.call-start = ((), (), s32[]{:S(2)}) async-start(), calls=%async_computation.1 | async-start | bytes 2359296 | tf_op jit(solution)/shard_map/all_gather | solution.py:413
  11.0 25.6 %copy-start.9 = (bf16[128,2,2048]{2,1,0:T(2,128)(2,1)S(1)}, bf16[128,2,2048]{2,1,0:T(2,128)(2,1)}, u32[]{:S(2)}) copy-start(bf16[128,2,2048]{2,1,0:T(2,128)(2,1)} %param.16) | copy-start | bytes 3145732
  21.6 15.4 %copy-start.7 = (bf16[2,128,2048]{2,1,0:T(8,128)(2,1)S(1)}, bf16[2,128,2048]{2,1,0:T(8,128)(2,1)}, u32[]{:S(2)}) copy-start(bf16[2,128,2048]{2,1,0:T(8,128)(2,1)} %ow_ref.1) | copy-start | bytes 3145732
  21.6 15.4 %copy-start.8 = (bf16[288,128]{1,0:T(8,128)(2,1)S(1)}, bf16[288,128]{1,0:T(8,128)(2,1)}, u32[]{:S(2)}) copy-start(bf16[288,128]{1,0:T(8,128)(2,1)} %get-tuple-element.37.p0) | copy-start | bytes 221188
  21.6 5.9 %collective-permute-start = (bf16[288,128]{1,0:T(8,128)(2,1)}, bf16[288,128]{1,0:T(8,128)(2,1)S(1)}, u32[]{:S(2)}, u32[]{:S(2)}) collective-permute-start(bf16[288,128]{1,0:T(8,128)(2,1)} %get-tuple-element.37.p0), channel_id=1, source_target_pairs={{0,64},{64,128},{128,192},{192,0},{1,65},{65,129},{129,193},{193,1... | collective-permute-start | bytes 221192 | tf_op jit(solution)/shard_map/ppermute | solution.py:407
  23.8 5.8 %collective-permute-start.1 = (bf16[288,128]{1,0:T(8,128)(2,1)}, bf16[288,128]{1,0:T(8,128)(2,1)S(1)}, u32[]{:S(2)}, u32[]{:S(2)}) collective-permute-start(bf16[288,128]{1,0:T(8,128)(2,1)} %get-tuple-element.37.p0), channel_id=1, source_target_pairs={{0,128},{64,192},{128,0},{192,64},{1,129},{65,193},{129,1},{193,65... | collective-permute-start | bytes 221192 | tf_op jit(solution)/shard_map/ppermute | solution.py:407
  26.4 3.7 %collective-permute-start.2 = (bf16[288,128]{1,0:T(8,128)(2,1)}, bf16[288,128]{1,0:T(8,128)(2,1)S(1)}, u32[]{:S(2)}, u32[]{:S(2)}) collective-permute-start(bf16[288,128]{1,0:T(8,128)(2,1)} %get-tuple-element.37.p0), channel_id=1, source_target_pairs={{0,192},{64,0},{128,64},{192,128},{1,193},{65,1},{129,65},{193,129... | collective-permute-start | bytes 221192 | tf_op jit(solution)/shard_map/ppermute | solution.py:407
  30.1 39.9 %collective-permute-start.5 = (bf16[3072,256]{1,0:T(8,128)(2,1)}, bf16[3072,256]{1,0:T(8,128)(2,1)S(1)}, u32[]{:S(2)}, u32[]{:S(2)}) collective-permute-start(bf16[3072,256]{1,0:T(8,128)(2,1)} %get-tuple-element.43), channel_id=1, source_target_pairs={{0,0},{8,128},{16,16},{24,144},{32,32},{40,160},{48,48},{56,176},{... | collective-permute-start | bytes 4718600 | tf_op jit(solution)/shard_map/ppermute | solution.py:409
  35.5 38.1 %collective-permute-start.6 = (bf16[3072,256]{1,0:T(8,128)(2,1)}, bf16[3072,256]{1,0:T(8,128)(2,1)}, u32[]{:S(2)}, u32[]{:S(2)}) collective-permute-start(bf16[3072,256]{1,0:T(8,128)(2,1)} %get-tuple-element.44), channel_id=1, source_target_pairs={{0,64},{8,192},{16,80},{24,208},{32,96},{40,224},{48,112},{56,240}... | collective-permute-start | bytes 4718600 | tf_op jit(solution)/shard_map/ppermute | solution.py:409
  70.0 3.6 %copy-start.11 = (bf16[3072,256]{1,0:T(8,128)(2,1)}, bf16[3072,256]{1,0:T(8,128)(2,1)S(1)}, u32[]{:S(2)}) copy-start(bf16[3072,256]{1,0:T(8,128)(2,1)S(1)} %collective-permute-done.5.refs_0_) | copy-start | bytes 4718596
  73.6 3.8 %collective-permute-start.7 = (bf16[3072,256]{1,0:T(8,128)(2,1)}, bf16[3072,256]{1,0:T(8,128)(2,1)}, u32[]{:S(2)}, u32[]{:S(2)}) collective-permute-start(bf16[3072,256]{1,0:T(8,128)(2,1)} %get-tuple-element.45.refs_0_), channel_id=1, source_target_pairs={{0,8},{8,0},{16,24},{24,16},{32,40},{40,32},{48,56},{56,48},{1,9},... | collective-permute-start | bytes 4718600 | tf_op jit(solution)/shard_map/ppermute | solution.py:415
  73.6 8.2 %collective-permute-start.8 = (bf16[3072,256]{1,0:T(8,128)(2,1)}, bf16[3072,256]{1,0:T(8,128)(2,1)}, u32[]{:S(2)}, u32[]{:S(2)}) collective-permute-start(bf16[3072,256]{1,0:T(8,128)(2,1)} %get-tuple-element.46.refs_1_), channel_id=1, source_target_pairs={{0,8},{8,0},{16,24},{24,16},{32,40},{40,32},{48,56},{56,48},{1,9},... | collective-permute-start | bytes 4718600 | tf_op jit(solution)/shard_map/ppermute | solution.py:415
  74.1 32.8 %collective-permute-start.3 = (bf16[3072,256]{1,0:T(8,128)(2,1)}, bf16[3072,256]{1,0:T(8,128)(2,1)S(1)}, u32[]{:S(2)}, u32[]{:S(2)}) collective-permute-start(bf16[3072,256]{1,0:T(8,128)(2,1)} %get-tuple-element.41), channel_id=1, source_target_pairs={{0,8},{8,136},{16,24},{24,152},{32,40},{40,168},{48,56},{56,184},{... | collective-permute-start | bytes 4718600 | tf_op jit(solution)/shard_map/ppermute | solution.py:409
  74.8 36.7 %collective-permute-start.4 = (bf16[3072,256]{1,0:T(8,128)(2,1)}, bf16[3072,256]{1,0:T(8,128)(2,1)}, u32[]{:S(2)}, u32[]{:S(2)}) collective-permute-start(bf16[3072,256]{1,0:T(8,128)(2,1)} %get-tuple-element.42), channel_id=1, source_target_pairs={{0,72},{8,200},{16,88},{24,216},{32,104},{40,232},{48,120},{56,248... | collective-permute-start | bytes 4718600 | tf_op jit(solution)/shard_map/ppermute | solution.py:409
  106.9 4.6 %copy-start.3 = (bf16[3072,256]{1,0:T(8,128)(2,1)}, bf16[3072,256]{1,0:T(8,128)(2,1)S(1)}, u32[]{:S(2)}) copy-start(bf16[3072,256]{1,0:T(8,128)(2,1)S(1)} %collective-permute-done.3.refs_0_) | copy-start | bytes 4718596
  111.5 10.9 %collective-permute-start.10 = (bf16[3072,256]{1,0:T(8,128)(2,1)}, bf16[3072,256]{1,0:T(8,128)(2,1)}, u32[]{:S(2)}, u32[]{:S(2)}) collective-permute-start(bf16[3072,256]{1,0:T(8,128)(2,1)} %get-tuple-element.53.refs_1_), channel_id=1, source_target_pairs={{0,8},{8,0},{16,24},{24,16},{32,40},{40,32},{48,56},{56,48},{1,9},... | collective-permute-start | bytes 4718600 | tf_op jit(solution)/shard_map/ppermute | solution.py:415
  115.3 7.1 %copy-start.1 = (f32[512,2048]{1,0:T(8,128)S(1)}, f32[512,2048]{1,0:T(8,128)}, u32[]{:S(2)}) copy-start(f32[512,2048]{1,0:T(8,128)} %get-tuple-element.49.so_far.so_far_all) | copy-start | bytes 12582916
  115.3 7.1 %copy-start.2 = (bf16[512,2048]{1,0:T(8,128)(2,1)S(1)}, bf16[512,2048]{1,0:T(8,128)(2,1)}, u32[]{:S(2)}) copy-start(bf16[512,2048]{1,0:T(8,128)(2,1)} %get-tuple-element.48.normed.normed_all) | copy-start | bytes 6291460
  115.3 7.1 %copy-start.4 = (bf16[3072,256]{1,0:T(8,128)(2,1)S(1)}, bf16[3072,256]{1,0:T(8,128)(2,1)}, u32[]{:S(2)}) copy-start(bf16[3072,256]{1,0:T(8,128)(2,1)} %get-tuple-element.52.refs_0_) | copy-start | bytes 4718596
  115.3 7.1 %collective-permute-start.9 = (bf16[3072,256]{1,0:T(8,128)(2,1)}, bf16[3072,256]{1,0:T(8,128)(2,1)}, u32[]{:S(2)}, u32[]{:S(2)}) collective-permute-start(bf16[3072,256]{1,0:T(8,128)(2,1)} %get-tuple-element.52.refs_0_), channel_id=1, source_target_pairs={{0,8},{8,0},{16,24},{24,16},{32,40},{40,32},{48,56},{56,48},{1,9},... | collective-permute-start | bytes 4718600 | tf_op jit(solution)/shard_map/ppermute | solution.py:415
  122.4 1.0 copy-start.6
  123.4 9.3 %copy-start.5 = (bf16[3072,256]{1,0:T(8,128)(2,1)S(1)}, bf16[3072,256]{1,0:T(8,128)(2,1)}, u32[]{:S(2)}) copy-start(bf16[3072,256]{1,0:T(8,128)(2,1)} %get-tuple-element.52.refs_0_) | copy-start | bytes 4718596
  127.0 11.1 %collective-permute-start.11 = (bf16[64,1024]{1,0:T(8,128)(2,1)S(1)}, bf16[64,1024]{1,0:T(8,128)(2,1)S(1)}, u32[]{:S(2)}, u32[]{:S(2)}) collective-permute-start(bf16[64,1024]{1,0:T(8,128)(2,1)S(1)} %get-tuple-element.54), channel_id=1, source_target_pairs={{0,1},{1,2},{2,3},{3,4},{4,5},{5,6},{6,7},{7,0},{8,9},{9,10},{10,1... | collective-permute-start | bytes 393224 | tf_op jit(solution)/shard_map/ppermute | solution.py:429
  128.4 9.7 %collective-permute-start.12 = (bf16[64,1024]{1,0:T(8,128)(2,1)S(1)}, bf16[64,1024]{1,0:T(8,128)(2,1)S(1)}, u32[]{:S(2)}, u32[]{:S(2)}) collective-permute-start(bf16[64,1024]{1,0:T(8,128)(2,1)S(1)} %get-tuple-element.55), channel_id=1, source_target_pairs={{0,7},{1,0},{2,1},{3,2},{4,3},{5,4},{6,5},{7,6},{8,15},{9,8},{10,9... | collective-permute-start | bytes 393224 | tf_op jit(solution)/shard_map/ppermute | solution.py:429
  138.2 8.6 %collective-permute-start.13 = (bf16[64,2048]{1,0:T(8,128)(2,1)S(1)}, bf16[64,2048]{1,0:T(8,128)(2,1)S(1)}, u32[]{:S(2)}, u32[]{:S(2)}) collective-permute-start(bf16[64,2048]{1,0:T(8,128)(2,1)S(1)} %get-tuple-element.56), channel_id=1, source_target_pairs={{0,1},{1,2},{2,3},{3,4},{4,5},{5,6},{6,7},{7,0},{8,9},{9,10},{10,1... | collective-permute-start | bytes 786440 | tf_op jit(solution)/shard_map/ppermute | solution.py:433
  138.3 8.5 %collective-permute-start.14 = (bf16[64,2048]{1,0:T(8,128)(2,1)S(1)}, bf16[64,2048]{1,0:T(8,128)(2,1)S(1)}, u32[]{:S(2)}, u32[]{:S(2)}) collective-permute-start(bf16[64,2048]{1,0:T(8,128)(2,1)S(1)} %get-tuple-element.57), channel_id=1, source_target_pairs={{0,7},{1,0},{2,1},{3,2},{4,3},{5,4},{6,5},{7,6},{8,15},{9,8},{10,9... | collective-permute-start | bytes 786440 | tf_op jit(solution)/shard_map/ppermute | solution.py:433
  147.6 7.9 %collective-permute-start.15 = (bf16[64,2048]{1,0:T(8,128)(2,1)}, bf16[64,2048]{1,0:T(8,128)(2,1)}, u32[]{:S(2)}, u32[]{:S(2)}) collective-permute-start(bf16[64,2048]{1,0:T(8,128)(2,1)} %get-tuple-element.58), channel_id=1, source_target_pairs={{0,1},{1,2},{2,3},{3,4},{4,5},{5,6},{6,7},{7,0},{8,9},{9,10},{10,1... | collective-permute-start | bytes 786440 | tf_op jit(solution)/shard_map/ppermute | solution.py:433
  147.6 7.9 %collective-permute-start.16 = (bf16[64,2048]{1,0:T(8,128)(2,1)S(1)}, bf16[64,2048]{1,0:T(8,128)(2,1)}, u32[]{:S(2)}, u32[]{:S(2)}) collective-permute-start(bf16[64,2048]{1,0:T(8,128)(2,1)S(1)} %get-tuple-element.59), channel_id=1, source_target_pairs={{0,7},{1,0},{2,1},{3,2},{4,3},{5,4},{6,5},{7,6},{8,15},{9,8},{10,9... | collective-permute-start | bytes 786440 | tf_op jit(solution)/shard_map/ppermute | solution.py:433
  156.6 6.5 %collective-permute-start.17 = (bf16[64,2048]{1,0:T(8,128)(2,1)S(1)}, bf16[64,2048]{1,0:T(8,128)(2,1)S(1)}, u32[]{:S(2)}, u32[]{:S(2)}) collective-permute-start(bf16[64,2048]{1,0:T(8,128)(2,1)S(1)} %get-tuple-element.60), channel_id=1, source_target_pairs={{0,1},{1,2},{2,3},{3,4},{4,5},{5,6},{6,7},{7,0},{8,9},{9,10},{10,1... | collective-permute-start | bytes 786440 | tf_op jit(solution)/shard_map/ppermute | solution.py:433
  157.0 6.1 %collective-permute-start.18 = (bf16[64,2048]{1,0:T(8,128)(2,1)S(1)}, bf16[64,2048]{1,0:T(8,128)(2,1)S(1)}, u32[]{:S(2)}, u32[]{:S(2)}) collective-permute-start(bf16[64,2048]{1,0:T(8,128)(2,1)S(1)} %get-tuple-element.61), channel_id=1, source_target_pairs={{0,7},{1,0},{2,1},{3,2},{4,3},{5,4},{6,5},{7,6},{8,15},{9,8},{10,9... | collective-permute-start | bytes 786440 | tf_op jit(solution)/shard_map/ppermute | solution.py:433
  163.3 9.8 %collective-permute-start.19 = (bf16[16,2048]{1,0:T(8,128)(2,1)S(1)}, bf16[16,2048]{1,0:T(8,128)(2,1)S(1)}, u32[]{:S(2)}, u32[]{:S(2)}) collective-permute-start(bf16[16,2048]{1,0:T(8,128)(2,1)S(1)} %get-tuple-element.76), channel_id=1, source_target_pairs={{0,0},{128,8},{16,16},{144,24},{32,32},{160,40},{48,48},{176,56},{... | collective-permute-start | bytes 196616 | tf_op jit(solution)/shard_map/ppermute | solution.py:444
  166.4 6.7 %collective-permute-start.20 = (bf16[16,2048]{1,0:T(8,128)(2,1)S(1)}, bf16[16,2048]{1,0:T(8,128)(2,1)S(1)}, u32[]{:S(2)}, u32[]{:S(2)}) collective-permute-start(bf16[16,2048]{1,0:T(8,128)(2,1)S(1)} %get-tuple-element.79), channel_id=1, source_target_pairs={{8,0},{136,8},{24,16},{152,24},{40,32},{168,40},{56,48},{184,56},{... | collective-permute-start | bytes 196616 | tf_op jit(solution)/shard_map/ppermute | solution.py:444
  167.6 5.5 %collective-permute-start.21 = (bf16[16,2048]{1,0:T(8,128)(2,1)S(1)}, bf16[16,2048]{1,0:T(8,128)(2,1)S(1)}, u32[]{:S(2)}, u32[]{:S(2)}) collective-permute-start(bf16[16,2048]{1,0:T(8,128)(2,1)S(1)} %get-tuple-element.78), channel_id=1, source_target_pairs={{64,0},{192,8},{80,16},{208,24},{96,32},{224,40},{112,48},{240,56}... | collective-permute-start | bytes 196616 | tf_op jit(solution)/shard_map/ppermute | solution.py:444
  168.6 6.5 %collective-permute-start.22 = (bf16[16,2048]{1,0:T(8,128)(2,1)S(1)}, bf16[16,2048]{1,0:T(8,128)(2,1)S(1)}, u32[]{:S(2)}, u32[]{:S(2)}) collective-permute-start(bf16[16,2048]{1,0:T(8,128)(2,1)S(1)} %get-tuple-element.77), channel_id=1, source_target_pairs={{72,0},{200,8},{88,16},{216,24},{104,32},{232,40},{120,48},{248,56... | collective-permute-start | bytes 196616 | tf_op jit(solution)/shard_map/ppermute | solution.py:444
  173.0 3.7 %copy-start.10 = (bf16[2,2048,256]{2,1,0:T(8,128)(2,1)S(1)}, bf16[2,2048,256]{2,1,0:T(8,128)(2,1)}, u32[]{:S(2)}) copy-start(bf16[2,2048,256]{2,1,0:T(8,128)(2,1)} %param.29) | copy-start | bytes 6291460
  175.1 12.4 %copy-start.12 = (bf16[256,4]{0,1:T(4,128)(2,1)S(1)}, bf16[256,4]{0,1:T(4,128)(2,1)}, u32[]{:S(2)}) copy-start(bf16[256,4]{0,1:T(4,128)(2,1)} %param.31) | copy-start | bytes 6148
  175.2 12.4 %copy-start.13 = (f32[256]{0:T(256)S(1)}, f32[256]{0:T(256)}, u32[]{:S(2)}) copy-start(f32[256]{0:T(256)} %param.30) | copy-start | bytes 3076
  177.0 2.9 %collective-permute-start.23 = (f32[32,256]{1,0:T(8,128)S(1)}, f32[32,256]{1,0:T(8,128)S(1)}, u32[]{:S(2)}, u32[]{:S(2)}) collective-permute-start(f32[32,256]{1,0:T(8,128)S(1)} %convolution_add_fusion), channel_id=1, source_target_pairs={{0,8},{8,0},{16,24},{24,16},{32,40},{40,32},{48,56},{56,48},{1,9},... | collective-permute-start | bytes 98312 | tf_op jit(solution)/shard_map/ppermute | solution.py:415
  179.9 4.9 %collective-permute-start.24 = (f32[32,256]{1,0:T(8,128)S(1)}, f32[32,256]{1,0:T(8,128)S(1)}, u32[]{:S(2)}, u32[]{:S(2)}) collective-permute-start(f32[32,256]{1,0:T(8,128)S(1)} %add.127), channel_id=1, source_target_pairs={{0,16},{8,24},{16,0},{24,8},{32,48},{40,56},{48,32},{56,40},{1,17}... | collective-permute-start | bytes 98312 | tf_op jit(solution)/shard_map/ppermute | solution.py:454
  181.2 4.3 %collective-permute-start.25 = (f32[32,256]{1,0:T(8,128)S(1)}, f32[32,256]{1,0:T(8,128)S(1)}, u32[]{:S(2)}, u32[]{:S(2)}) collective-permute-start(f32[32,256]{1,0:T(8,128)S(1)} %add.127), channel_id=1, source_target_pairs={{0,32},{8,40},{16,48},{24,56},{32,0},{40,8},{48,16},{56,24},{1,33}... | collective-permute-start | bytes 98312 | tf_op jit(solution)/shard_map/ppermute | solution.py:454
  183.6 4.0 %collective-permute-start.26 = (f32[32,256]{1,0:T(8,128)S(1)}, f32[32,256]{1,0:T(8,128)S(1)}, u32[]{:S(2)}, u32[]{:S(2)}) collective-permute-start(f32[32,256]{1,0:T(8,128)S(1)} %add.127), channel_id=1, source_target_pairs={{0,48},{8,56},{16,32},{24,40},{32,16},{40,24},{48,0},{56,8},{1,49}... | collective-permute-start | bytes 98312 | tf_op jit(solution)/shard_map/ppermute | solution.py:454
Sparse Core Ops, SparseCore 0:
  48.6 37.7 all-gather.2

commit v4 on v3

--- a/solution.py
+++ b/solution.py
@@ -58,7 +58,7 @@
         owner_ref[0:128, :] = user[:, 0:1]
         owner_ref[128:256, :] = user[:, 0:1]
 
-    @pl.when(step == 3)
+    @pl.when(step == 1)
     def _():
         for copy in pack_copies(gate_ref, up_ref, down_ref, held, sem):
             copy.wait()
@@ -232,9 +232,9 @@
         pltpu.make_async_copy(normed_all.at[pl.ds(256, 64)], normed, sem.at[0]),
         pltpu.make_async_copy(so_far_all.at[pl.ds(256, 64)], so_far, sem.at[1]),
     ] + [pltpu.make_async_copy(late[p].at[pl.ds(2048, 1024)], downs.at[p], sem.at[2 + p]) for p in range(2)]
+    copies.append(pltpu.make_async_copy(hidden_all.at[pl.ds(256, 64)], hidden.at[:, pl.ds(0, 256)], sem.at[4]))
     for copy in copies:
         copy.start()
-    hidden[:, 0:256] = hidden_all[256:320, :]
     copies[0].wait()
     for p in range(2):
         hidden_part(normed, swapped[p][0:2048, :], hidden, 2 + p)
@@ -322,14 +322,14 @@
     return pl.pallas_call(
         far_kernel,
         out_shape=[jax.ShapeDtypeStruct((64, 1024), BF16)] * 2,
-        in_specs=[ANY_SPEC, ANY_SPEC, VMEM_SPEC, ANY_SPEC, ANY_SPEC, VMEM_SPEC, VMEM_SPEC],
+        in_specs=[ANY_SPEC] * 5 + [VMEM_SPEC] * 2,
         out_specs=[VMEM_SPEC] * 2,
         scratch_shapes=[
             pltpu.VMEM((64, 512), BF16),
             pltpu.VMEM((64, 2048), BF16),
             pltpu.VMEM((64, 2048), F32),
             pltpu.VMEM((2, 1024, 256), BF16),
-            pltpu.SemaphoreType.DMA((4,)),
+            pltpu.SemaphoreType.DMA((5,)),
         ],
         compiler_params=pltpu.CompilerParams(vmem_limit_bytes=28 << 20),
         cost_estimate=FFN_COST,

time: 197 us -> 197 us (level)
  no operation moved by 1% of the time
where the time goes in v4:
time: 197 us; the launch traced here: 196 us
  waiting for transfers between devices  69.7 us (35%)
  starting transfers between devices  49.4 us (25%)
  Pallas kernels  39 us (20%)
  between operations  14.4 us (7%)
  blocking collectives  10.9 us (6%)
  matrix products  5.15 us (3%)
  local copies, waits for them, and re-layouts  4.7 us (2%)
  other arithmetic  2.35 us (1%)
    ppermute x4, waiting for transfers between devices, shards(): lax.ppermute(pack, both, exchange_pairs(r, False))  38.6 us
    ppermute x3, waiting for transfers between devices, shards(): lax.ppermute(up, 'cand', right)  13.5 us
    pallas_call x1, Pallas kernels, feed_forward_first(): pl.pallas_call(first_kernel, out_shape=[jax.ShapeDtypeStruct((512, 2048),...  11.5 us
    pallas_call x1, Pallas kernels, attention(): pl.pallas_call(attention_kernel, out_shape=[jax.ShapeDtypeStruct((288, 12...  11 us
    all_to_all x1, blocking collectives, shards(): lax.all_to_all(outgoing, 'tok', split_axis=0, concat_axis=0, tiled=True)  10.9 us
    ppermute x4, starting transfers between devices, shards(): arrived.append(lax.ppermute(send, both, exchange_pairs(r, True)))  9.72 us
    ppermute x4, starting transfers between devices, shards(): lax.ppermute(pack, both, exchange_pairs(r, False))  9.5 us
    ppermute x3, starting transfers between devices, shards(): lax.ppermute(down, 'cand', left)  7.66 us
  transfers between devices with their start and end apart: 28, of which 16 were waited for; matrix products, arithmetic and copies ran while one was open for 1% of the time, Pallas kernels for 12%

profile of v4, /device:TPU:1, one launch (start us, length us, event | category | flops | bytes accessed | tf_op | source)
XLA Modules:
  0.0 195.6 jit_solution(16036956266869704468)
XLA Ops:
  7.2 1.2 copy-done
  8.4 2.6 %convolution_convert_fusion = bf16[2,128,128]{2,1,0:T(8,128)(2,1)} fusion(bf16[2,2048,128]{2,1,0:T(8,128)(2,1)S(1)} %copy-done, bf16[128,2,2048]{2,1,0:T(2,128)(2,1)} %param.16), kind=kOutput, calls=%fused_computation | convolution fusion | flops 134250496 | bytes 2162688 | tf_op jit(solution)/shard_map/tbd,tdk->tbk/dot_general | solution.py:393
  11.0 11.0 %attention.1 = (bf16[288,128]{1,0:T(8,128)(2,1)}, bf16[3072,256]{1,0:T(8,128)(2,1)}, bf16[3072,256]{1,0:T(8,128)(2,1)}, bf16[3072,256]{1,0:T(8,128)(2,1)}, bf16[3072,256]{1,0:T(8,128)(2,1)}) custom-call(s32[2]{0:T(128)} %length_ref.1, bf16[256,128]{1,0:T(8,128)(2,1)} %bitcast.89, s32[1,128]{1,0:T(1,128)} %bitcast.96, bf16[2,2560,128]{2,1,0:T(8,128)(2,1)} %hist_ref.1, ...), custom_call_target="tpu_custom_call" | custom-call | flops 1000000 | bytes 100000 | tf_op jit(solution)/shard_map/attention/pallas_call | solution.py:112
  22.0 2.2 %collective-permute-start = (bf16[288,128]{1,0:T(8,128)(2,1)}, bf16[288,128]{1,0:T(8,128)(2,1)S(1)}, u32[]{:S(2)}, u32[]{:S(2)}) collective-permute-start(bf16[288,128]{1,0:T(8,128)(2,1)} %get-tuple-element.37.p0), channel_id=1, source_target_pairs={{0,64},{64,128},{128,192},{192,0},{1,65},{65,129},{129,193},{193,1... | collective-permute-start | bytes 221192 | tf_op jit(solution)/shard_map/ppermute | solution.py:407
  24.2 2.6 %collective-permute-start.1 = (bf16[288,128]{1,0:T(8,128)(2,1)}, bf16[288,128]{1,0:T(8,128)(2,1)S(1)}, u32[]{:S(2)}, u32[]{:S(2)}) collective-permute-start(bf16[288,128]{1,0:T(8,128)(2,1)} %get-tuple-element.37.p0), channel_id=1, source_target_pairs={{0,128},{64,192},{128,0},{192,64},{1,129},{65,193},{129,1},{193,65... | collective-permute-start | bytes 221192 | tf_op jit(solution)/shard_map/ppermute | solution.py:407
  26.9 1.1 collective-permute-start.2
  27.9 2.1 %collective-permute-done.1.p2 = bf16[288,128]{1,0:T(8,128)(2,1)S(1)} collective-permute-done((bf16[288,128]{1,0:T(8,128)(2,1)}, bf16[288,128]{1,0:T(8,128)(2,1)S(1)}, u32[]{:S(2)}, u32[]{:S(2)}) %collective-permute-start.1) | collective-permute-done | bytes 73760 | tf_op jit(solution)/shard_map/ppermute | solution.py:407
  30.6 5.3 %collective-permute-start.5 = (bf16[3072,256]{1,0:T(8,128)(2,1)}, bf16[3072,256]{1,0:T(8,128)(2,1)S(1)}, u32[]{:S(2)}, u32[]{:S(2)}) collective-permute-start(bf16[3072,256]{1,0:T(8,128)(2,1)} %get-tuple-element.43), channel_id=1, source_target_pairs={{0,0},{8,128},{16,16},{24,144},{32,32},{40,160},{48,48},{56,176},{... | collective-permute-start | bytes 4718600 | tf_op jit(solution)/shard_map/ppermute | solution.py:409
  35.9 1.1 collective-permute-start.6
  38.0 10.9 %all_to_all.5 = bf16[8,64,256]{2,1,0:T(8,128)(2,1)} all-to-all(bf16[8,64,256]{2,1,0:T(8,128)(2,1)S(1)} %merge.1), channel_id=1, replica_groups=mesh['hist'=4,'tok'=8,'cand'=8] {'tok'}, dimensions={0} | all-to-all | bytes 524288 | tf_op jit(solution)/shard_map/all_to_all | solution.py:412
  48.9 21.5 %collective-permute-done.5.refs_0_ = bf16[3072,256]{1,0:T(8,128)(2,1)S(1)} collective-permute-done((bf16[3072,256]{1,0:T(8,128)(2,1)}, bf16[3072,256]{1,0:T(8,128)(2,1)S(1)}, u32[]{:S(2)}, u32[]{:S(2)}) %collective-permute-start.5) | collective-permute-done | bytes 1572896 | tf_op jit(solution)/shard_map/ppermute | solution.py:409
  70.4 3.6 %collective-permute-done.6.refs_1_ = bf16[3072,256]{1,0:T(8,128)(2,1)} collective-permute-done((bf16[3072,256]{1,0:T(8,128)(2,1)}, bf16[3072,256]{1,0:T(8,128)(2,1)}, u32[]{:S(2)}, u32[]{:S(2)}) %collective-permute-start.6) | collective-permute-done | bytes 1572896 | tf_op jit(solution)/shard_map/ppermute | solution.py:409
  74.5 0.7 collective-permute-start.3
  75.2 2.3 %collective-permute-start.4 = (bf16[3072,256]{1,0:T(8,128)(2,1)}, bf16[3072,256]{1,0:T(8,128)(2,1)}, u32[]{:S(2)}, u32[]{:S(2)}) collective-permute-start(bf16[3072,256]{1,0:T(8,128)(2,1)} %get-tuple-element.42), channel_id=1, source_target_pairs={{0,72},{8,200},{16,88},{24,216},{32,104},{40,232},{48,120},{56,248... | collective-permute-start | bytes 4718600 | tf_op jit(solution)/shard_map/ppermute | solution.py:409
  77.8 4.5 %collective-permute-done.8.refs_3_ = bf16[3072,256]{1,0:T(8,128)(2,1)} collective-permute-done((bf16[3072,256]{1,0:T(8,128)(2,1)}, bf16[3072,256]{1,0:T(8,128)(2,1)}, u32[]{:S(2)}, u32[]{:S(2)}) %collective-permute-start.8) | collective-permute-done | bytes 1572896 | tf_op jit(solution)/shard_map/ppermute | solution.py:415
  82.3 4.6 %all-gather.3.cloned.1.call-done = bf16[64,64,256]{2,1,0:T(8,128)(2,1)} async-done(((bf16[8,64,256]{2,1,0:T(8,128)(2,1)}), bf16[64,64,256]{2,1,0:T(8,128)(2,1)}) %all-gather.3.cloned.1.call-update) | async-done | bytes 2097168 | tf_op jit(solution)/shard_map/all_gather | solution.py:413
  86.9 11.5 %feed_forward_first.1 = (bf16[512,2048]{1,0:T(8,128)(2,1)}, f32[512,2048]{1,0:T(8,128)}) custom-call(bf16[8,8,64,256]{3,2,1,0:T(8,128)(2,1)} %bitcast.94, bf16[3072,256]{1,0:T(8,128)(2,1)} %get-tuple-element.45.refs_0_, bf16[3072,256]{1,0:T(8,128)(2,1)} %get-tuple-element.46.refs_1_, bf16[3072,256]{1,0:T(8,128)(2,1)} %collective-permute-done.7.refs_2_, ...), custom_call_target="tpu_custom_call" | custom-call | flops 3000000000 | bytes 8000000 | tf_op jit(solution)/shard_map/feed_forward_first/pallas_call | solution.py:292
  98.4 8.9 %collective-permute-done.3.refs_0_ = bf16[3072,256]{1,0:T(8,128)(2,1)S(1)} collective-permute-done((bf16[3072,256]{1,0:T(8,128)(2,1)}, bf16[3072,256]{1,0:T(8,128)(2,1)S(1)}, u32[]{:S(2)}, u32[]{:S(2)}) %collective-permute-start.3) | collective-permute-done | bytes 1572896 | tf_op jit(solution)/shard_map/ppermute | solution.py:409
  107.3 4.6 %collective-permute-done.4.refs_1_ = bf16[3072,256]{1,0:T(8,128)(2,1)} collective-permute-done((bf16[3072,256]{1,0:T(8,128)(2,1)}, bf16[3072,256]{1,0:T(8,128)(2,1)}, u32[]{:S(2)}, u32[]{:S(2)}) %collective-permute-start.4) | collective-permute-done | bytes 1572896 | tf_op jit(solution)/shard_map/ppermute | solution.py:409
  111.9 3.8 %collective-permute-start.10 = (bf16[3072,256]{1,0:T(8,128)(2,1)}, bf16[3072,256]{1,0:T(8,128)(2,1)}, u32[]{:S(2)}, u32[]{:S(2)}) collective-permute-start(bf16[3072,256]{1,0:T(8,128)(2,1)} %get-tuple-element.53.refs_1_), channel_id=1, source_target_pairs={{0,8},{8,0},{16,24},{24,16},{32,40},{40,32},{48,56},{56,48},{1,9},... | collective-permute-start | bytes 4718600 | tf_op jit(solution)/shard_map/ppermute | solution.py:415
  115.8 7.0 %feed_forward_middle.1.hidden_in.hidden_all = bf16[512,256]{1,0:T(8,128)(2,1)} custom-call(bf16[512,2048]{1,0:T(8,128)(2,1)} %get-tuple-element.48.normed.normed_all, bf16[3072,256]{1,0:T(8,128)(2,1)} %get-tuple-element.52.refs_0_, bf16[3072,256]{1,0:T(8,128)(2,1)} %get-tuple-element.53.refs_1_), custom_call_target="tpu_custom_call" | custom-call | flops 3000000000 | bytes 8000000 | tf_op jit(solution)/shard_map/feed_forward_middle/pallas_call | solution.py:309
  122.9 0.9 copy-done.6
  123.8 3.7 %feed_forward_far.1 = (bf16[64,1024]{1,0:T(8,128)(2,1)S(1)}, bf16[64,1024]{1,0:T(8,128)(2,1)S(1)}) custom-call(bf16[512,2048]{1,0:T(8,128)(2,1)S(1)} %copy-done.2, f32[512,2048]{1,0:T(8,128)S(1)} %copy-done.1, bf16[512,256]{1,0:T(8,128)(2,1)S(1)} %copy-done.6, bf16[3072,256]{1,0:T(8,128)(2,1)S(1)} %copy-done.4, bf16[3072,256]{1,0:T(8,128)(2,1)} %get-tuple-element.53.refs_1_, ...), custom_call_target="tpu_custom_call" | custom-call | flops 3000000000 | bytes 8000000 | tf_op jit(solution)/shard_map/feed_forward_far/pallas_call | solution.py:322
  127.5 1.4 collective-permute-start.11
  128.8 4.3 %collective-permute-start.12 = (bf16[64,1024]{1,0:T(8,128)(2,1)S(1)}, bf16[64,1024]{1,0:T(8,128)(2,1)S(1)}, u32[]{:S(2)}, u32[]{:S(2)}) collective-permute-start(bf16[64,1024]{1,0:T(8,128)(2,1)S(1)} %get-tuple-element.55), channel_id=1, source_target_pairs={{0,7},{1,0},{2,1},{3,2},{4,3},{5,4},{6,5},{7,6},{8,15},{9,8},{10,9... | collective-permute-start | bytes 393224 | tf_op jit(solution)/shard_map/ppermute | solution.py:429
  133.1 5.4 %feed_forward_near.1 = bf16[8,64,2048]{2,1,0:T(8,128)(2,1)S(1)} custom-call(bf16[512,2048]{1,0:T(8,128)(2,1)S(1)} %copy-done.2, f32[512,2048]{1,0:T(8,128)S(1)} %copy-done.1, bf16[512,256]{1,0:T(8,128)(2,1)S(1)} %copy-done.6, bf16[3072,256]{1,0:T(8,128)(2,1)S(1)} %copy-done.5, bf16[3072,256]{1,0:T(8,128)(2,1)} %get-tuple-element.53.refs_1_, ...), custom_call_target="tpu_custom_call" | custom-call | flops 3000000000 | bytes 8000000 | tf_op jit(solution)/shard_map/feed_forward_near/pallas_call | solution.py:341
  138.7 2.7 %collective-permute-start.14 = (bf16[64,2048]{1,0:T(8,128)(2,1)S(1)}, bf16[64,2048]{1,0:T(8,128)(2,1)S(1)}, u32[]{:S(2)}, u32[]{:S(2)}) collective-permute-start(bf16[64,2048]{1,0:T(8,128)(2,1)S(1)} %get-tuple-element.57), channel_id=1, source_target_pairs={{0,7},{1,0},{2,1},{3,2},{4,3},{5,4},{6,5},{7,6},{8,15},{9,8},{10,9... | collective-permute-start | bytes 786440 | tf_op jit(solution)/shard_map/ppermute | solution.py:433
  141.4 5.8 %collective-permute-done.13 = bf16[64,2048]{1,0:T(8,128)(2,1)S(1)} collective-permute-done((bf16[64,2048]{1,0:T(8,128)(2,1)S(1)}, bf16[64,2048]{1,0:T(8,128)(2,1)S(1)}, u32[]{:S(2)}, u32[]{:S(2)}) %collective-permute-start.13) | collective-permute-done | bytes 262176 | tf_op jit(solution)/shard_map/ppermute | solution.py:433
  147.2 0.8 fusion.6
  148.0 2.7 %collective-permute-start.16 = (bf16[64,2048]{1,0:T(8,128)(2,1)S(1)}, bf16[64,2048]{1,0:T(8,128)(2,1)}, u32[]{:S(2)}, u32[]{:S(2)}) collective-permute-start(bf16[64,2048]{1,0:T(8,128)(2,1)S(1)} %get-tuple-element.59), channel_id=1, source_target_pairs={{0,7},{1,0},{2,1},{3,2},{4,3},{5,4},{6,5},{7,6},{8,15},{9,8},{10,9... | collective-permute-start | bytes 786440 | tf_op jit(solution)/shard_map/ppermute | solution.py:433
  150.7 5.2 %collective-permute-done.15 = bf16[64,2048]{1,0:T(8,128)(2,1)} collective-permute-done((bf16[64,2048]{1,0:T(8,128)(2,1)}, bf16[64,2048]{1,0:T(8,128)(2,1)}, u32[]{:S(2)}, u32[]{:S(2)}) %collective-permute-start.15) | collective-permute-done | bytes 262176 | tf_op jit(solution)/shard_map/ppermute | solution.py:433
  155.9 1.2 fusion.5
  157.5 2.3 %collective-permute-start.18 = (bf16[64,2048]{1,0:T(8,128)(2,1)S(1)}, bf16[64,2048]{1,0:T(8,128)(2,1)S(1)}, u32[]{:S(2)}, u32[]{:S(2)}) collective-permute-start(bf16[64,2048]{1,0:T(8,128)(2,1)S(1)} %get-tuple-element.61), channel_id=1, source_target_pairs={{0,7},{1,0},{2,1},{3,2},{4,3},{5,4},{6,5},{7,6},{8,15},{9,8},{10,9... | collective-permute-start | bytes 786440 | tf_op jit(solution)/shard_map/ppermute | solution.py:433
  159.8 1.0 constant_dynamic-slice_fusion
  161.0 2.5 %collective-permute-done.17 = bf16[64,2048]{1,0:T(8,128)(2,1)S(1)} collective-permute-done((bf16[64,2048]{1,0:T(8,128)(2,1)S(1)}, bf16[64,2048]{1,0:T(8,128)(2,1)S(1)}, u32[]{:S(2)}, u32[]{:S(2)}) %collective-permute-start.17) | collective-permute-done | bytes 262176 | tf_op jit(solution)/shard_map/ppermute | solution.py:433
  163.7 3.1 %collective-permute-start.19 = (bf16[16,2048]{1,0:T(8,128)(2,1)S(1)}, bf16[16,2048]{1,0:T(8,128)(2,1)S(1)}, u32[]{:S(2)}, u32[]{:S(2)}) collective-permute-start(bf16[16,2048]{1,0:T(8,128)(2,1)S(1)} %get-tuple-element.76), channel_id=1, source_target_pairs={{0,0},{128,8},{16,16},{144,24},{32,32},{160,40},{48,48},{176,56},{... | collective-permute-start | bytes 196616 | tf_op jit(solution)/shard_map/ppermute | solution.py:444
  166.8 1.2 collective-permute-start.20
  168.0 1.0 collective-permute-start.21
  169.0 4.4 %collective-permute-start.22 = (bf16[16,2048]{1,0:T(8,128)(2,1)S(1)}, bf16[16,2048]{1,0:T(8,128)(2,1)S(1)}, u32[]{:S(2)}, u32[]{:S(2)}) collective-permute-start(bf16[16,2048]{1,0:T(8,128)(2,1)S(1)} %get-tuple-element.77), channel_id=1, source_target_pairs={{72,0},{200,8},{88,16},{216,24},{104,32},{232,40},{120,48},{248,56... | collective-permute-start | bytes 196616 | tf_op jit(solution)/shard_map/ppermute | solution.py:444
  173.5 2.0 %collective-permute-done.22 = bf16[16,2048]{1,0:T(8,128)(2,1)S(1)} collective-permute-done((bf16[16,2048]{1,0:T(8,128)(2,1)S(1)}, bf16[16,2048]{1,0:T(8,128)(2,1)S(1)}, u32[]{:S(2)}, u32[]{:S(2)}) %collective-permute-start.22) | collective-permute-done | bytes 65568 | tf_op jit(solution)/shard_map/ppermute | solution.py:444
  175.6 1.5 fusion.1
  177.4 2.1 %collective-permute-start.23 = (f32[32,256]{1,0:T(8,128)S(1)}, f32[32,256]{1,0:T(8,128)S(1)}, u32[]{:S(2)}, u32[]{:S(2)}) collective-permute-start(f32[32,256]{1,0:T(8,128)S(1)} %convolution_add_fusion), channel_id=1, source_target_pairs={{0,8},{8,0},{16,24},{24,16},{32,40},{40,32},{48,56},{56,48},{1,9},... | collective-permute-start | bytes 98312 | tf_op jit(solution)/shard_map/ppermute | solution.py:415
  179.5 0.8 collective-permute-done.23
  180.4 1.2 collective-permute-start.24
  181.6 2.4 %collective-permute-start.25 = (f32[32,256]{1,0:T(8,128)S(1)}, f32[32,256]{1,0:T(8,128)S(1)}, u32[]{:S(2)}, u32[]{:S(2)}) collective-permute-start(f32[32,256]{1,0:T(8,128)S(1)} %add.127), channel_id=1, source_target_pairs={{0,32},{8,40},{16,48},{24,56},{32,0},{40,8},{48,16},{56,24},{1,33}... | collective-permute-start | bytes 98312 | tf_op jit(solution)/shard_map/ppermute | solution.py:454
  184.3 1.0 copy.29
  185.9 2.1 %collective-permute-done.26 = f32[32,256]{1,0:T(8,128)S(1)} collective-permute-done((f32[32,256]{1,0:T(8,128)S(1)}, f32[32,256]{1,0:T(8,128)S(1)}, u32[]{:S(2)}, u32[]{:S(2)}) %collective-permute-start.26) | collective-permute-done | bytes 32800 | tf_op jit(solution)/shard_map/ppermute | solution.py:454
  188.0 0.7 fusion.17
  (65 shorter events, 4.7 us)
Async XLA Ops:
  7.2 1.2 copy-start
  7.2 79.7 %all-gather.3.cloned.1.call-start = ((), (), s32[]{:S(2)}) async-start(), calls=%async_computation.1 | async-start | bytes 2359296 | tf_op jit(solution)/shard_map/all_gather | solution.py:413
  11.0 26.0 %copy-start.9 = (bf16[128,2,2048]{2,1,0:T(2,128)(2,1)S(1)}, bf16[128,2,2048]{2,1,0:T(2,128)(2,1)}, u32[]{:S(2)}) copy-start(bf16[128,2,2048]{2,1,0:T(2,128)(2,1)} %param.16) | copy-start | bytes 3145732
  22.0 15.4 %copy-start.7 = (bf16[2,128,2048]{2,1,0:T(8,128)(2,1)S(1)}, bf16[2,128,2048]{2,1,0:T(8,128)(2,1)}, u32[]{:S(2)}) copy-start(bf16[2,128,2048]{2,1,0:T(8,128)(2,1)} %ow_ref.1) | copy-start | bytes 3145732
  22.0 15.4 %copy-start.8 = (bf16[288,128]{1,0:T(8,128)(2,1)S(1)}, bf16[288,128]{1,0:T(8,128)(2,1)}, u32[]{:S(2)}) copy-start(bf16[288,128]{1,0:T(8,128)(2,1)} %get-tuple-element.37.p0) | copy-start | bytes 221188
  22.0 5.9 %collective-permute-start = (bf16[288,128]{1,0:T(8,128)(2,1)}, bf16[288,128]{1,0:T(8,128)(2,1)S(1)}, u32[]{:S(2)}, u32[]{:S(2)}) collective-permute-start(bf16[288,128]{1,0:T(8,128)(2,1)} %get-tuple-element.37.p0), channel_id=1, source_target_pairs={{0,64},{64,128},{128,192},{192,0},{1,65},{65,129},{129,193},{193,1... | collective-permute-start | bytes 221192 | tf_op jit(solution)/shard_map/ppermute | solution.py:407
  24.2 5.8 %collective-permute-start.1 = (bf16[288,128]{1,0:T(8,128)(2,1)}, bf16[288,128]{1,0:T(8,128)(2,1)S(1)}, u32[]{:S(2)}, u32[]{:S(2)}) collective-permute-start(bf16[288,128]{1,0:T(8,128)(2,1)} %get-tuple-element.37.p0), channel_id=1, source_target_pairs={{0,128},{64,192},{128,0},{192,64},{1,129},{65,193},{129,1},{193,65... | collective-permute-start | bytes 221192 | tf_op jit(solution)/shard_map/ppermute | solution.py:407
  26.9 3.7 %collective-permute-start.2 = (bf16[288,128]{1,0:T(8,128)(2,1)}, bf16[288,128]{1,0:T(8,128)(2,1)S(1)}, u32[]{:S(2)}, u32[]{:S(2)}) collective-permute-start(bf16[288,128]{1,0:T(8,128)(2,1)} %get-tuple-element.37.p0), channel_id=1, source_target_pairs={{0,192},{64,0},{128,64},{192,128},{1,193},{65,1},{129,65},{193,129... | collective-permute-start | bytes 221192 | tf_op jit(solution)/shard_map/ppermute | solution.py:407
  30.6 39.9 %collective-permute-start.5 = (bf16[3072,256]{1,0:T(8,128)(2,1)}, bf16[3072,256]{1,0:T(8,128)(2,1)S(1)}, u32[]{:S(2)}, u32[]{:S(2)}) collective-permute-start(bf16[3072,256]{1,0:T(8,128)(2,1)} %get-tuple-element.43), channel_id=1, source_target_pairs={{0,0},{8,128},{16,16},{24,144},{32,32},{40,160},{48,48},{56,176},{... | collective-permute-start | bytes 4718600 | tf_op jit(solution)/shard_map/ppermute | solution.py:409
  35.9 38.1 %collective-permute-start.6 = (bf16[3072,256]{1,0:T(8,128)(2,1)}, bf16[3072,256]{1,0:T(8,128)(2,1)}, u32[]{:S(2)}, u32[]{:S(2)}) collective-permute-start(bf16[3072,256]{1,0:T(8,128)(2,1)} %get-tuple-element.44), channel_id=1, source_target_pairs={{0,64},{8,192},{16,80},{24,208},{32,96},{40,224},{48,112},{56,240}... | collective-permute-start | bytes 4718600 | tf_op jit(solution)/shard_map/ppermute | solution.py:409
  70.4 3.6 %copy-start.11 = (bf16[3072,256]{1,0:T(8,128)(2,1)}, bf16[3072,256]{1,0:T(8,128)(2,1)S(1)}, u32[]{:S(2)}) copy-start(bf16[3072,256]{1,0:T(8,128)(2,1)S(1)} %collective-permute-done.5.refs_0_) | copy-start | bytes 4718596
  74.0 3.8 %collective-permute-start.7 = (bf16[3072,256]{1,0:T(8,128)(2,1)}, bf16[3072,256]{1,0:T(8,128)(2,1)}, u32[]{:S(2)}, u32[]{:S(2)}) collective-permute-start(bf16[3072,256]{1,0:T(8,128)(2,1)} %get-tuple-element.45.refs_0_), channel_id=1, source_target_pairs={{0,8},{8,0},{16,24},{24,16},{32,40},{40,32},{48,56},{56,48},{1,9},... | collective-permute-start | bytes 4718600 | tf_op jit(solution)/shard_map/ppermute | solution.py:415
  74.0 8.2 %collective-permute-start.8 = (bf16[3072,256]{1,0:T(8,128)(2,1)}, bf16[3072,256]{1,0:T(8,128)(2,1)}, u32[]{:S(2)}, u32[]{:S(2)}) collective-permute-start(bf16[3072,256]{1,0:T(8,128)(2,1)} %get-tuple-element.46.refs_1_), channel_id=1, source_target_pairs={{0,8},{8,0},{16,24},{24,16},{32,40},{40,32},{48,56},{56,48},{1,9},... | collective-permute-start | bytes 4718600 | tf_op jit(solution)/shard_map/ppermute | solution.py:415
  74.5 32.7 %collective-permute-start.3 = (bf16[3072,256]{1,0:T(8,128)(2,1)}, bf16[3072,256]{1,0:T(8,128)(2,1)S(1)}, u32[]{:S(2)}, u32[]{:S(2)}) collective-permute-start(bf16[3072,256]{1,0:T(8,128)(2,1)} %get-tuple-element.41), channel_id=1, source_target_pairs={{0,8},{8,136},{16,24},{24,152},{32,40},{40,168},{48,56},{56,184},{... | collective-permute-start | bytes 4718600 | tf_op jit(solution)/shard_map/ppermute | solution.py:409
  75.2 36.7 %collective-permute-start.4 = (bf16[3072,256]{1,0:T(8,128)(2,1)}, bf16[3072,256]{1,0:T(8,128)(2,1)}, u32[]{:S(2)}, u32[]{:S(2)}) collective-permute-start(bf16[3072,256]{1,0:T(8,128)(2,1)} %get-tuple-element.42), channel_id=1, source_target_pairs={{0,72},{8,200},{16,88},{24,216},{32,104},{40,232},{48,120},{56,248... | collective-permute-start | bytes 4718600 | tf_op jit(solution)/shard_map/ppermute | solution.py:409
  107.3 4.7 %copy-start.3 = (bf16[3072,256]{1,0:T(8,128)(2,1)}, bf16[3072,256]{1,0:T(8,128)(2,1)S(1)}, u32[]{:S(2)}) copy-start(bf16[3072,256]{1,0:T(8,128)(2,1)S(1)} %collective-permute-done.3.refs_0_) | copy-start | bytes 4718596
  111.9 10.9 %collective-permute-start.10 = (bf16[3072,256]{1,0:T(8,128)(2,1)}, bf16[3072,256]{1,0:T(8,128)(2,1)}, u32[]{:S(2)}, u32[]{:S(2)}) collective-permute-start(bf16[3072,256]{1,0:T(8,128)(2,1)} %get-tuple-element.53.refs_1_), channel_id=1, source_target_pairs={{0,8},{8,0},{16,24},{24,16},{32,40},{40,32},{48,56},{56,48},{1,9},... | collective-permute-start | bytes 4718600 | tf_op jit(solution)/shard_map/ppermute | solution.py:415
  115.7 7.1 %copy-start.1 = (f32[512,2048]{1,0:T(8,128)S(1)}, f32[512,2048]{1,0:T(8,128)}, u32[]{:S(2)}) copy-start(f32[512,2048]{1,0:T(8,128)} %get-tuple-element.49.so_far.so_far_all) | copy-start | bytes 12582916
  115.7 7.1 %copy-start.2 = (bf16[512,2048]{1,0:T(8,128)(2,1)S(1)}, bf16[512,2048]{1,0:T(8,128)(2,1)}, u32[]{:S(2)}) copy-start(bf16[512,2048]{1,0:T(8,128)(2,1)} %get-tuple-element.48.normed.normed_all) | copy-start | bytes 6291460
  115.7 7.1 %copy-start.4 = (bf16[3072,256]{1,0:T(8,128)(2,1)S(1)}, bf16[3072,256]{1,0:T(8,128)(2,1)}, u32[]{:S(2)}) copy-start(bf16[3072,256]{1,0:T(8,128)(2,1)} %get-tuple-element.52.refs_0_) | copy-start | bytes 4718596
  115.7 7.1 %collective-permute-start.9 = (bf16[3072,256]{1,0:T(8,128)(2,1)}, bf16[3072,256]{1,0:T(8,128)(2,1)}, u32[]{:S(2)}, u32[]{:S(2)}) collective-permute-start(bf16[3072,256]{1,0:T(8,128)(2,1)} %get-tuple-element.52.refs_0_), channel_id=1, source_target_pairs={{0,8},{8,0},{16,24},{24,16},{32,40},{40,32},{48,56},{56,48},{1,9},... | collective-permute-start | bytes 4718600 | tf_op jit(solution)/shard_map/ppermute | solution.py:415
  122.8 1.0 copy-start.6
  123.8 9.3 %copy-start.5 = (bf16[3072,256]{1,0:T(8,128)(2,1)S(1)}, bf16[3072,256]{1,0:T(8,128)(2,1)}, u32[]{:S(2)}) copy-start(bf16[3072,256]{1,0:T(8,128)(2,1)} %get-tuple-element.52.refs_0_) | copy-start | bytes 4718596
  127.5 11.1 %collective-permute-start.11 = (bf16[64,1024]{1,0:T(8,128)(2,1)S(1)}, bf16[64,1024]{1,0:T(8,128)(2,1)S(1)}, u32[]{:S(2)}, u32[]{:S(2)}) collective-permute-start(bf16[64,1024]{1,0:T(8,128)(2,1)S(1)} %get-tuple-element.54), channel_id=1, source_target_pairs={{0,1},{1,2},{2,3},{3,4},{4,5},{5,6},{6,7},{7,0},{8,9},{9,10},{10,1... | collective-permute-start | bytes 393224 | tf_op jit(solution)/shard_map/ppermute | solution.py:429
  128.8 9.7 %collective-permute-start.12 = (bf16[64,1024]{1,0:T(8,128)(2,1)S(1)}, bf16[64,1024]{1,0:T(8,128)(2,1)S(1)}, u32[]{:S(2)}, u32[]{:S(2)}) collective-permute-start(bf16[64,1024]{1,0:T(8,128)(2,1)S(1)} %get-tuple-element.55), channel_id=1, source_target_pairs={{0,7},{1,0},{2,1},{3,2},{4,3},{5,4},{6,5},{7,6},{8,15},{9,8},{10,9... | collective-permute-start | bytes 393224 | tf_op jit(solution)/shard_map/ppermute | solution.py:429
  138.6 8.6 %collective-permute-start.13 = (bf16[64,2048]{1,0:T(8,128)(2,1)S(1)}, bf16[64,2048]{1,0:T(8,128)(2,1)S(1)}, u32[]{:S(2)}, u32[]{:S(2)}) collective-permute-start(bf16[64,2048]{1,0:T(8,128)(2,1)S(1)} %get-tuple-element.56), channel_id=1, source_target_pairs={{0,1},{1,2},{2,3},{3,4},{4,5},{5,6},{6,7},{7,0},{8,9},{9,10},{10,1... | collective-permute-start | bytes 786440 | tf_op jit(solution)/shard_map/ppermute | solution.py:433
  138.7 8.5 %collective-permute-start.14 = (bf16[64,2048]{1,0:T(8,128)(2,1)S(1)}, bf16[64,2048]{1,0:T(8,128)(2,1)S(1)}, u32[]{:S(2)}, u32[]{:S(2)}) collective-permute-start(bf16[64,2048]{1,0:T(8,128)(2,1)S(1)} %get-tuple-element.57), channel_id=1, source_target_pairs={{0,7},{1,0},{2,1},{3,2},{4,3},{5,4},{6,5},{7,6},{8,15},{9,8},{10,9... | collective-permute-start | bytes 786440 | tf_op jit(solution)/shard_map/ppermute | solution.py:433
  148.0 7.9 %collective-permute-start.15 = (bf16[64,2048]{1,0:T(8,128)(2,1)}, bf16[64,2048]{1,0:T(8,128)(2,1)}, u32[]{:S(2)}, u32[]{:S(2)}) collective-permute-start(bf16[64,2048]{1,0:T(8,128)(2,1)} %get-tuple-element.58), channel_id=1, source_target_pairs={{0,1},{1,2},{2,3},{3,4},{4,5},{5,6},{6,7},{7,0},{8,9},{9,10},{10,1... | collective-permute-start | bytes 786440 | tf_op jit(solution)/shard_map/ppermute | solution.py:433
  148.0 7.9 %collective-permute-start.16 = (bf16[64,2048]{1,0:T(8,128)(2,1)S(1)}, bf16[64,2048]{1,0:T(8,128)(2,1)}, u32[]{:S(2)}, u32[]{:S(2)}) collective-permute-start(bf16[64,2048]{1,0:T(8,128)(2,1)S(1)} %get-tuple-element.59), channel_id=1, source_target_pairs={{0,7},{1,0},{2,1},{3,2},{4,3},{5,4},{6,5},{7,6},{8,15},{9,8},{10,9... | collective-permute-start | bytes 786440 | tf_op jit(solution)/shard_map/ppermute | solution.py:433
  157.0 6.5 %collective-permute-start.17 = (bf16[64,2048]{1,0:T(8,128)(2,1)S(1)}, bf16[64,2048]{1,0:T(8,128)(2,1)S(1)}, u32[]{:S(2)}, u32[]{:S(2)}) collective-permute-start(bf16[64,2048]{1,0:T(8,128)(2,1)S(1)} %get-tuple-element.60), channel_id=1, source_target_pairs={{0,1},{1,2},{2,3},{3,4},{4,5},{5,6},{6,7},{7,0},{8,9},{9,10},{10,1... | collective-permute-start | bytes 786440 | tf_op jit(solution)/shard_map/ppermute | solution.py:433
  157.5 6.1 %collective-permute-start.18 = (bf16[64,2048]{1,0:T(8,128)(2,1)S(1)}, bf16[64,2048]{1,0:T(8,128)(2,1)S(1)}, u32[]{:S(2)}, u32[]{:S(2)}) collective-permute-start(bf16[64,2048]{1,0:T(8,128)(2,1)S(1)} %get-tuple-element.61), channel_id=1, source_target_pairs={{0,7},{1,0},{2,1},{3,2},{4,3},{5,4},{6,5},{7,6},{8,15},{9,8},{10,9... | collective-permute-start | bytes 786440 | tf_op jit(solution)/shard_map/ppermute | solution.py:433
  163.7 9.8 %collective-permute-start.19 = (bf16[16,2048]{1,0:T(8,128)(2,1)S(1)}, bf16[16,2048]{1,0:T(8,128)(2,1)S(1)}, u32[]{:S(2)}, u32[]{:S(2)}) collective-permute-start(bf16[16,2048]{1,0:T(8,128)(2,1)S(1)} %get-tuple-element.76), channel_id=1, source_target_pairs={{0,0},{128,8},{16,16},{144,24},{32,32},{160,40},{48,48},{176,56},{... | collective-permute-start | bytes 196616 | tf_op jit(solution)/shard_map/ppermute | solution.py:444
  166.8 6.7 %collective-permute-start.20 = (bf16[16,2048]{1,0:T(8,128)(2,1)S(1)}, bf16[16,2048]{1,0:T(8,128)(2,1)S(1)}, u32[]{:S(2)}, u32[]{:S(2)}) collective-permute-start(bf16[16,2048]{1,0:T(8,128)(2,1)S(1)} %get-tuple-element.79), channel_id=1, source_target_pairs={{8,0},{136,8},{24,16},{152,24},{40,32},{168,40},{56,48},{184,56},{... | collective-permute-start | bytes 196616 | tf_op jit(solution)/shard_map/ppermute | solution.py:444
  168.0 5.5 %collective-permute-start.21 = (bf16[16,2048]{1,0:T(8,128)(2,1)S(1)}, bf16[16,2048]{1,0:T(8,128)(2,1)S(1)}, u32[]{:S(2)}, u32[]{:S(2)}) collective-permute-start(bf16[16,2048]{1,0:T(8,128)(2,1)S(1)} %get-tuple-element.78), channel_id=1, source_target_pairs={{64,0},{192,8},{80,16},{208,24},{96,32},{224,40},{112,48},{240,56}... | collective-permute-start | bytes 196616 | tf_op jit(solution)/shard_map/ppermute | solution.py:444
  169.0 6.5 %collective-permute-start.22 = (bf16[16,2048]{1,0:T(8,128)(2,1)S(1)}, bf16[16,2048]{1,0:T(8,128)(2,1)S(1)}, u32[]{:S(2)}, u32[]{:S(2)}) collective-permute-start(bf16[16,2048]{1,0:T(8,128)(2,1)S(1)} %get-tuple-element.77), channel_id=1, source_target_pairs={{72,0},{200,8},{88,16},{216,24},{104,32},{232,40},{120,48},{248,56... | collective-permute-start | bytes 196616 | tf_op jit(solution)/shard_map/ppermute | solution.py:444
  173.5 3.7 %copy-start.10 = (bf16[2,2048,256]{2,1,0:T(8,128)(2,1)S(1)}, bf16[2,2048,256]{2,1,0:T(8,128)(2,1)}, u32[]{:S(2)}) copy-start(bf16[2,2048,256]{2,1,0:T(8,128)(2,1)} %param.29) | copy-start | bytes 6291460
  175.6 12.4 %copy-start.12 = (bf16[256,4]{0,1:T(4,128)(2,1)S(1)}, bf16[256,4]{0,1:T(4,128)(2,1)}, u32[]{:S(2)}) copy-start(bf16[256,4]{0,1:T(4,128)(2,1)} %param.31) | copy-start | bytes 6148
  175.6 12.4 %copy-start.13 = (f32[256]{0:T(256)S(1)}, f32[256]{0:T(256)}, u32[]{:S(2)}) copy-start(f32[256]{0:T(256)} %param.30) | copy-start | bytes 3076
  177.4 3.0 %collective-permute-start.23 = (f32[32,256]{1,0:T(8,128)S(1)}, f32[32,256]{1,0:T(8,128)S(1)}, u32[]{:S(2)}, u32[]{:S(2)}) collective-permute-start(f32[32,256]{1,0:T(8,128)S(1)} %convolution_add_fusion), channel_id=1, source_target_pairs={{0,8},{8,0},{16,24},{24,16},{32,40},{40,32},{48,56},{56,48},{1,9},... | collective-permute-start | bytes 98312 | tf_op jit(solution)/shard_map/ppermute | solution.py:415
  180.4 4.9 %collective-permute-start.24 = (f32[32,256]{1,0:T(8,128)S(1)}, f32[32,256]{1,0:T(8,128)S(1)}, u32[]{:S(2)}, u32[]{:S(2)}) collective-permute-start(f32[32,256]{1,0:T(8,128)S(1)} %add.127), channel_id=1, source_target_pairs={{0,16},{8,24},{16,0},{24,8},{32,48},{40,56},{48,32},{56,40},{1,17}... | collective-permute-start | bytes 98312 | tf_op jit(solution)/shard_map/ppermute | solution.py:454
  181.6 4.3 %collective-permute-start.25 = (f32[32,256]{1,0:T(8,128)S(1)}, f32[32,256]{1,0:T(8,128)S(1)}, u32[]{:S(2)}, u32[]{:S(2)}) collective-permute-start(f32[32,256]{1,0:T(8,128)S(1)} %add.127), channel_id=1, source_target_pairs={{0,32},{8,40},{16,48},{24,56},{32,0},{40,8},{48,16},{56,24},{1,33}... | collective-permute-start | bytes 98312 | tf_op jit(solution)/shard_map/ppermute | solution.py:454
  184.0 4.0 %collective-permute-start.26 = (f32[32,256]{1,0:T(8,128)S(1)}, f32[32,256]{1,0:T(8,128)S(1)}, u32[]{:S(2)}, u32[]{:S(2)}) collective-permute-start(f32[32,256]{1,0:T(8,128)S(1)} %add.127), channel_id=1, source_target_pairs={{0,48},{8,56},{16,32},{24,40},{32,16},{40,24},{48,0},{56,8},{1,49}... | collective-permute-start | bytes 98312 | tf_op jit(solution)/shard_map/ppermute | solution.py:454
Sparse Core Ops, SparseCore 0:
  49.0 37.7 all-gather.2
